TPU v7x, 32 devices: a whole 2x2x4 slice. The times are simulated.
32 devices in a mesh: fib: 4 (over y, x), row: 4 (over z), slab: 2 (over core).
Axes of the slice: x: 2, y: 2, z: 4, core: 2. Of those that a mesh axis runs over, the one named last changes fastest.
Arguments:
- tensor: float32 [128, 128, 64, 128], P('fib', 'row', 'slab'), may hold values from -300 to 300
- factor_one: float32 [128, 64], replicated, may hold values from -0.5 to 0.5
- factor_two: float32 [128, 64], P('row'), may hold values from -50 to 50
- factor_three: float32 [64, 64], P('slab'), may hold values from -50 to 50
- factor_four: float32 [128, 64], replicated, may hold values from -0.5 to 0.5
Outputs:
- updated_factor: float32 [128, 64], replicated
- core_tensor: float32 [64, 64, 64, 64], P(None, ('row', 'slab'), 'fib')
All inputs are finite; a program needn't handle non-finite values.
Results may differ from a plain program's by a relative error of at most 0.00015.
Values sent between devices are 32-bit elements; how exact they have to be, the bound alone decides.
No kernel may reach another device: no remote copies, remote signals or barrier semaphores. Data moves between devices by JAX's collectives and lax.ppermute only.
A program may use at most 256 MiB of HBM per device.

v0:
```python
import jax
import jax.numpy as jnp
from jax import lax
from jax.sharding import PartitionSpec as P


def orthonormal(target):
    highest = lax.Precision.HIGHEST
    result = target
    for repeat in range(2):
        crossed = jnp.dot(result.T, result, precision=highest)
        cholesky_factor = jnp.linalg.cholesky(crossed)
        result = jax.scipy.linalg.solve_triangular(cholesky_factor, result.T, lower=True).T
    return result


def body(tensor, factor_one, factor_two, factor_three, factor_four):
    highest = lax.Precision.HIGHEST
    reduced = jnp.einsum("ijkl,lr->ijkr", tensor, factor_four, precision=highest)
    halfway = jnp.einsum("ijkr,jq->qikr", reduced, factor_two, precision=highest)
    summed = lax.psum_scatter(
        jnp.einsum("qikr,kp->qipr", halfway, factor_three, precision=highest),
        ("row", "slab"),
        scatter_dimension=0,
        tiled=True,
    )
    fibers = lax.all_to_all(summed, "fib", split_axis=2, concat_axis=1, tiled=True)
    local_gram = jnp.einsum("qipr,qjpr->ij", fibers, fibers, precision=highest)
    gram = lax.psum(local_gram, ("fib", "row", "slab"))
    target = jnp.dot(gram, factor_one, precision=highest)
    updated = orthonormal(target)
    core = jnp.einsum("ia,qipr->aqpr", updated, fibers, precision=highest)
    return (updated, core)


def solution(mesh):
    in_specs = (P("fib", "row", "slab", None), P(), P("row", None), P("slab", None), P())
    out_specs = (P(), P(None, ("row", "slab"), "fib", None))
    return jax.shard_map(body, mesh=mesh, in_specs=in_specs, out_specs=out_specs, check_vma=False)
```

profile of v0, /device:TPU:17, one launch (start us, length us, event | category | flops | bytes accessed | tf_op | source)
XLA Modules:
  0.0 1167.1 jit_solution(13523008680324693547)
XLA Ops:
  7.2 0.7 copy-done
  7.9 26.5 %fusion = f32[32,32,32,64]{3,1,2,0:T(8,128)S(1)} fusion(f32[32,32,32,128]{3,2,1,0:T(8,128)} %param.8, f32[128,64]{0,1:T(8,128)S(1)} %copy-done), kind=kOutput, calls=%fused_computation.1 | convolution fusion | flops 3221225472 | bytes 25198592 | tf_op jit(solution)/shard_map/ijkl,lr->ijkr/dot_general | solution.py:19
  34.4 56.3 %convolution_bitcast_fusion.1 = f32[64,32,32,64]{0,3,2,1:T(8,128)} fusion(f32[32,32,32,64]{3,1,2,0:T(8,128)S(1)} %fusion, f32[32,64]{1,0:T(8,128)S(1)} %copy-done.5), kind=kOutput, calls=%fused_computation.3 | convolution fusion | flops 1610612736 | bytes 25174016 | tf_op jit(solution)/shard_map/ijkr,jq->qikr/dot_general | solution.py:20
  90.7 34.8 %copy.18 = f32[64,32,32,64]{3,2,1,0:T(8,128)} copy(f32[64,32,32,64]{0,3,2,1:T(8,128)} %convolution_bitcast_fusion.1) | data formatting | bytes 33554432 | tf_op jit(solution)/shard_map/ijkr,jq->qikr/dot_general | solution.py:20
  125.5 111.6 %convolution_bitcast_fusion = f32[64,32,64,64]{2,3,1,0:T(8,128)} fusion(f32[64,32,32,64]{3,2,1,0:T(8,128)} %copy.18, f32[32,64]{1,0:T(8,128)S(1)} %copy-done.6), kind=kOutput, calls=%fused_computation | convolution fusion | flops 3221225472 | bytes 50339840 | tf_op jit(solution)/shard_map/qikr,kp->qipr/dot_general | solution.py:22
  237.2 639.7 %reduce-scatter.2.cloned.1.call-done = f32[8,32,64,64]{2,3,1,0:T(8,128)} async-done(((f32[64,32,64,64]{2,3,1,0:T(8,128)}), f32[8,32,64,64]{2,3,1,0:T(8,128)}) %reduce-scatter.2.cloned.1.call-update) | async-done | bytes 4194320 | tf_op jit(solution)/shard_map/reduce_scatter | solution.py:21
  876.9 9.6 copy.19
  886.5 8.6 reshape.17
  895.1 53.5 %all_to_all.18 = f32[4,1,262144]{2,1,0:T(1,128)} all-to-all(f32[4,1,262144]{2,1,0:T(1,128)} %reshape.17), channel_id=1, replica_groups=mesh['fib'=4,'row'=4,'slab'=2] {'fib'}, dimensions={0} | all-to-all | bytes 8388608 | tf_op jit(solution)/shard_map/all_to_all | solution.py:27
  948.6 0.5 broadcast.36
  949.1 15.3 %reduce.4 = f32[4,262144]{1,0:T(4,128)} reduce(f32[4,1,262144]{2,1,0:T(1,128)} %all_to_all.18, f32[]{:T(128)} %broadcast.36), dimensions={1}, to_apply=%all_to_all.13.reduce_sub_computation | reduce | bytes 8388612 | tf_op jit(solution)/shard_map/all_to_all | solution.py:27
  964.4 9.3 reshape.18
  973.7 11.4 copy.21
  985.1 3.2 copy-done.2
  988.3 13.7 %fusion.6 = f32[128,128]{1,0:T(8,128)} fusion(f32[8,128,16,64]{3,2,1,0:T(8,128)S(1)} %bitcast.65), kind=kOutput, calls=%fused_computation.8 | convolution fusion | flops 1610612736 | bytes 4259840 | tf_op jit(solution)/shard_map/qipr,qjpr->ij/dot_general | solution.py:28
  1002.0 116.2 %all-reduce.2.cloned.1.call-done = f32[128,128]{1,0:T(8,128)} async-done(((f32[128,128]{1,0:T(8,128)}), f32[128,128]{1,0:T(8,128)}) %all-reduce.2.cloned.1.call-update) | async-done | bytes 65552 | tf_op jit(solution)/shard_map/psum | solution.py:29
  1118.2 1.1 fusion.24
  1119.3 0.2 fusion.25
  1119.5 0.1 copy.24
  1119.6 5.8 cholesky.44
  1125.5 0.6 compare_reduce_fusion.1
  1126.1 0.7 fusion.9
  1126.8 4.9 custom-call.6
  1131.7 0.3 fusion.16
  1131.9 0.2 fusion.26
  1132.2 5.8 cholesky.55
  1138.1 0.6 compare_reduce_fusion
  1138.7 0.7 fusion.10
  1139.4 4.9 custom-call.7
  1144.3 0.3 fusion.13
  1144.6 11.0 fusion.2
  1155.6 4.4 copy.27
  (21 shorter events, 0.3 us)
Async XLA Ops:
  7.2 0.8 copy-start
  7.2 27.2 %copy-start.5 = (f32[32,64]{1,0:T(8,128)S(1)}, f32[32,64]{1,0:T(8,128)}, u32[]{:S(2)}) copy-start(f32[32,64]{1,0:T(8,128)} %param.10) | copy-start | bytes 24580
  7.2 869.7 %reduce-scatter.2.cloned.1.call-start = ((), (), s32[]{:S(2)}) async-start(), calls=%async_computation.2 | async-start | bytes 75497472 | tf_op jit(solution)/shard_map/reduce_scatter | solution.py:21
  90.7 34.8 %copy-start.6 = (f32[32,64]{1,0:T(8,128)S(1)}, f32[32,64]{1,0:T(8,128)}, u32[]{:S(2)}) copy-start(f32[32,64]{1,0:T(8,128)} %param.11) | copy-start | bytes 24580
  237.2 881.0 %all-reduce.2.cloned.1.call-start = ((), (), s32[]{:S(2)}) async-start(), calls=%async_computation.3 | async-start | bytes 131072 | tf_op jit(solution)/shard_map/psum | solution.py:29
  964.4 153.8 %copy-start.4 = (f32[128,64]{0,1:T(8,128)S(1)}, f32[128,64]{0,1:T(8,128)}, u32[]{:S(2)}) copy-start(f32[128,64]{0,1:T(8,128)} %param.9) | copy-start | bytes 98308
  973.7 186.3 %copy-start.1 = (f32[128,64]{0,1:T(8,128)S(1)}, f32[128,64]{0,1:T(8,128)}, u32[]{:S(2)}) copy-start(f32[128,64]{0,1:T(8,128)} %param.12) | copy-start | bytes 98308
  985.0 3.2 copy-start.2
  1144.6 15.5 %copy-start.3 = (f32[64,128]{1,0:T(8,128)}, f32[64,128]{1,0:T(8,128)S(1)}, u32[]{:S(2)}) copy-start(f32[64,128]{1,0:T(8,128)S(1)} %fusion.13) | copy-start | bytes 98308
Sparse Core Ops, SparseCore 0:
  237.3 639.5 reduce-scatter.1
  1002.1 116.0 all-reduce.1
where the time goes:
time: 1180 us; the launch traced here: 1170 us
  waiting for transfers between devices  756 us (64%)
  matrix products  221 us (19%)
  local copies, waits for them, and re-layouts  82.7 us (7%)
  blocking collectives  53.5 us (5%)
  other arithmetic  39.4 us (3%)
  between operations  14.4 us (1%)
    reduce_scatter x1, waiting for transfers between devices, body(): lax.psum_scatter(jnp.einsum('qikr,kp->qipr', halfway, factor_three, preci...  640 us
    psum x1, waiting for transfers between devices, body(): gram = lax.psum(local_gram, ('fib', 'row', 'slab'))  116 us
    dot_general x1, matrix products, body(): jnp.einsum('qikr,kp->qipr', halfway, factor_three, precision=highest)  112 us
    dot_general x1, matrix products, body(): jnp.einsum('ijkr,jq->qikr', reduced, factor_two, precision=highest)  56.3 us
    all_to_all x1, blocking collectives, body(): lax.all_to_all(summed, 'fib', split_axis=2, concat_axis=1, tiled=True)  53.5 us
    dot_general x1, local copies, waits for them, and re-layouts, body(): jnp.einsum('ijkr,jq->qikr', reduced, factor_two, precision=highest)  34.8 us
    dot_general x1, matrix products, body(): jnp.einsum('ijkl,lr->ijkr', tensor, factor_four, precision=highest)  26.5 us
    unnamed x17, local copies, waits for them, and re-layouts  26.3 us
  transfers between devices with their start and end apart: 2, of which 2 were waited for; matrix products, arithmetic and copies ran while one was open for 0% of the time, Pallas kernels for 0%

commit v1 on v0

v1 whole, which is shorter than its diff:
```python
import functools
import itertools

import jax
import jax.numpy as jnp
from jax import lax
from jax.experimental import pallas as pl
from jax.experimental.pallas import tpu as pltpu
from jax.sharding import PartitionSpec as P

F32 = jnp.float32
BF16 = jnp.bfloat16
HIGHEST = lax.Precision.HIGHEST
LANES = 128
TILE = 8
NT = (((1,), (1,)), ((), ()))
NN = (((1,), (0,)), ((), ()))


def split(x):
    high = x.astype(BF16)
    return high, (x - high.astype(F32)).astype(BF16)


def split_outside(x):
    high = lax.reduce_precision(x, 8, 7)
    return high.astype(BF16), (x - high).astype(BF16)


def dot(a, b, dims=NN):
    return lax.dot_general(a, b, dims, preferred_element_type=F32)


def relative(x, axis, count, me):
    shape = x.shape
    width = 1
    while width < count:
        cut = shape[:axis] + (count // (2 * width), 2, shape[axis] // count * width) + shape[axis + 1:]
        y = x.reshape(cut)
        x = jnp.where((me // width) % 2 == 1, jnp.flip(y, axis + 1), y).reshape(shape)
        width *= 2
    return x


def partner(x, axes, count, distance):
    return lax.ppermute(x, axes, [(s, s ^ distance) for s in range(count)])


def in_hbm(x):
    return pltpu.with_memory_space_constraint(x, pltpu.HBM)


def gathered(x, axes, count):
    return [x] + [partner(x, axes, count, b) for b in range(1, count)]


def tree_sum(parts):
    while len(parts) > 1:
        parts = [a + b for a, b in zip(parts[::2], parts[1::2])]
    return parts[0]


def params(steps, megabytes=12):
    return pltpu.CompilerParams(
        dimension_semantics=("arbitrary",) * steps, vmem_limit_bytes=megabytes * 2 ** 20
    )


def contract_four(tensor, factor, me, first, chunk, parts, after):
    _, jl, kl, depth = tensor.shape
    ranks = factor.shape[1]
    m = LANES // jl
    groups = kl // m
    own = ranks // parts
    per = own // m

    def kernel(me_ref, x_ref, f_ref, *refs):
        outs, w_ref, s_ref = refs[len(after):-2], refs[-2], refs[-1]

        @pl.when(pl.program_id(0) == 0)
        def _():
            high, low = split(f_ref[...].T)
            w_ref[...] = jnp.concatenate(
                [jnp.concatenate([high, high], 1), jnp.concatenate([low, jnp.zeros_like(low)], 1)], 0)

        lane = lax.broadcasted_iota(jnp.int32, (1, 1, LANES), 2)
        weights = w_ref[...]
        for group in range(groups):
            rows = jnp.concatenate([x_ref[0, :, q * groups + group, :] for q in range(m)], axis=0)
            high, low = split(rows)
            found = dot(weights, jnp.concatenate([high, low], axis=1), NT)
            s_ref[:, group, :] = found[:ranks] + found[ranks:]
        for part in range(parts):
            mine = s_ref[pl.ds((me_ref[0] ^ part) * own, own)].reshape(per, m, groups, LANES)
            blocks = [mine[:, q] for q in range(m)]
            width = m // 2
            while width:
                upper = (lane // (jl * width)) % 2 == 1
                shift = jl * width
                for q in range(m):
                    if q & width == 0:
                        a, b = blocks[q], blocks[q + width]
                        blocks[q] = jnp.where(upper, pltpu.roll(b, shift, 2), a)
                        blocks[q + width] = jnp.where(upper, b, pltpu.roll(a, LANES - shift, 2))
                width //= 2
            for q in range(m):
                outs[part][0, :, q * groups:(q + 1) * groups, :] = blocks[q]

    return pl.pallas_call(
        kernel,
        grid_spec=pltpu.PrefetchScalarGridSpec(
            num_scalar_prefetch=1,
            grid=(chunk,),
            in_specs=[
                pl.BlockSpec((1, jl, kl, depth), lambda i, me: (first + i, 0, 0, 0)),
                pl.BlockSpec(factor.shape, lambda i, me: (0, 0)),
            ] + [pl.BlockSpec(memory_space=pl.ANY)] * len(after),
            out_specs=[pl.BlockSpec((1, per, kl, LANES), lambda i, me: (i, 0, 0, 0))] * parts,
            scratch_shapes=[
                pltpu.VMEM((2 * ranks, 2 * depth), BF16), pltpu.VMEM((ranks, groups, LANES), F32)],
        ),
        out_shape=[jax.ShapeDtypeStruct((chunk, per, kl, LANES), F32)] * parts,
        compiler_params=params(1),
        cost_estimate=pl.CostEstimate(
            flops=12 * chunk * jl * kl * depth * ranks, bytes_accessed=6 * chunk * jl * kl * depth, transcendentals=0
        ),
        name="mode_four",
    )(me, tensor, factor, *after)


def spread(pieces, m):
    jl, ranks = pieces[0].shape
    rows, wide = len(pieces) * m * jl, m * ranks

    def kernel(*refs):
        out_ref = refs[-1]
        out_ref[...] = jnp.zeros_like(out_ref)
        for n, ref in enumerate(refs[:-1]):
            for half, value in enumerate(split(ref[...])):
                for r in range(m):
                    at = (n * m + r) * jl
                    out_ref[at:at + jl, half * wide + r * ranks:half * wide + (r + 1) * ranks] = value

    return pl.pallas_call(
        kernel,
        in_specs=[pl.BlockSpec(memory_space=pltpu.VMEM)] * len(pieces),
        out_specs=pl.BlockSpec(memory_space=pltpu.VMEM),
        out_shape=jax.ShapeDtypeStruct((rows, 2 * wide), BF16),
        compiler_params=params(0),
        name="spread",
    )(*pieces)


def contract_two_three(pieces, order, weights_two, weights_three, rows, slabs, targets, after):
    chunk, per, kl, _ = pieces[0].shape
    wide = weights_two.shape[1] // 2
    ranks = weights_three.shape[0]
    share = ranks // targets
    count = len(pieces)

    def kernel(*refs):
        ins, two_ref, three_ref, outs = refs[:count], refs[count], refs[count + 1], refs[count + 2 + len(after):]
        taken = []
        for slab in range(slabs):
            taken.append(jnp.concatenate(
                [ins[order.index(row * slabs + slab)][...].reshape(chunk * kl, LANES) for row in range(rows)], axis=1))
        high, low = split(jnp.concatenate(taken, axis=0))
        two_high, two_low = two_ref[:, :wide], two_ref[:, wide:]
        half = dot(high, two_high) + dot(low, two_high) + dot(high, two_low)
        high, low = split(half)
        for i in range(chunk):
            spots = [slice((slab * chunk + i) * kl, (slab * chunk + i + 1) * kl) for slab in range(slabs)]
            own_high = jnp.concatenate([high[s] for s in spots], axis=0)
            own_low = jnp.concatenate([low[s] for s in spots], axis=0)
            full = dot(three_ref[...], jnp.concatenate([own_high, own_low, own_high], axis=0))
            for target in range(targets):
                outs[target][0, :, i, :] = full[target * share:(target + 1) * share]

    return pl.pallas_call(
        kernel,
        grid=(per,),
        in_specs=[pl.BlockSpec((chunk, 1, kl, LANES), lambda g: (0, g, 0, 0))] * count
        + [
            pl.BlockSpec(weights_two.shape, lambda g: (0, 0)),
            pl.BlockSpec(weights_three.shape, lambda g: (0, 0)),
        ] + [pl.BlockSpec(memory_space=pl.ANY)] * len(after),
        out_specs=[pl.BlockSpec((1, share, chunk, wide), lambda g: (g, 0, 0, 0))] * targets,
        out_shape=[jax.ShapeDtypeStruct((per, share, chunk, wide), F32)] * targets,
        compiler_params=params(1),
        cost_estimate=pl.CostEstimate(
            flops=6 * chunk * per * slabs * kl * (rows * LANES + ranks) * wide,
            bytes_accessed=8 * chunk * per * slabs * kl * rows * LANES,
            transcendentals=0,
        ),
        name="modes_two_three",
    )(*pieces, weights_two, weights_three, *after)


def held(values, after):
    count = len(values)

    def kernel(*refs):
        for source, target in zip(refs[:count], refs[count + len(after):]):
            target[...] = source[...]

    return pl.pallas_call(
        kernel,
        in_specs=[pl.BlockSpec(memory_space=pltpu.VMEM)] * count + [pl.BlockSpec(memory_space=pl.ANY)] * len(after),
        out_specs=[pl.BlockSpec(memory_space=pltpu.VMEM)] * count,
        out_shape=[jax.ShapeDtypeStruct(v.shape, v.dtype) for v in values],
        compiler_params=pltpu.CompilerParams(vmem_limit_bytes=60 * 2 ** 20),
        name="held",
    )(*values, *after)


def gram_times(pieces, factor, fib, spots):
    per, share, _, wide = pieces[0].shape
    count = len(pieces)
    total = sum(piece.shape[2] for piece in pieces)
    block = min(share, 4)

    def kernel(fib_ref, *refs):
        ins, f_ref, out_ref, acc_ref = refs[:count], refs[count], refs[count + 1], refs[count + 2]
        step = pl.program_id(0)

        @pl.when(step == 0)
        def _():
            acc_ref[...] = jnp.zeros_like(acc_ref)

        found = None
        for g in range(per):
            for p in range(block):
                high, low = split(jnp.concatenate([ref[g, p] for ref in ins], axis=0))
                term = dot(high, jnp.concatenate([high, low], axis=0), NT)
                found = term if found is None else found + term
        acc_ref[...] += found

        @pl.when(step == pl.num_programs(0) - 1)
        def _():
            mixed = acc_ref[:, total:]
            gram = acc_ref[:, :total] + mixed + mixed.T
            target = lax.dot_general(gram, f_ref[...], NN, precision=HIGHEST, preferred_element_type=F32)
            for n, (group, spot) in enumerate(spots):
                at = pl.multiple_of((fib_ref[0] ^ group) * (total // fibs), TILE)
                out_ref[pl.ds(at + spot, TILE), :] = target[n * TILE:(n + 1) * TILE]

    fibs = 1 + max(group for group, _ in spots)
    return pl.pallas_call(
        kernel,
        grid_spec=pltpu.PrefetchScalarGridSpec(
            num_scalar_prefetch=1,
            grid=(share // block,),
            in_specs=[
                pl.BlockSpec((per, block, piece.shape[2], wide), lambda s, fib: (0, s, 0, 0)) for piece in pieces]
            + [pl.BlockSpec(factor.shape, lambda s, fib: (0, 0))],
            out_specs=pl.BlockSpec(factor.shape, lambda s, fib: (0, 0)),
            scratch_shapes=[pltpu.VMEM((total, 2 * total), F32)],
        ),
        out_shape=jax.ShapeDtypeStruct(factor.shape, F32),
        compiler_params=params(1),
        name="gram",
    )(fib, *pieces, factor)


def core_parts(pieces, updated, me, first, pairs, parts):
    per, _, _, wide = pieces[0].shape
    count = len(pieces)
    ranks = updated.shape[1]
    m = wide // ranks
    width = ranks // parts

    def kernel(me_ref, *refs):
        ins, u_ref, outs, t_ref, w_ref = refs[:count], refs[count], refs[count + 1:-2], refs[-2], refs[-1]

        @pl.when(pl.program_id(0) == 0)
        def _():
            high, low = split(u_ref[...].T)
            w_ref[...] = jnp.concatenate(
                [jnp.concatenate([high, high], 1), jnp.concatenate([low, jnp.zeros_like(low)], 1)], 0)

        for g in range(per):
            pair = []
            for p in range(2):
                high, low = split(jnp.concatenate([ref[g, p] for ref in ins], axis=0))
                found = dot(w_ref[...], jnp.concatenate([high, low], axis=0))
                pair.append(found[:ranks] + found[ranks:])
            t_ref[g] = jnp.concatenate(pair, axis=0).T.reshape(m, parts, width, 2 * ranks)
        for g in range(per):
            for part in range(parts):
                for r in range(m):
                    outs[part][0, g * m + r] = t_ref[g, r, me_ref[0] ^ part]

    shape = (pairs, per * m, width, 2 * ranks)
    return pl.pallas_call(
        kernel,
        grid_spec=pltpu.PrefetchScalarGridSpec(
            num_scalar_prefetch=1,
            grid=(pairs,),
            in_specs=[
                pl.BlockSpec((per, 2, piece.shape[2], wide), lambda s, me: (0, first + s, 0, 0)) for piece in pieces]
            + [pl.BlockSpec(updated.shape, lambda s, me: (0, 0))],
            out_specs=[pl.BlockSpec((1,) + shape[1:], lambda s, me: (s, 0, 0, 0))] * parts,
            scratch_shapes=[
                pltpu.VMEM((per, m, parts, width, 2 * ranks), F32),
                pltpu.VMEM((2 * ranks, 2 * updated.shape[0]), BF16)],
        ),
        out_shape=[jax.ShapeDtypeStruct(shape, F32)] * parts,
        compiler_params=params(1),
        name="core",
    )(me, *pieces, updated)


def assemble(parts, me, ranks, number, total, whole):
    pairs, own, width, lanes = parts[0].shape
    count = len(parts)

    def kernel(me_ref, *refs):
        ins, out_ref, s_ref = refs[:count], refs[-2], refs[-1]
        for pair in range(pairs):
            for part in range(count):
                s_ref[pair, pl.ds((me_ref[0] ^ part) * own, own)] = ins[part][pair]
            for q in range(width):
                turned = s_ref[pair, :, q, :].T
                for p in range(2):
                    out_ref[:, q, 2 * pair + p, :] = turned[p * ranks:(p + 1) * ranks]

    return pl.pallas_call(
        kernel,
        grid_spec=pltpu.PrefetchScalarGridSpec(
            num_scalar_prefetch=1,
            grid=(1,),
            in_specs=[pl.BlockSpec((pairs, own, width, lanes), lambda s, me: (0, 0, 0, 0))] * count
            + [pl.BlockSpec(memory_space=pl.ANY)] * len(whole),
            out_specs=pl.BlockSpec((ranks, width, 2 * pairs, count * own), lambda s, me: (0, 0, number, 0)),
            scratch_shapes=[pltpu.VMEM((pairs, count * own, width, lanes), F32)],
        ),
        out_shape=jax.ShapeDtypeStruct((ranks, width, 2 * pairs * total, count * own), F32),
        input_output_aliases={1 + count: 0} if whole else {},
        compiler_params=params(1, 16),
        name="assemble",
    )(me, *parts, *whole)


def orthonormal(target, fib, spots):
    total, ranks = target.shape
    tile = 8

    fibs = 1 + max(group for group, _ in spots)

    def kernel(fib_ref, t_ref, out_ref, order_ref):
        z = t_ref[...]
        row = lax.broadcasted_iota(jnp.int32, (tile, 2 * ranks), 0)
        across = lax.broadcasted_iota(jnp.int32, (ranks, ranks), 1)
        down = lax.broadcasted_iota(jnp.int32, (ranks, ranks), 0)
        eye = jnp.where(across == down, jnp.float32(1), jnp.float32(0))
        for repeat in range(2):
            crossed = lax.dot_general(
                z, z, (((0,), (0,)), ((), ())), precision=HIGHEST, preferred_element_type=F32)
            whole = jnp.concatenate([crossed, eye], axis=1)
            blocks = [whole[b * tile:(b + 1) * tile] for b in range(ranks // tile)]
            for k in range(0, ranks, 2):
                home, spot = divmod(k, tile)
                first = {b: jnp.broadcast_to(blocks[b][:, k:k + 1], (tile, 2 * ranks))
                         for b in range(home, len(blocks))}
                second = {b: jnp.broadcast_to(blocks[b][:, k + 1:k + 2], (tile, 2 * ranks))
                          for b in range(home, len(blocks))}
                scale_one = lax.rsqrt(first[home][spot:spot + 1])
                side = first[home][spot + 1:spot + 2] * scale_one
                scale_two = lax.rsqrt(second[home][spot + 1:spot + 2] - side * side)
                one = blocks[home][spot:spot + 1] * scale_one
                two = (blocks[home][spot + 1:spot + 2] - side * one) * scale_two
                for b in range(home, len(blocks)):
                    left = first[b] * scale_one
                    right = (second[b] - side * left) * scale_two
                    fresh = blocks[b] - left * one - right * two
                    if b == home:
                        fresh = jnp.where(row > spot + 1, fresh, blocks[b])
                        fresh = jnp.where(row == spot, one, jnp.where(row == spot + 1, two, fresh))
                    blocks[b] = fresh
            inverse = jnp.concatenate(blocks, axis=0)[:, ranks:]
            z = lax.dot_general(z, inverse, NT, precision=HIGHEST, preferred_element_type=F32)
        out_ref[...] = z
        for n, (group, spot) in enumerate(spots):
            at = pl.multiple_of((fib_ref[0] ^ group) * (total // fibs), TILE)
            order_ref[n * TILE:(n + 1) * TILE, :] = out_ref[pl.ds(at + spot, TILE), :]

    return pl.pallas_call(
        kernel,
        in_specs=[pl.BlockSpec(memory_space=pltpu.SMEM), pl.BlockSpec(memory_space=pltpu.VMEM)],
        out_specs=[pl.BlockSpec(memory_space=pltpu.VMEM)] * 2,
        out_shape=[jax.ShapeDtypeStruct(target.shape, F32)] * 2,
        compiler_params=params(0),
        name="orthonormal",
    )(fib, target)


def body(fibs, rows, slabs, tensor, factor_one, factor_two, factor_three, factor_four):
    both = ("row", "slab")
    grid = rows * slabs
    il, jl, _, _ = tensor.shape
    ranks = factor_four.shape[1]
    m = LANES // jl
    sizes = [TILE] * (il // TILE)
    fib = lax.axis_index("fib")
    place = lax.axis_index("row") * slabs + lax.axis_index("slab")
    me = place.reshape(1).astype(jnp.int32)

    tensor = in_hbm(tensor)
    far = list(range(grid // 2, grid))
    near = list(range(slabs, grid // 2)) + list(range(1, slabs))
    order = [b for pair in itertools.zip_longest(far, near) for b in pair if b is not None] + [0]
    sent, pieces = [], []

    def send(after):
        c = len(sent)
        parts = contract_four(tensor, factor_four, me, sum(sizes[:c]), sizes[c], grid, after)
        sent.append([partner(parts[b], both, grid, b) if b else parts[b] for b in order])

    send([])
    if len(sizes) > 1:
        send([sent[0][0]])
    factor_two, factor_three = held([factor_two, factor_three], [sent[0][3]])
    two = spread(gathered(factor_two, "row", rows), m)
    three = jnp.concatenate(gathered(relative(factor_three, 1, fibs, fib), "slab", slabs)).T
    high, low = split_outside(three)
    three = jnp.concatenate([high, high, low], axis=1)

    for c in range(len(sizes)):
        shares = contract_two_three(sent[c], order, two, three, rows, slabs, fibs, pieces[-fibs:])
        pieces.append(shares[0])
        for b in range(1, fibs):
            pieces.append(partner(shares[b], "fib", fibs, b))
        if c + 2 < len(sizes):
            send([shares[0]])

    def local_order(x):
        y = relative(x, 0, fibs, fib).reshape(fibs, il, ranks)
        starts = [sum(sizes[:c]) for c in range(len(sizes))]
        return jnp.concatenate([y[:, at:at + n].reshape(fibs * n, ranks) for at, n in zip(starts, sizes)])

    spots = [(a, sum(sizes[:c])) for c in range(len(sizes)) for a in range(fibs)]
    here = fib.reshape(1).astype(jnp.int32)
    target = gram_times(pieces, local_order(factor_one), here, spots)
    for axis, count in (("slab", slabs), ("row", rows), ("fib", fibs)):
        target = tree_sum(gathered(target, axis, count))
    updated, ordered = orthonormal(target, here, spots)

    pairs = pieces[0].shape[1] // 2
    total = max(1, pairs // 4)
    pairs //= total
    got = []
    for n in range(total):
        parts = core_parts(pieces, ordered, me, n * pairs, pairs, grid)
        got.append([parts[0]] + [partner(parts[b], both, grid, b) for b in range(1, grid)])
    whole = []
    for n in range(total):
        whole = [assemble(got[n], me, ranks, n, total, whole)]
    return (updated, whole[0])


def solution(mesh):
    in_specs = (P("fib", "row", "slab", None), P(), P("row", None), P("slab", None), P())
    out_specs = (P(), P(None, ("row", "slab"), "fib", None))
    sizes = [mesh.shape[axis] for axis in ("fib", "row", "slab")]
    return jax.shard_map(
        functools.partial(body, *sizes), mesh=mesh, in_specs=in_specs, out_specs=out_specs, check_vma=False)
```

time: 1180 us -> 317 us (0.27)
  waiting for transfers between devices: 756 us -> 155 us
  matrix products: 221 us -> 0 us
  starting transfers between devices: 0.08 us -> 81.7 us
  local copies, waits for them, and re-layouts: 82.7 us -> 11 us
  Pallas kernels: 0 us -> 66.1 us
  blocking collectives: 53.5 us -> 0 us
  other arithmetic: 39.4 us -> 0.25 us
  between operations: 14.4 us -> 1 us
    reduce_scatter x1 -> x0, waiting for transfers between devices: 640 us -> none  [body(): lax.psum_scatter(jnp.einsum('qikr,kp->qipr', halfway, factor_three, preci...]
    dot_general x8 -> x0, matrix products: 221 us -> none  [the longest x1 112 us: body(): jnp.einsum('qikr,kp->qipr', halfway, factor_three, precision=highest)]
    ppermute x0 -> x65, waiting for transfers between devices: none -> 155 us  [partner(): return lax.ppermute(x, axes, [(s, s ^ distance) for s in range(count)])]
    psum x1 -> x0, waiting for transfers between devices: 116 us -> none  [body(): gram = lax.psum(local_gram, ('fib', 'row', 'slab'))]
    ppermute x0 -> x65, starting transfers between devices: none -> 81.7 us  [partner(): return lax.ppermute(x, axes, [(s, s ^ distance) for s in range(count)])]
    pallas_call x0 -> x16, Pallas kernels: none -> 66.1 us  [the longest x4 33.4 us: contract_four(): pl.pallas_call(kernel, grid_spec=pltpu.PrefetchScalarGridSpec(num_scalar_...]
    all_to_all x1 -> x0, blocking collectives: 53.5 us -> none  [body(): lax.all_to_all(summed, 'fib', split_axis=2, concat_axis=1, tiled=True)]
    dot_general x3 -> x0, local copies, waits for them, and re-layouts: 35 us -> none  [the longest x1 34.8 us: body(): jnp.einsum('ijkr,jq->qikr', reduced, factor_two, precision=highest)]
  transfers between devices with their start and end apart: 2 -> 65, of which waited for: 2 -> 34; matrix products, arithmetic and copies ran while one was open for 0% -> 1% of each run, Pallas kernels for 0% -> 12%
where the time goes in v1:
time: 317 us; the launch traced here: 316 us
  waiting for transfers between devices  155 us (49%)
  starting transfers between devices  81.7 us (26%)
  Pallas kernels  66.1 us (21%)
  local copies, waits for them, and re-layouts  11 us (3%)
    ppermute x65, waiting for transfers between devices, partner(): return lax.ppermute(x, axes, [(s, s ^ distance) for s in range(count)])  155 us
    ppermute x65, starting transfers between devices, partner(): return lax.ppermute(x, axes, [(s, s ^ distance) for s in range(count)])  81.7 us
    pallas_call x4, Pallas kernels, contract_four(): pl.pallas_call(kernel, grid_spec=pltpu.PrefetchScalarGridSpec(num_scalar_...  33.4 us
    unnamed x39, local copies, waits for them, and re-layouts  10.2 us
    pallas_call x4, Pallas kernels, contract_two_three(): pl.pallas_call(kernel, grid=(per,), in_specs=[pl.BlockSpec((chunk, 1, kl,...  9.62 us
    pallas_call x1, Pallas kernels, orthonormal(): pl.pallas_call(kernel, in_specs=[pl.BlockSpec(memory_space=pltpu.SMEM), p...  7.38 us
  transfers between devices with their start and end apart: 65, of which 34 were waited for; matrix products, arithmetic and copies ran while one was open for 1% of the time, Pallas kernels for 12%

profile of v1, /device:TPU:17, one launch (start us, length us, event | category | flops | bytes accessed | tf_op | source)
XLA Modules:
  0.0 315.6 jit_solution(17199772313606158153)
XLA Ops:
  1.5 8.2 %mode_four.4 = (f32[8,2,32,128]{3,2,1,0:T(8,128)S(1)}, f32[8,2,32,128]{3,2,1,0:T(8,128)S(1)}, f32[8,2,32,128]{3,2,1,0:T(8,128)S(1)}, f32[8,2,32,128]{3,2,1,0:T(8...) custom-call(s32[1]{0:T(128)} %bitcast.1.me_ref, ...), custom_call_target="tpu_custom_call" | custom-call | flops 805306368 | bytes 6291456 | tf_op jit(solution)/shard_map/mode_four/pallas_call | solution.py:109
  14.6 7.5 %collective-permute-done.3.refs_2_.refs_3_ = f32[8,2,32,128]{3,2,1,0:T(8,128)S(1)} collective-permute-done((f32[8,2,32,128]{3,2,1,0:T(8,128)S(1)}, f32[8,2,32,128]{3,2,1,0:T(8,128)S(1)}, u32[]{:S(2)}, u32[]{:S(2)}) %collective-permute-start.3) | collective-permute-done | bytes 262176 | tf_op jit(solution)/shard_map/ppermute | solution.py:46
  24.1 4.3 %collective-permute-start.8 = (f32[32,64]{1,0:T(8,128)}, f32[32,64]{1,0:T(8,128)S(1)}, u32[]{:S(2)}, u32[]{:S(2)}) collective-permute-start(f32[32,64]{1,0:T(8,128)} %get-tuple-element.78.refs_0_), channel_id=1, source_target_pairs={{0,4},{2,6},{4,0},{6,2},{1,5},{3,7},{5,1},{7,3},{8,12},{10,14},{12... | collective-permute-start | bytes 24584 | tf_op jit(solution)/shard_map/ppermute | solution.py:46
  29.6 3.7 %collective-permute-done.1.refs_1_ = f32[8,2,32,128]{3,2,1,0:T(8,128)S(1)} collective-permute-done((f32[8,2,32,128]{3,2,1,0:T(8,128)S(1)}, f32[8,2,32,128]{3,2,1,0:T(8,128)S(1)}, u32[]{:S(2)}, u32[]{:S(2)}) %collective-permute-start.1) | collective-permute-done | bytes 262176 | tf_op jit(solution)/shard_map/ppermute | solution.py:46
  33.8 14.6 %collective-permute-done.9.refs_3_ = f32[32,64]{1,0:T(8,128)S(1)} collective-permute-done((f32[32,64]{1,0:T(8,128)}, f32[32,64]{1,0:T(8,128)S(1)}, u32[]{:S(2)}, u32[]{:S(2)}) %collective-permute-start.9) | collective-permute-done | bytes 8224 | tf_op jit(solution)/shard_map/ppermute | solution.py:46
  53.8 8.2 %mode_four.5 = (f32[8,2,32,128]{3,2,1,0:T(8,128)S(1)}, f32[8,2,32,128]{3,2,1,0:T(8,128)S(1)}, f32[8,2,32,128]{3,2,1,0:T(8,128)S(1)}, f32[8,2,32,128]{3,2,1,0:T(8...) custom-call(s32[1]{0:T(128)} %bitcast.1.me_ref, ...), custom_call_target="tpu_custom_call" | custom-call | flops 805306368 | bytes 6291456 | tf_op jit(solution)/shard_map/mode_four/pallas_call | solution.py:109
  69.3 5.7 %collective-permute-done.14.refs_0_ = f32[8,2,32,128]{3,2,1,0:T(8,128)S(1)} collective-permute-done((f32[8,2,32,128]{3,2,1,0:T(8,128)S(1)}, f32[8,2,32,128]{3,2,1,0:T(8,128)S(1)}, u32[]{:S(2)}, u32[]{:S(2)}) %collective-permute-start.14) | collective-permute-done | bytes 262176 | tf_op jit(solution)/shard_map/ppermute | solution.py:46
  78.1 8.1 %collective-permute-done.16.refs_2_ = f32[8,2,32,128]{3,2,1,0:T(8,128)S(1)} collective-permute-done((f32[8,2,32,128]{3,2,1,0:T(8,128)S(1)}, f32[8,2,32,128]{3,2,1,0:T(8,128)S(1)}, u32[]{:S(2)}, u32[]{:S(2)}) %collective-permute-start.16) | collective-permute-done | bytes 262176 | tf_op jit(solution)/shard_map/ppermute | solution.py:46
  89.6 15.5 %collective-permute-done.18.refs_4_ = f32[8,2,32,128]{3,2,1,0:T(8,128)S(1)} collective-permute-done((f32[8,2,32,128]{3,2,1,0:T(8,128)S(1)}, f32[8,2,32,128]{3,2,1,0:T(8,128)S(1)}, u32[]{:S(2)}, u32[]{:S(2)}) %collective-permute-start.18) | collective-permute-done | bytes 262176 | tf_op jit(solution)/shard_map/ppermute | solution.py:46
  107.3 8.2 %mode_four.6 = (f32[8,2,32,128]{3,2,1,0:T(8,128)S(1)}, f32[8,2,32,128]{3,2,1,0:T(8,128)S(1)}, f32[8,2,32,128]{3,2,1,0:T(8,128)S(1)}, f32[8,2,32,128]{3,2,1,0:T(8...) custom-call(s32[1]{0:T(128)} %bitcast.1.me_ref, ...), custom_call_target="tpu_custom_call" | custom-call | flops 805306368 | bytes 6291456 | tf_op jit(solution)/shard_map/mode_four/pallas_call | solution.py:109
  122.0 4.4 %collective-permute-done.24.refs_0_ = f32[8,2,32,128]{3,2,1,0:T(8,128)S(1)} collective-permute-done((f32[8,2,32,128]{3,2,1,0:T(8,128)S(1)}, f32[8,2,32,128]{3,2,1,0:T(8,128)S(1)}, u32[]{:S(2)}, u32[]{:S(2)}) %collective-permute-start.24) | collective-permute-done | bytes 262176 | tf_op jit(solution)/shard_map/ppermute | solution.py:46
  126.4 3.3 %collective-permute-start.29 = (f32[8,2,32,128]{3,2,1,0:T(8,128)S(1)}, f32[8,2,32,128]{3,2,1,0:T(8,128)S(1)}, u32[]{:S(2)}, u32[]{:S(2)}) collective-permute-start(f32[8,2,32,128]{3,2,1,0:T(8,128)S(1)} %get-tuple-element.101), channel_id=1, source_target_pairs={{0,1},{1,0},{2,3},{3,2},{4,5},{5,4},{6,7},{7,6},{8,9},{9,8},{10,11... | collective-permute-start | bytes 786440 | tf_op jit(solution)/shard_map/ppermute | solution.py:46
  132.2 5.5 %collective-permute-done.26.refs_2_ = f32[8,2,32,128]{3,2,1,0:T(8,128)S(1)} collective-permute-done((f32[8,2,32,128]{3,2,1,0:T(8,128)S(1)}, f32[8,2,32,128]{3,2,1,0:T(8,128)S(1)}, u32[]{:S(2)}, u32[]{:S(2)}) %collective-permute-start.26) | collective-permute-done | bytes 262176 | tf_op jit(solution)/shard_map/ppermute | solution.py:46
  137.9 4.5 %collective-permute-done.27.refs_3_ = f32[8,2,32,128]{3,2,1,0:T(8,128)S(1)} collective-permute-done((f32[8,2,32,128]{3,2,1,0:T(8,128)S(1)}, f32[8,2,32,128]{3,2,1,0:T(8,128)S(1)}, u32[]{:S(2)}, u32[]{:S(2)}) %collective-permute-start.27) | collective-permute-done | bytes 262176 | tf_op jit(solution)/shard_map/ppermute | solution.py:46
  142.6 12.3 %collective-permute-done.28.refs_4_ = f32[8,2,32,128]{3,2,1,0:T(8,128)S(1)} collective-permute-done((f32[8,2,32,128]{3,2,1,0:T(8,128)S(1)}, f32[8,2,32,128]{3,2,1,0:T(8,128)S(1)}, u32[]{:S(2)}, u32[]{:S(2)}) %collective-permute-start.28) | collective-permute-done | bytes 262176 | tf_op jit(solution)/shard_map/ppermute | solution.py:46
  155.1 8.9 %mode_four.7 = (f32[8,2,32,128]{3,2,1,0:T(8,128)S(1)}, f32[8,2,32,128]{3,2,1,0:T(8,128)S(1)}, f32[8,2,32,128]{3,2,1,0:T(8,128)}, f32[8,2,32,128]{3,2,1,0:T(8,128...) custom-call(s32[1]{0:T(128)} %bitcast.1.me_ref, ...), custom_call_target="tpu_custom_call" | custom-call | flops 805306368 | bytes 6291456 | tf_op jit(solution)/shard_map/mode_four/pallas_call | solution.py:109
  185.3 4.9 %collective-permute-done.36.refs_2_ = f32[8,2,32,128]{3,2,1,0:T(8,128)} collective-permute-done((f32[8,2,32,128]{3,2,1,0:T(8,128)}, f32[8,2,32,128]{3,2,1,0:T(8,128)}, u32[]{:S(2)}, u32[]{:S(2)}) %collective-permute-start.36) | collective-permute-done | bytes 262176 | tf_op jit(solution)/shard_map/ppermute | solution.py:46
  191.4 3.9 %collective-permute-done.37.refs_3_ = f32[8,2,32,128]{3,2,1,0:T(8,128)} collective-permute-done((f32[8,2,32,128]{3,2,1,0:T(8,128)}, f32[8,2,32,128]{3,2,1,0:T(8,128)}, u32[]{:S(2)}, u32[]{:S(2)}) %collective-permute-start.37) | collective-permute-done | bytes 262176 | tf_op jit(solution)/shard_map/ppermute | solution.py:46
  196.6 11.0 %collective-permute-done.38.refs_4_ = f32[8,2,32,128]{3,2,1,0:T(8,128)} collective-permute-done((f32[8,2,32,128]{3,2,1,0:T(8,128)}, f32[8,2,32,128]{3,2,1,0:T(8,128)}, u32[]{:S(2)}, u32[]{:S(2)}) %collective-permute-start.38) | collective-permute-done | bytes 262176 | tf_op jit(solution)/shard_map/ppermute | solution.py:46
  209.8 4.1 %collective-permute-done.40.refs_6_ = f32[8,2,32,128]{3,2,1,0:T(8,128)S(1)} collective-permute-done((f32[8,2,32,128]{3,2,1,0:T(8,128)}, f32[8,2,32,128]{3,2,1,0:T(8,128)S(1)}, u32[]{:S(2)}, u32[]{:S(2)}) %collective-permute-start.40) | collective-permute-done | bytes 262176 | tf_op jit(solution)/shard_map/ppermute | solution.py:46
  215.4 3.1 modes_two_three.7
  226.6 3.3 %collective-permute-done.43.refs_15_ = f32[2,16,8,256]{3,2,1,0:T(8,128)S(1)} collective-permute-done((f32[2,16,8,256]{3,2,1,0:T(8,128)S(1)}, f32[2,16,8,256]{3,2,1,0:T(8,128)S(1)}, u32[]{:S(2)}, u32[]{:S(2)}) %collective-permute-start.43) | collective-permute-done | bytes 262176 | tf_op jit(solution)/shard_map/ppermute | solution.py:46
  232.9 4.3 %collective-permute-start.44 = (f32[128,64]{1,0:T(8,128)S(1)}, f32[128,64]{1,0:T(8,128)S(1)}, u32[]{:S(2)}, u32[]{:S(2)}) collective-permute-start(f32[128,64]{1,0:T(8,128)S(1)} %gram.1), channel_id=1, source_target_pairs={{0,1},{1,0},{2,3},{3,2},{4,5},{5,4},{6,7},{7,6},{8,9},{9,8},{10,11... | collective-permute-start | bytes 98312 | tf_op jit(solution)/shard_map/ppermute | solution.py:46
  249.1 7.4 %orthonormal.1 = (f32[128,64]{1,0:T(8,128)S(1)}, f32[128,64]{1,0:T(8,128)S(1)}) custom-call(s32[1]{0:T(128)} %bitcast.fib_ref, f32[128,64]{1,0:T(8,128)S(1)} %add_add_fusion.t_ref), custom_call_target="tpu_custom_call" | custom-call | tf_op jit(solution)/shard_map/orthonormal/pallas_call | solution.py:387
  258.7 3.3 %collective-permute-start.58 = (f32[4,8,8,128]{3,2,1,0:T(8,128)S(1)}, f32[4,8,8,128]{3,2,1,0:T(8,128)S(1)}, u32[]{:S(2)}, u32[]{:S(2)}) collective-permute-start(f32[4,8,8,128]{3,2,1,0:T(8,128)S(1)} %get-tuple-element.131), channel_id=1, source_target_pairs={{0,1},{1,0},{2,3},{3,2},{4,5},{5,4},{6,7},{7,6},{8,9},{9,8},{10,11... | collective-permute-start | bytes 393224 | tf_op jit(solution)/shard_map/ppermute | solution.py:46
  274.8 6.6 %collective-permute-done.62.refs_5_ = f32[4,8,8,128]{3,2,1,0:T(8,128)S(1)} collective-permute-done((f32[4,8,8,128]{3,2,1,0:T(8,128)S(1)}, f32[4,8,8,128]{3,2,1,0:T(8,128)S(1)}, u32[]{:S(2)}, u32[]{:S(2)}) %collective-permute-start.62) | collective-permute-done | bytes 131104 | tf_op jit(solution)/shard_map/ppermute | solution.py:46
  281.4 4.2 %collective-permute-start.53 = (f32[4,8,8,128]{3,2,1,0:T(8,128)}, f32[4,8,8,128]{3,2,1,0:T(8,128)S(1)}, u32[]{:S(2)}, u32[]{:S(2)}) collective-permute-start(f32[4,8,8,128]{3,2,1,0:T(8,128)} %get-tuple-element.125), channel_id=1, source_target_pairs={{0,3},{1,2},{2,1},{3,0},{4,7},{5,6},{6,5},{7,4},{8,11},{9,10},{10,... | collective-permute-start | bytes 393224 | tf_op jit(solution)/shard_map/ppermute | solution.py:46
  286.9 5.1 %collective-permute-done.64.refs_7_ = f32[4,8,8,128]{3,2,1,0:T(8,128)S(1)} collective-permute-done((f32[4,8,8,128]{3,2,1,0:T(8,128)S(1)}, f32[4,8,8,128]{3,2,1,0:T(8,128)S(1)}, u32[]{:S(2)}, u32[]{:S(2)}) %collective-permute-start.64) | collective-permute-done | bytes 131104 | tf_op jit(solution)/shard_map/ppermute | solution.py:46
  292.8 3.1 assemble.2.refs_8_
  295.9 7.5 %collective-permute-done.55.refs_5_ = f32[4,8,8,128]{3,2,1,0:T(8,128)S(1)} collective-permute-done((f32[4,8,8,128]{3,2,1,0:T(8,128)}, f32[4,8,8,128]{3,2,1,0:T(8,128)S(1)}, u32[]{:S(2)}, u32[]{:S(2)}) %collective-permute-start.55) | collective-permute-done | bytes 131104 | tf_op jit(solution)/shard_map/ppermute | solution.py:46
  303.4 6.0 %collective-permute-done.56.refs_6_ = f32[4,8,8,128]{3,2,1,0:T(8,128)S(1)} collective-permute-done((f32[4,8,8,128]{3,2,1,0:T(8,128)}, f32[4,8,8,128]{3,2,1,0:T(8,128)S(1)}, u32[]{:S(2)}, u32[]{:S(2)}) %collective-permute-start.56) | collective-permute-done | bytes 131104 | tf_op jit(solution)/shard_map/ppermute | solution.py:46
  312.5 3.1 assemble.3
  (165 shorter events, 111.0 us)
Async XLA Ops:
  11.7 21.7 %collective-permute-start.1 = (f32[8,2,32,128]{3,2,1,0:T(8,128)S(1)}, f32[8,2,32,128]{3,2,1,0:T(8,128)S(1)}, u32[]{:S(2)}, u32[]{:S(2)}) collective-permute-start(f32[8,2,32,128]{3,2,1,0:T(8,128)S(1)} %get-tuple-element.71), channel_id=1, source_target_pairs={{0,2},{1,3},{2,0},{3,1},{4,6},{5,7},{6,4},{7,5},{8,10},{9,11},{10,... | collective-permute-start | bytes 786440 | tf_op jit(solution)/shard_map/ppermute | solution.py:46
  11.8 50.3 %collective-permute-start.2 = (f32[8,2,32,128]{3,2,1,0:T(8,128)S(1)}, f32[8,2,32,128]{3,2,1,0:T(8,128)S(1)}, u32[]{:S(2)}, u32[]{:S(2)}) collective-permute-start(f32[8,2,32,128]{3,2,1,0:T(8,128)S(1)} %get-tuple-element.72), channel_id=1, source_target_pairs={{0,5},{1,4},{2,7},{3,6},{4,1},{5,0},{6,3},{7,2},{8,13},{9,12},{10,... | collective-permute-start | bytes 786440 | tf_op jit(solution)/shard_map/ppermute | solution.py:46
  24.1 24.2 %collective-permute-start.9 = (f32[32,64]{1,0:T(8,128)}, f32[32,64]{1,0:T(8,128)S(1)}, u32[]{:S(2)}, u32[]{:S(2)}) collective-permute-start(f32[32,64]{1,0:T(8,128)} %get-tuple-element.78.refs_0_), channel_id=1, source_target_pairs={{0,6},{2,4},{4,2},{6,0},{1,7},{3,5},{5,3},{7,1},{8,14},{10,12},{12... | collective-permute-start | bytes 24584 | tf_op jit(solution)/shard_map/ppermute | solution.py:46
  24.1 25.7 %collective-permute-start.8 = (f32[32,64]{1,0:T(8,128)}, f32[32,64]{1,0:T(8,128)S(1)}, u32[]{:S(2)}, u32[]{:S(2)}) collective-permute-start(f32[32,64]{1,0:T(8,128)} %get-tuple-element.78.refs_0_), channel_id=1, source_target_pairs={{0,4},{2,6},{4,0},{6,2},{1,5},{3,7},{5,1},{7,3},{8,12},{10,14},{12... | collective-permute-start | bytes 24584 | tf_op jit(solution)/shard_map/ppermute | solution.py:46
  29.3 34.2 %collective-permute-start.4 = (f32[8,2,32,128]{3,2,1,0:T(8,128)S(1)}, f32[8,2,32,128]{3,2,1,0:T(8,128)S(1)}, u32[]{:S(2)}, u32[]{:S(2)}) collective-permute-start(f32[8,2,32,128]{3,2,1,0:T(8,128)S(1)} %get-tuple-element.74), channel_id=1, source_target_pairs={{0,6},{1,7},{2,4},{3,5},{4,2},{5,3},{6,0},{7,1},{8,14},{9,15},{10,... | collective-permute-start | bytes 786440 | tf_op jit(solution)/shard_map/ppermute | solution.py:46
  33.3 30.6 %collective-permute-start.5 = (f32[8,2,32,128]{3,2,1,0:T(8,128)S(1)}, f32[8,2,32,128]{3,2,1,0:T(8,128)S(1)}, u32[]{:S(2)}, u32[]{:S(2)}) collective-permute-start(f32[8,2,32,128]{3,2,1,0:T(8,128)S(1)} %get-tuple-element.75), channel_id=1, source_target_pairs={{0,1},{1,0},{2,3},{3,2},{4,5},{5,4},{6,7},{7,6},{8,9},{9,8},{10,11... | collective-permute-start | bytes 786440 | tf_op jit(solution)/shard_map/ppermute | solution.py:46
  48.4 18.2 %collective-permute-start.6 = (f32[8,2,32,128]{3,2,1,0:T(8,128)S(1)}, f32[8,2,32,128]{3,2,1,0:T(8,128)S(1)}, u32[]{:S(2)}, u32[]{:S(2)}) collective-permute-start(f32[8,2,32,128]{3,2,1,0:T(8,128)S(1)} %get-tuple-element.76), channel_id=1, source_target_pairs={{0,7},{1,6},{2,5},{3,4},{4,3},{5,2},{6,1},{7,0},{8,15},{9,14},{10,... | collective-permute-start | bytes 786440 | tf_op jit(solution)/shard_map/ppermute | solution.py:46
  63.9 22.2 %collective-permute-start.16 = (f32[8,2,32,128]{3,2,1,0:T(8,128)S(1)}, f32[8,2,32,128]{3,2,1,0:T(8,128)S(1)}, u32[]{:S(2)}, u32[]{:S(2)}) collective-permute-start(f32[8,2,32,128]{3,2,1,0:T(8,128)S(1)} %get-tuple-element.86), channel_id=1, source_target_pairs={{0,5},{1,4},{2,7},{3,6},{4,1},{5,0},{6,3},{7,2},{8,13},{9,12},{10,... | collective-permute-start | bytes 786440 | tf_op jit(solution)/shard_map/ppermute | solution.py:46
  66.6 21.7 %collective-permute-start.17 = (f32[8,2,32,128]{3,2,1,0:T(8,128)S(1)}, f32[8,2,32,128]{3,2,1,0:T(8,128)S(1)}, u32[]{:S(2)}, u32[]{:S(2)}) collective-permute-start(f32[8,2,32,128]{3,2,1,0:T(8,128)S(1)} %get-tuple-element.87), channel_id=1, source_target_pairs={{0,3},{1,2},{2,1},{3,0},{4,7},{5,6},{6,5},{7,4},{8,11},{9,10},{10,... | collective-permute-start | bytes 786440 | tf_op jit(solution)/shard_map/ppermute | solution.py:46
  66.6 38.5 %collective-permute-start.18 = (f32[8,2,32,128]{3,2,1,0:T(8,128)S(1)}, f32[8,2,32,128]{3,2,1,0:T(8,128)S(1)}, u32[]{:S(2)}, u32[]{:S(2)}) collective-permute-start(f32[8,2,32,128]{3,2,1,0:T(8,128)S(1)} %get-tuple-element.88), channel_id=1, source_target_pairs={{0,6},{1,7},{2,4},{3,5},{4,2},{5,3},{6,0},{7,1},{8,14},{9,15},{10,... | collective-permute-start | bytes 786440 | tf_op jit(solution)/shard_map/ppermute | solution.py:46
  75.0 40.5 %collective-permute-start.19 = (f32[8,2,32,128]{3,2,1,0:T(8,128)S(1)}, f32[8,2,32,128]{3,2,1,0:T(8,128)S(1)}, u32[]{:S(2)}, u32[]{:S(2)}) collective-permute-start(f32[8,2,32,128]{3,2,1,0:T(8,128)S(1)} %get-tuple-element.89), channel_id=1, source_target_pairs={{0,1},{1,0},{2,3},{3,2},{4,5},{5,4},{6,7},{7,6},{8,9},{9,8},{10,11... | collective-permute-start | bytes 786440 | tf_op jit(solution)/shard_map/ppermute | solution.py:46
  76.4 39.1 %collective-permute-start.20 = (f32[8,2,32,128]{3,2,1,0:T(8,128)S(1)}, f32[8,2,32,128]{3,2,1,0:T(8,128)S(1)}, u32[]{:S(2)}, u32[]{:S(2)}) collective-permute-start(f32[8,2,32,128]{3,2,1,0:T(8,128)S(1)} %get-tuple-element.90), channel_id=1, source_target_pairs={{0,7},{1,6},{2,5},{3,4},{4,3},{5,2},{6,1},{7,0},{8,15},{9,14},{10,... | collective-permute-start | bytes 786440 | tf_op jit(solution)/shard_map/ppermute | solution.py:46
  86.2 30.7 %collective-permute-start.11 = (f32[2,16,8,256]{3,2,1,0:T(8,128)S(1)}, f32[2,16,8,256]{3,2,1,0:T(8,128)S(1)}, u32[]{:S(2)}, u32[]{:S(2)}) collective-permute-start(f32[2,16,8,256]{3,2,1,0:T(8,128)S(1)} %get-tuple-element.81), channel_id=1, source_target_pairs={{0,8},{8,0},{16,24},{24,16},{1,9},{9,1},{17,25},{25,17},{2,10},{10... | collective-permute-start | bytes 786440 | tf_op jit(solution)/shard_map/ppermute | solution.py:46
  88.3 30.6 %collective-permute-start.12 = (f32[2,16,8,256]{3,2,1,0:T(8,128)S(1)}, f32[2,16,8,256]{3,2,1,0:T(8,128)S(1)}, u32[]{:S(2)}, u32[]{:S(2)}) collective-permute-start(f32[2,16,8,256]{3,2,1,0:T(8,128)S(1)} %get-tuple-element.82), channel_id=1, source_target_pairs={{0,16},{8,24},{16,0},{24,8},{1,17},{9,25},{17,1},{25,9},{2,18},{10... | collective-permute-start | bytes 786440 | tf_op jit(solution)/shard_map/ppermute | solution.py:46
  116.9 20.7 %collective-permute-start.26 = (f32[8,2,32,128]{3,2,1,0:T(8,128)S(1)}, f32[8,2,32,128]{3,2,1,0:T(8,128)S(1)}, u32[]{:S(2)}, u32[]{:S(2)}) collective-permute-start(f32[8,2,32,128]{3,2,1,0:T(8,128)S(1)} %get-tuple-element.98), channel_id=1, source_target_pairs={{0,5},{1,4},{2,7},{3,6},{4,1},{5,0},{6,3},{7,2},{8,13},{9,12},{10,... | collective-permute-start | bytes 786440 | tf_op jit(solution)/shard_map/ppermute | solution.py:46
  118.9 23.5 %collective-permute-start.27 = (f32[8,2,32,128]{3,2,1,0:T(8,128)S(1)}, f32[8,2,32,128]{3,2,1,0:T(8,128)S(1)}, u32[]{:S(2)}, u32[]{:S(2)}) collective-permute-start(f32[8,2,32,128]{3,2,1,0:T(8,128)S(1)} %get-tuple-element.99), channel_id=1, source_target_pairs={{0,3},{1,2},{2,1},{3,0},{4,7},{5,6},{6,5},{7,4},{8,11},{9,10},{10,... | collective-permute-start | bytes 786440 | tf_op jit(solution)/shard_map/ppermute | solution.py:46
  119.7 35.3 %collective-permute-start.28 = (f32[8,2,32,128]{3,2,1,0:T(8,128)S(1)}, f32[8,2,32,128]{3,2,1,0:T(8,128)S(1)}, u32[]{:S(2)}, u32[]{:S(2)}) collective-permute-start(f32[8,2,32,128]{3,2,1,0:T(8,128)S(1)} %get-tuple-element.100), channel_id=1, source_target_pairs={{0,6},{1,7},{2,4},{3,5},{4,2},{5,3},{6,0},{7,1},{8,14},{9,15},{10,... | collective-permute-start | bytes 786440 | tf_op jit(solution)/shard_map/ppermute | solution.py:46
  126.4 38.4 %collective-permute-start.29 = (f32[8,2,32,128]{3,2,1,0:T(8,128)S(1)}, f32[8,2,32,128]{3,2,1,0:T(8,128)S(1)}, u32[]{:S(2)}, u32[]{:S(2)}) collective-permute-start(f32[8,2,32,128]{3,2,1,0:T(8,128)S(1)} %get-tuple-element.101), channel_id=1, source_target_pairs={{0,1},{1,0},{2,3},{3,2},{4,5},{5,4},{6,7},{7,6},{8,9},{9,8},{10,11... | collective-permute-start | bytes 786440 | tf_op jit(solution)/shard_map/ppermute | solution.py:46
  129.7 35.8 %collective-permute-start.30 = (f32[8,2,32,128]{3,2,1,0:T(8,128)S(1)}, f32[8,2,32,128]{3,2,1,0:T(8,128)S(1)}, u32[]{:S(2)}, u32[]{:S(2)}) collective-permute-start(f32[8,2,32,128]{3,2,1,0:T(8,128)S(1)} %get-tuple-element.102), channel_id=1, source_target_pairs={{0,7},{1,6},{2,5},{3,4},{4,3},{5,2},{6,1},{7,0},{8,15},{9,14},{10,... | collective-permute-start | bytes 786440 | tf_op jit(solution)/shard_map/ppermute | solution.py:46
  137.7 31.6 %collective-permute-start.21 = (f32[2,16,8,256]{3,2,1,0:T(8,128)S(1)}, f32[2,16,8,256]{3,2,1,0:T(8,128)S(1)}, u32[]{:S(2)}, u32[]{:S(2)}) collective-permute-start(f32[2,16,8,256]{3,2,1,0:T(8,128)S(1)} %get-tuple-element.93), channel_id=1, source_target_pairs={{0,8},{8,0},{16,24},{24,16},{1,9},{9,1},{17,25},{25,17},{2,10},{10... | collective-permute-start | bytes 786440 | tf_op jit(solution)/shard_map/ppermute | solution.py:46
  142.4 29.9 %collective-permute-start.22 = (f32[2,16,8,256]{3,2,1,0:T(8,128)S(1)}, f32[2,16,8,256]{3,2,1,0:T(8,128)S(1)}, u32[]{:S(2)}, u32[]{:S(2)}) collective-permute-start(f32[2,16,8,256]{3,2,1,0:T(8,128)S(1)} %get-tuple-element.94), channel_id=1, source_target_pairs={{0,16},{8,24},{16,0},{24,8},{1,17},{9,25},{17,1},{25,9},{2,18},{10... | collective-permute-start | bytes 786440 | tf_op jit(solution)/shard_map/ppermute | solution.py:46
  169.3 20.9 %collective-permute-start.36 = (f32[8,2,32,128]{3,2,1,0:T(8,128)}, f32[8,2,32,128]{3,2,1,0:T(8,128)}, u32[]{:S(2)}, u32[]{:S(2)}) collective-permute-start(f32[8,2,32,128]{3,2,1,0:T(8,128)} %get-tuple-element.110), channel_id=1, source_target_pairs={{0,5},{1,4},{2,7},{3,6},{4,1},{5,0},{6,3},{7,2},{8,13},{9,12},{10,... | collective-permute-start | bytes 786440 | tf_op jit(solution)/shard_map/ppermute | solution.py:46
  172.3 23.0 %collective-permute-start.37 = (f32[8,2,32,128]{3,2,1,0:T(8,128)}, f32[8,2,32,128]{3,2,1,0:T(8,128)}, u32[]{:S(2)}, u32[]{:S(2)}) collective-permute-start(f32[8,2,32,128]{3,2,1,0:T(8,128)} %get-tuple-element.111), channel_id=1, source_target_pairs={{0,3},{1,2},{2,1},{3,0},{4,7},{5,6},{6,5},{7,4},{8,11},{9,10},{10,... | collective-permute-start | bytes 786440 | tf_op jit(solution)/shard_map/ppermute | solution.py:46
  172.3 35.2 %collective-permute-start.38 = (f32[8,2,32,128]{3,2,1,0:T(8,128)}, f32[8,2,32,128]{3,2,1,0:T(8,128)}, u32[]{:S(2)}, u32[]{:S(2)}) collective-permute-start(f32[8,2,32,128]{3,2,1,0:T(8,128)} %get-tuple-element.112), channel_id=1, source_target_pairs={{0,6},{1,7},{2,4},{3,5},{4,2},{5,3},{6,0},{7,1},{8,14},{9,15},{10,... | collective-permute-start | bytes 786440 | tf_op jit(solution)/shard_map/ppermute | solution.py:46
  180.3 29.5 %collective-permute-start.39 = (f32[8,2,32,128]{3,2,1,0:T(8,128)}, f32[8,2,32,128]{3,2,1,0:T(8,128)S(1)}, u32[]{:S(2)}, u32[]{:S(2)}) collective-permute-start(f32[8,2,32,128]{3,2,1,0:T(8,128)} %copy-done.16), channel_id=1, source_target_pairs={{0,1},{1,0},{2,3},{3,2},{4,5},{5,4},{6,7},{7,6},{8,9},{9,8},{10,11... | collective-permute-start | bytes 786440 | tf_op jit(solution)/shard_map/ppermute | solution.py:46
  182.7 31.1 %collective-permute-start.40 = (f32[8,2,32,128]{3,2,1,0:T(8,128)}, f32[8,2,32,128]{3,2,1,0:T(8,128)S(1)}, u32[]{:S(2)}, u32[]{:S(2)}) collective-permute-start(f32[8,2,32,128]{3,2,1,0:T(8,128)} %copy-done.15), channel_id=1, source_target_pairs={{0,7},{1,6},{2,5},{3,4},{4,3},{5,2},{6,1},{7,0},{8,15},{9,14},{10,... | collective-permute-start | bytes 786440 | tf_op jit(solution)/shard_map/ppermute | solution.py:46
  190.2 23.6 %collective-permute-start.31 = (f32[2,16,8,256]{3,2,1,0:T(8,128)S(1)}, f32[2,16,8,256]{3,2,1,0:T(8,128)S(1)}, u32[]{:S(2)}, u32[]{:S(2)}) collective-permute-start(f32[2,16,8,256]{3,2,1,0:T(8,128)S(1)} %get-tuple-element.105), channel_id=1, source_target_pairs={{0,8},{8,0},{16,24},{24,16},{1,9},{9,1},{17,25},{25,17},{2,10},{10... | collective-permute-start | bytes 786440 | tf_op jit(solution)/shard_map/ppermute | solution.py:46
  195.3 18.5 %collective-permute-start.32 = (f32[2,16,8,256]{3,2,1,0:T(8,128)S(1)}, f32[2,16,8,256]{3,2,1,0:T(8,128)S(1)}, u32[]{:S(2)}, u32[]{:S(2)}) collective-permute-start(f32[2,16,8,256]{3,2,1,0:T(8,128)S(1)} %get-tuple-element.106), channel_id=1, source_target_pairs={{0,16},{8,24},{16,0},{24,8},{1,17},{9,25},{17,1},{25,9},{2,18},{10... | collective-permute-start | bytes 786440 | tf_op jit(solution)/shard_map/ppermute | solution.py:46
  269.8 22.2 %collective-permute-start.64 = (f32[4,8,8,128]{3,2,1,0:T(8,128)S(1)}, f32[4,8,8,128]{3,2,1,0:T(8,128)S(1)}, u32[]{:S(2)}, u32[]{:S(2)}) collective-permute-start(f32[4,8,8,128]{3,2,1,0:T(8,128)S(1)} %get-tuple-element.137), channel_id=1, source_target_pairs={{0,7},{1,6},{2,5},{3,4},{4,3},{5,2},{6,1},{7,0},{8,15},{9,14},{10,... | collective-permute-start | bytes 393224 | tf_op jit(solution)/shard_map/ppermute | solution.py:46
  272.1 19.9 %collective-permute-start.51 = (f32[4,8,8,128]{3,2,1,0:T(8,128)S(1)}, f32[4,8,8,128]{3,2,1,0:T(8,128)S(1)}, u32[]{:S(2)}, u32[]{:S(2)}) collective-permute-start(f32[4,8,8,128]{3,2,1,0:T(8,128)S(1)} %get-tuple-element.123), channel_id=1, source_target_pairs={{0,1},{1,0},{2,3},{3,2},{4,5},{5,4},{6,7},{7,6},{8,9},{9,8},{10,11... | collective-permute-start | bytes 393224 | tf_op jit(solution)/shard_map/ppermute | solution.py:46
  273.0 19.1 %collective-permute-start.52 = (f32[4,8,8,128]{3,2,1,0:T(8,128)S(1)}, f32[4,8,8,128]{3,2,1,0:T(8,128)S(1)}, u32[]{:S(2)}, u32[]{:S(2)}) collective-permute-start(f32[4,8,8,128]{3,2,1,0:T(8,128)S(1)} %get-tuple-element.124), channel_id=1, source_target_pairs={{0,2},{1,3},{2,0},{3,1},{4,6},{5,7},{6,4},{7,5},{8,10},{9,11},{10,... | collective-permute-start | bytes 393224 | tf_op jit(solution)/shard_map/ppermute | solution.py:46
  292.0 20.5 %collective-permute-start.57 = (f32[4,8,8,128]{3,2,1,0:T(8,128)}, f32[4,8,8,128]{3,2,1,0:T(8,128)S(1)}, u32[]{:S(2)}, u32[]{:S(2)}) collective-permute-start(f32[4,8,8,128]{3,2,1,0:T(8,128)} %get-tuple-element.129), channel_id=1, source_target_pairs={{0,7},{1,6},{2,5},{3,4},{4,3},{5,2},{6,1},{7,0},{8,15},{9,14},{10,... | collective-permute-start | bytes 393224 | tf_op jit(solution)/shard_map/ppermute | solution.py:46
  (51 other events, 462.7 us)

commit v2 on v1

--- a/solution.py
+++ b/solution.py
@@ -54,35 +54,46 @@
     return [x] + [partner(x, axes, count, b) for b in range(1, count)]
 
 
-def tree_sum(parts):
-    while len(parts) > 1:
-        parts = [a + b for a, b in zip(parts[::2], parts[1::2])]
-    return parts[0]
-
-
 def params(steps, megabytes=12):
     return pltpu.CompilerParams(
         dimension_semantics=("arbitrary",) * steps, vmem_limit_bytes=megabytes * 2 ** 20
     )
 
 
-def contract_four(tensor, factor, me, first, chunk, parts, after):
+def contract_four(tensor, factor, me, first, chunk, parts, after, riders, carriers):
     _, jl, kl, depth = tensor.shape
     ranks = factor.shape[1]
     m = LANES // jl
     groups = kl // m
     own = ranks // parts
     per = own // m
+    steps = chunk + 1 if riders else chunk
 
     def kernel(me_ref, x_ref, f_ref, *refs):
-        outs, w_ref, s_ref = refs[len(after):-2], refs[-2], refs[-1]
-
-        @pl.when(pl.program_id(0) == 0)
+        outs, w_ref, s_ref = refs[len(after) + len(riders):-2], refs[-2], refs[-1]
+        step = pl.program_id(0)
+
+        @pl.when(step == 0)
         def _():
             high, low = split(f_ref[...].T)
             w_ref[...] = jnp.concatenate(
                 [jnp.concatenate([high, high], 1), jnp.concatenate([low, jnp.zeros_like(low)], 1)], 0)
 
+        if riders:
+            @pl.when(step == chunk)
+            def _():
+                loads = jnp.concatenate([ref[...] for ref in refs[:len(riders)]], axis=1)
+                for part in carriers:
+                    outs[part][0] = jnp.zeros((per, kl, LANES), F32)
+                    outs[part][0, 0] = loads
+
+            @pl.when(step < chunk)
+            def _():
+                work(me_ref, x_ref, outs, w_ref, s_ref)
+        else:
+            work(me_ref, x_ref, outs, w_ref, s_ref)
+
+    def work(me_ref, x_ref, outs, w_ref, s_ref):
         lane = lax.broadcasted_iota(jnp.int32, (1, 1, LANES), 2)
         weights = w_ref[...]
         for group in range(groups):
@@ -110,49 +121,59 @@
         kernel,
         grid_spec=pltpu.PrefetchScalarGridSpec(
             num_scalar_prefetch=1,
-            grid=(chunk,),
+            grid=(steps,),
             in_specs=[
-                pl.BlockSpec((1, jl, kl, depth), lambda i, me: (first + i, 0, 0, 0)),
+                pl.BlockSpec((1, jl, kl, depth), lambda i, me: (first + jnp.minimum(i, chunk - 1), 0, 0, 0)),
                 pl.BlockSpec(factor.shape, lambda i, me: (0, 0)),
-            ] + [pl.BlockSpec(memory_space=pl.ANY)] * len(after),
-            out_specs=[pl.BlockSpec((1, per, kl, LANES), lambda i, me: (i, 0, 0, 0))] * parts,
+            ] + [pl.BlockSpec(rider.shape, lambda i, me: (0, 0)) for rider in riders]
+            + [pl.BlockSpec(memory_space=pl.ANY)] * len(after),
+            out_specs=[
+                pl.BlockSpec((1, per, kl, LANES), lambda i, me: (i, 0, 0, 0)) if riders and part in carriers else
+                pl.BlockSpec((1, per, kl, LANES), lambda i, me: (jnp.minimum(i, chunk - 1), 0, 0, 0))
+                for part in range(parts)],
             scratch_shapes=[
                 pltpu.VMEM((2 * ranks, 2 * depth), BF16), pltpu.VMEM((ranks, groups, LANES), F32)],
         ),
-        out_shape=[jax.ShapeDtypeStruct((chunk, per, kl, LANES), F32)] * parts,
+        out_shape=[
+            jax.ShapeDtypeStruct((steps if part in carriers else chunk, per, kl, LANES), F32)
+            for part in range(parts)],
         compiler_params=params(1),
         cost_estimate=pl.CostEstimate(
             flops=12 * chunk * jl * kl * depth * ranks, bytes_accessed=6 * chunk * jl * kl * depth, transcendentals=0
         ),
         name="mode_four",
-    )(me, tensor, factor, *after)
-
-
-def spread(pieces, m):
-    jl, ranks = pieces[0].shape
-    rows, wide = len(pieces) * m * jl, m * ranks
+    )(me, tensor, factor, *riders, *after)
+
+
+def spread(own, carried, m, after):
+    jl, ranks = own.shape
+    count = 1 + len(carried)
+    rows, wide = count * m * jl, m * ranks
 
     def kernel(*refs):
         out_ref = refs[-1]
         out_ref[...] = jnp.zeros_like(out_ref)
-        for n, ref in enumerate(refs[:-1]):
-            for half, value in enumerate(split(ref[...])):
+        for n, ref in enumerate(refs[:count]):
+            for half, value in enumerate(split(ref[0, 0, :, :ranks] if n else ref[...])):
                 for r in range(m):
                     at = (n * m + r) * jl
                     out_ref[at:at + jl, half * wide + r * ranks:half * wide + (r + 1) * ranks] = value
 
     return pl.pallas_call(
         kernel,
-        in_specs=[pl.BlockSpec(memory_space=pltpu.VMEM)] * len(pieces),
-        out_specs=pl.BlockSpec(memory_space=pltpu.VMEM),
+        grid=(1,),
+        in_specs=[pl.BlockSpec((jl, ranks), lambda s: (0, 0))]
+        + [pl.BlockSpec((1, 1, jl, LANES), lambda s, last=x.shape[0] - 1: (last, 0, 0, 0)) for x in carried]
+        + [pl.BlockSpec(memory_space=pl.ANY)] * len(after),
+        out_specs=pl.BlockSpec((rows, 2 * wide), lambda s: (0, 0)),
         out_shape=jax.ShapeDtypeStruct((rows, 2 * wide), BF16),
-        compiler_params=params(0),
+        compiler_params=params(1),
         name="spread",
-    )(*pieces)
+    )(own, *carried, *after)
 
 
 def contract_two_three(pieces, order, weights_two, weights_three, rows, slabs, targets, after):
-    chunk, per, kl, _ = pieces[0].shape
+    chunk, per, kl, _ = pieces[-1].shape
     wide = weights_two.shape[1] // 2
     ranks = weights_three.shape[0]
     share = ranks // targets
@@ -196,23 +217,6 @@
     )(*pieces, weights_two, weights_three, *after)
 
 
-def held(values, after):
-    count = len(values)
-
-    def kernel(*refs):
-        for source, target in zip(refs[:count], refs[count + len(after):]):
-            target[...] = source[...]
-
-    return pl.pallas_call(
-        kernel,
-        in_specs=[pl.BlockSpec(memory_space=pltpu.VMEM)] * count + [pl.BlockSpec(memory_space=pl.ANY)] * len(after),
-        out_specs=[pl.BlockSpec(memory_space=pltpu.VMEM)] * count,
-        out_shape=[jax.ShapeDtypeStruct(v.shape, v.dtype) for v in values],
-        compiler_params=pltpu.CompilerParams(vmem_limit_bytes=60 * 2 ** 20),
-        name="held",
-    )(*values, *after)
-
-
 def gram_times(pieces, factor, fib, spots):
     per, share, _, wide = pieces[0].shape
     count = len(pieces)
@@ -310,15 +314,15 @@
     )(me, *pieces, updated)
 
 
-def assemble(parts, me, ranks, number, total, whole):
+def assemble(parts, order, me, ranks, number, total, whole):
     pairs, own, width, lanes = parts[0].shape
     count = len(parts)
 
     def kernel(me_ref, *refs):
         ins, out_ref, s_ref = refs[:count], refs[-2], refs[-1]
         for pair in range(pairs):
-            for part in range(count):
-                s_ref[pair, pl.ds((me_ref[0] ^ part) * own, own)] = ins[part][pair]
+            for ref, part in zip(ins, order):
+                s_ref[pair, pl.ds((me_ref[0] ^ part) * own, own)] = ref[pair]
             for q in range(width):
                 turned = s_ref[pair, :, q, :].T
                 for p in range(2):
@@ -411,27 +415,32 @@
     order = [b for pair in itertools.zip_longest(far, near) for b in pair if b is not None] + [0]
     sent, pieces = [], []
 
-    def send(after):
+    carriers = [b for b in range(1, grid) if b < slabs or b % slabs == 0]
+
+    def send(after, riders=()):
         c = len(sent)
-        parts = contract_four(tensor, factor_four, me, sum(sizes[:c]), sizes[c], grid, after)
+        parts = contract_four(
+            tensor, factor_four, me, sum(sizes[:c]), sizes[c], grid, after, riders, carriers if riders else ())
         sent.append([partner(parts[b], both, grid, b) if b else parts[b] for b in order])
 
-    send([])
+    send([], [factor_two, factor_three])
     if len(sizes) > 1:
         send([sent[0][0]])
-    factor_two, factor_three = held([factor_two, factor_three], [sent[0][3]])
-    two = spread(gathered(factor_two, "row", rows), m)
-    three = jnp.concatenate(gathered(relative(factor_three, 1, fibs, fib), "slab", slabs)).T
+    two = spread(factor_two, [sent[0][order.index(b)] for b in range(slabs, grid, slabs)], m, [sent[-1][-1]])
+    three = [factor_three] + [sent[0][order.index(b)][-1, 0, :, ranks:] for b in range(1, slabs)]
+    three = relative(jnp.concatenate(three), 1, fibs, fib).T
     high, low = split_outside(three)
     three = jnp.concatenate([high, high, low], axis=1)
 
     for c in range(len(sizes)):
-        shares = contract_two_three(sent[c], order, two, three, rows, slabs, fibs, pieces[-fibs:])
+        after = pieces[max(0, c - 1) * fibs:] if c < len(sizes) - 1 else pieces[max(0, c - 2) * fibs:(c - 1) * fibs]
+        if c + 2 < len(sizes):
+            send([sent[max(c, 1)][0]])
+            after = after + [sent[-1][-1]]
+        shares = contract_two_three(sent[c], order, two, three, rows, slabs, fibs, after)
         pieces.append(shares[0])
         for b in range(1, fibs):
             pieces.append(partner(shares[b], "fib", fibs, b))
-        if c + 2 < len(sizes):
-            send([shares[0]])
 
     def local_order(x):
         y = relative(x, 0, fibs, fib).reshape(fibs, il, ranks)
@@ -442,7 +451,10 @@
     here = fib.reshape(1).astype(jnp.int32)
     target = gram_times(pieces, local_order(factor_one), here, spots)
     for axis, count in (("slab", slabs), ("row", rows), ("fib", fibs)):
-        target = tree_sum(gathered(target, axis, count))
+        distance = 1
+        while distance < count:
+            target = target + partner(target, axis, count, distance)
+            distance *= 2
     updated, ordered = orthonormal(target, here, spots)
 
     pairs = pieces[0].shape[1] // 2
@@ -451,10 +463,10 @@
     got = []
     for n in range(total):
         parts = core_parts(pieces, ordered, me, n * pairs, pairs, grid)
-        got.append([parts[0]] + [partner(parts[b], both, grid, b) for b in range(1, grid)])
+        got.append([partner(parts[b], both, grid, b) if b else parts[b] for b in order])
     whole = []
     for n in range(total):
-        whole = [assemble(got[n], me, ranks, n, total, whole)]
+        whole = [assemble(got[n], order, me, ranks, n, total, whole)]
     return (updated, whole[0])
 
 

time: 317 us -> 301 us (0.950)
  waiting for transfers between devices: 155 us -> 120 us
  starting transfers between devices: 81.7 us -> 99.4 us
    ppermute x65 -> x59, waiting for transfers between devices: 155 us -> 120 us  [partner(): return lax.ppermute(x, axes, [(s, s ^ distance) for s in range(count)])]
    ppermute x65 -> x59, starting transfers between devices: 81.7 us -> 99.4 us  [partner(): return lax.ppermute(x, axes, [(s, s ^ distance) for s in range(count)])]
    unnamed x39 -> x48, local copies, waits for them, and re-layouts: 10.2 us -> 12.4 us
  transfers between devices with their start and end apart: 65 -> 59, of which waited for: 34 -> 25; matrix products, arithmetic and copies ran while one was open for 1% -> 0% of each run, Pallas kernels for 12% -> 14%
where the time goes in v2:
time: 301 us; the launch traced here: 299 us
  waiting for transfers between devices  120 us (40%)
  starting transfers between devices  99.4 us (33%)
  Pallas kernels  66.2 us (22%)
  local copies, waits for them, and re-layouts  12.5 us (4%)
    ppermute x59, waiting for transfers between devices, partner(): return lax.ppermute(x, axes, [(s, s ^ distance) for s in range(count)])  120 us
    ppermute x59, starting transfers between devices, partner(): return lax.ppermute(x, axes, [(s, s ^ distance) for s in range(count)])  99.4 us
    pallas_call x4, Pallas kernels, contract_four(): pl.pallas_call(kernel, grid_spec=pltpu.PrefetchScalarGridSpec(num_scalar_...  34.3 us
    unnamed x48, local copies, waits for them, and re-layouts  12.4 us
    pallas_call x4, Pallas kernels, contract_two_three(): pl.pallas_call(kernel, grid=(per,), in_specs=[pl.BlockSpec((chunk, 1, kl,...  11 us
    pallas_call x1, Pallas kernels, orthonormal(): pl.pallas_call(kernel, in_specs=[pl.BlockSpec(memory_space=pltpu.SMEM), p...  7.38 us
    pallas_call x2, Pallas kernels, assemble(): pl.pallas_call(kernel, grid_spec=pltpu.PrefetchScalarGridSpec(num_scalar_...  6.23 us
  transfers between devices with their start and end apart: 59, of which 25 were waited for; matrix products, arithmetic and copies ran while one was open for 0% of the time, Pallas kernels for 14%

profile of v2, /device:TPU:17, one launch (start us, length us, event | category | flops | bytes accessed | tf_op | source)
XLA Modules:
  0.0 299.4 jit_solution(18443943062740440962)
XLA Ops:
  2.9 9.1 %mode_four.4 = (f32[8,2,32,128]{3,2,1,0:T(8,128)S(1)}, f32[9,2,32,128]{3,2,1,0:T(8,128)S(1)}, f32[9,2,32,128]{3,2,1,0:T(8,128)S(1)}, f32[8,2,32,128]{3,2,1,0:T(8...) custom-call(s32[1]{0:T(128)} %bitcast.1.me_ref, ...), custom_call_target="tpu_custom_call" | custom-call | flops 805306368 | bytes 6291456 | tf_op jit(solution)/shard_map/mode_four/pallas_call | solution.py:120
  17.5 8.2 %collective-permute-done.refs_0_.refs_2_ = f32[9,2,32,128]{3,2,1,0:T(8,128)S(1)} collective-permute-done((f32[9,2,32,128]{3,2,1,0:T(8,128)S(1)}, f32[9,2,32,128]{3,2,1,0:T(8,128)S(1)}, u32[]{:S(2)}, u32[]{:S(2)}) %collective-permute-start) | collective-permute-done | bytes 294944 | tf_op jit(solution)/shard_map/ppermute | solution.py:46
  25.7 8.2 %mode_four.5 = (f32[8,2,32,128]{3,2,1,0:T(8,128)S(1)}, f32[8,2,32,128]{3,2,1,0:T(8,128)S(1)}, f32[8,2,32,128]{3,2,1,0:T(8,128)S(1)}, f32[8,2,32,128]{3,2,1,0:T(8...) custom-call(s32[1]{0:T(128)} %bitcast.1.me_ref, ...), custom_call_target="tpu_custom_call" | custom-call | flops 805306368 | bytes 6291456 | tf_op jit(solution)/shard_map/mode_four/pallas_call | solution.py:120
  33.8 3.2 %collective-permute-start.7 = (f32[8,2,32,128]{3,2,1,0:T(8,128)S(1)}, f32[8,2,32,128]{3,2,1,0:T(8,128)S(1)}, u32[]{:S(2)}, u32[]{:S(2)}) collective-permute-start(f32[8,2,32,128]{3,2,1,0:T(8,128)S(1)} %get-tuple-element.77), channel_id=1, source_target_pairs={{0,4},{1,5},{2,6},{3,7},{4,0},{5,1},{6,2},{7,3},{8,12},{9,13},{10,... | collective-permute-start | bytes 786440 | tf_op jit(solution)/shard_map/ppermute | solution.py:46
  37.1 3.7 %collective-permute-start.6 = (f32[8,2,32,128]{3,2,1,0:T(8,128)}, f32[8,2,32,128]{3,2,1,0:T(8,128)S(1)}, u32[]{:S(2)}, u32[]{:S(2)}) collective-permute-start(f32[8,2,32,128]{3,2,1,0:T(8,128)} %get-tuple-element.74), channel_id=1, source_target_pairs={{0,7},{1,6},{2,5},{3,4},{4,3},{5,2},{6,1},{7,0},{8,15},{9,14},{10,... | collective-permute-start | bytes 786440 | tf_op jit(solution)/shard_map/ppermute | solution.py:46
  40.9 23.2 %collective-permute-done.4.refs_3_.refs_4_ = f32[9,2,32,128]{3,2,1,0:T(8,128)S(1)} collective-permute-done((f32[9,2,32,128]{3,2,1,0:T(8,128)S(1)}, f32[9,2,32,128]{3,2,1,0:T(8,128)S(1)}, u32[]{:S(2)}, u32[]{:S(2)}) %collective-permute-start.4) | collective-permute-done | bytes 294944 | tf_op jit(solution)/shard_map/ppermute | solution.py:46
  66.5 3.9 %collective-permute-start.12 = (f32[8,2,32,128]{3,2,1,0:T(8,128)S(1)}, f32[8,2,32,128]{3,2,1,0:T(8,128)S(1)}, u32[]{:S(2)}, u32[]{:S(2)}) collective-permute-start(f32[8,2,32,128]{3,2,1,0:T(8,128)S(1)} %get-tuple-element.84), channel_id=1, source_target_pairs={{0,5},{1,4},{2,7},{3,6},{4,1},{5,0},{6,3},{7,2},{8,13},{9,12},{10,... | collective-permute-start | bytes 786440 | tf_op jit(solution)/shard_map/ppermute | solution.py:46
  70.4 8.2 %mode_four.6 = (f32[8,2,32,128]{3,2,1,0:T(8,128)S(1)}, f32[8,2,32,128]{3,2,1,0:T(8,128)S(1)}, f32[8,2,32,128]{3,2,1,0:T(8,128)S(1)}, f32[8,2,32,128]{3,2,1,0:T(8...) custom-call(s32[1]{0:T(128)} %bitcast.1.me_ref, ...), custom_call_target="tpu_custom_call" | custom-call | flops 805306368 | bytes 6291456 | tf_op jit(solution)/shard_map/mode_four/pallas_call | solution.py:120
  81.5 3.0 modes_two_three.4
  85.8 16.7 %collective-permute-done.13.refs_3_ = f32[8,2,32,128]{3,2,1,0:T(8,128)S(1)} collective-permute-done((f32[8,2,32,128]{3,2,1,0:T(8,128)S(1)}, f32[8,2,32,128]{3,2,1,0:T(8,128)S(1)}, u32[]{:S(2)}, u32[]{:S(2)}) %collective-permute-start.13) | collective-permute-done | bytes 262176 | tf_op jit(solution)/shard_map/ppermute | solution.py:46
  106.0 3.2 %collective-permute-done.16.refs_6_ = f32[8,2,32,128]{3,2,1,0:T(8,128)S(1)} collective-permute-done((f32[8,2,32,128]{3,2,1,0:T(8,128)S(1)}, f32[8,2,32,128]{3,2,1,0:T(8,128)S(1)}, u32[]{:S(2)}, u32[]{:S(2)}) %collective-permute-start.16) | collective-permute-done | bytes 262176 | tf_op jit(solution)/shard_map/ppermute | solution.py:46
  110.8 4.7 %collective-permute-done.9.refs_12_.refs_2_ = f32[2,16,8,256]{3,2,1,0:T(8,128)S(1)} collective-permute-done((f32[2,16,8,256]{3,2,1,0:T(8,128)S(1)}, f32[2,16,8,256]{3,2,1,0:T(8,128)S(1)}, u32[]{:S(2)}, u32[]{:S(2)}) %collective-permute-start.9) | collective-permute-done | bytes 262176 | tf_op jit(solution)/shard_map/ppermute | solution.py:46
  115.5 3.3 %collective-permute-start.23 = (f32[8,2,32,128]{3,2,1,0:T(8,128)S(1)}, f32[8,2,32,128]{3,2,1,0:T(8,128)S(1)}, u32[]{:S(2)}, u32[]{:S(2)}) collective-permute-start(f32[8,2,32,128]{3,2,1,0:T(8,128)S(1)} %get-tuple-element.97), channel_id=1, source_target_pairs={{0,3},{1,2},{2,1},{3,0},{4,7},{5,6},{6,5},{7,4},{8,11},{9,10},{10,... | collective-permute-start | bytes 786440 | tf_op jit(solution)/shard_map/ppermute | solution.py:46
  123.1 8.8 %mode_four.7 = (f32[8,2,32,128]{3,2,1,0:T(8,128)S(1)}, f32[8,2,32,128]{3,2,1,0:T(8,128)S(1)}, f32[8,2,32,128]{3,2,1,0:T(8,128)}, f32[8,2,32,128]{3,2,1,0:T(8,128...) custom-call(s32[1]{0:T(128)} %bitcast.1.me_ref, ...), custom_call_target="tpu_custom_call" | custom-call | flops 805306368 | bytes 6291456 | tf_op jit(solution)/shard_map/mode_four/pallas_call | solution.py:120
  131.9 17.7 %collective-permute-start.30 = (f32[8,2,32,128]{3,2,1,0:T(8,128)}, f32[8,2,32,128]{3,2,1,0:T(8,128)}, u32[]{:S(2)}, u32[]{:S(2)}) collective-permute-start(f32[8,2,32,128]{3,2,1,0:T(8,128)} %get-tuple-element.105), channel_id=1, source_target_pairs={{0,4},{1,5},{2,6},{3,7},{4,0},{5,1},{6,2},{7,3},{8,12},{9,13},{10,... | collective-permute-start | bytes 786440 | tf_op jit(solution)/shard_map/ppermute | solution.py:46
  162.9 3.3 %collective-permute-start.32 = (f32[8,2,32,128]{3,2,1,0:T(8,128)}, f32[8,2,32,128]{3,2,1,0:T(8,128)S(1)}, u32[]{:S(2)}, u32[]{:S(2)}) collective-permute-start(f32[8,2,32,128]{3,2,1,0:T(8,128)} %copy-done.20), channel_id=1, source_target_pairs={{0,5},{1,4},{2,7},{3,6},{4,1},{5,0},{6,3},{7,2},{8,13},{9,12},{10,... | collective-permute-start | bytes 786440 | tf_op jit(solution)/shard_map/ppermute | solution.py:46
  168.5 2.9 collective-permute-start.35
  179.4 10.9 %collective-permute-done.33.refs_3_ = f32[8,2,32,128]{3,2,1,0:T(8,128)S(1)} collective-permute-done((f32[8,2,32,128]{3,2,1,0:T(8,128)}, f32[8,2,32,128]{3,2,1,0:T(8,128)S(1)}, u32[]{:S(2)}, u32[]{:S(2)}) %collective-permute-start.33) | collective-permute-done | bytes 262176 | tf_op jit(solution)/shard_map/ppermute | solution.py:46
  191.4 4.0 %collective-permute-done.34.refs_4_ = f32[8,2,32,128]{3,2,1,0:T(8,128)S(1)} collective-permute-done((f32[8,2,32,128]{3,2,1,0:T(8,128)}, f32[8,2,32,128]{3,2,1,0:T(8,128)S(1)}, u32[]{:S(2)}, u32[]{:S(2)}) %collective-permute-start.34) | collective-permute-done | bytes 262176 | tf_op jit(solution)/shard_map/ppermute | solution.py:46
  197.0 4.0 %collective-permute-done.36.refs_6_ = f32[8,2,32,128]{3,2,1,0:T(8,128)S(1)} collective-permute-done((f32[8,2,32,128]{3,2,1,0:T(8,128)}, f32[8,2,32,128]{3,2,1,0:T(8,128)S(1)}, u32[]{:S(2)}, u32[]{:S(2)}) %collective-permute-start.36) | collective-permute-done | bytes 262176 | tf_op jit(solution)/shard_map/ppermute | solution.py:46
  201.0 2.9 modes_two_three.7
  206.7 4.8 %collective-permute-done.37.refs_13_ = f32[2,16,8,256]{3,2,1,0:T(8,128)S(1)} collective-permute-done((f32[2,16,8,256]{3,2,1,0:T(8,128)S(1)}, f32[2,16,8,256]{3,2,1,0:T(8,128)S(1)}, u32[]{:S(2)}, u32[]{:S(2)}) %collective-permute-start.37) | collective-permute-done | bytes 262176 | tf_op jit(solution)/shard_map/ppermute | solution.py:46
  211.8 6.1 %collective-permute-done.39.refs_15_ = f32[2,16,8,256]{3,2,1,0:T(8,128)S(1)} collective-permute-done((f32[2,16,8,256]{3,2,1,0:T(8,128)S(1)}, f32[2,16,8,256]{3,2,1,0:T(8,128)S(1)}, u32[]{:S(2)}, u32[]{:S(2)}) %collective-permute-start.39) | collective-permute-done | bytes 262176 | tf_op jit(solution)/shard_map/ppermute | solution.py:46
  217.8 3.0 gram.1
  223.0 3.1 %collective-permute-done.41 = f32[128,64]{1,0:T(8,128)S(1)} collective-permute-done((f32[128,64]{1,0:T(8,128)S(1)}, f32[128,64]{1,0:T(8,128)S(1)}, u32[]{:S(2)}, u32[]{:S(2)}) %collective-permute-start.41) | collective-permute-done | bytes 32800 | tf_op jit(solution)/shard_map/ppermute | solution.py:46
  236.8 7.4 %orthonormal.1 = (f32[128,64]{1,0:T(8,128)S(1)}, f32[128,64]{1,0:T(8,128)S(1)}) custom-call(s32[1]{0:T(128)} %bitcast.fib_ref, f32[128,64]{1,0:T(8,128)S(1)} %add.36.t_ref), custom_call_target="tpu_custom_call" | custom-call | tf_op jit(solution)/shard_map/orthonormal/pallas_call | solution.py:391
  252.5 7.3 %collective-permute-start.54 = (f32[4,8,8,128]{3,2,1,0:T(8,128)S(1)}, f32[4,8,8,128]{3,2,1,0:T(8,128)S(1)}, u32[]{:S(2)}, u32[]{:S(2)}) collective-permute-start(f32[4,8,8,128]{3,2,1,0:T(8,128)S(1)} %get-tuple-element.128), channel_id=1, source_target_pairs={{0,5},{1,4},{2,7},{3,6},{4,1},{5,0},{6,3},{7,2},{8,13},{9,12},{10,... | collective-permute-start | bytes 393224 | tf_op jit(solution)/shard_map/ppermute | solution.py:46
  262.0 3.0 %collective-permute-start.57 = (f32[4,8,8,128]{3,2,1,0:T(8,128)S(1)}, f32[4,8,8,128]{3,2,1,0:T(8,128)S(1)}, u32[]{:S(2)}, u32[]{:S(2)}) collective-permute-start(f32[4,8,8,128]{3,2,1,0:T(8,128)S(1)} %get-tuple-element.131), channel_id=1, source_target_pairs={{0,1},{1,0},{2,3},{3,2},{4,5},{5,4},{6,7},{7,6},{8,9},{9,8},{10,11... | collective-permute-start | bytes 393224 | tf_op jit(solution)/shard_map/ppermute | solution.py:46
  271.1 7.0 %collective-permute-done.56.refs_4_ = f32[4,8,8,128]{3,2,1,0:T(8,128)S(1)} collective-permute-done((f32[4,8,8,128]{3,2,1,0:T(8,128)S(1)}, f32[4,8,8,128]{3,2,1,0:T(8,128)S(1)}, u32[]{:S(2)}, u32[]{:S(2)}) %collective-permute-start.56) | collective-permute-done | bytes 131104 | tf_op jit(solution)/shard_map/ppermute | solution.py:46
  283.2 5.0 %collective-permute-done.58.refs_6_ = f32[4,8,8,128]{3,2,1,0:T(8,128)S(1)} collective-permute-done((f32[4,8,8,128]{3,2,1,0:T(8,128)S(1)}, f32[4,8,8,128]{3,2,1,0:T(8,128)S(1)}, u32[]{:S(2)}, u32[]{:S(2)}) %collective-permute-start.58) | collective-permute-done | bytes 131104 | tf_op jit(solution)/shard_map/ppermute | solution.py:46
  288.8 3.1 %assemble.2.refs_8_ = f32[64,8,16,64]{3,2,1,0:T(8,128)} custom-call(s32[1]{0:T(128)} %bitcast.1.me_ref, f32[4,8,8,128]{3,2,1,0:T(8,128)S(1)} %collective-permute-done.52.refs_0_, f32[4,8,8,128]{3,2,1,0:T(8,128)S(1)} %collective-permute-done.53.refs_1_, f32[4,8,8,128]{3,2,1,0:T(8,128)S(1)} %collective-permute-done.54.refs_2_, ...), custom_call_target="tpu_custom_call" | custom-call | tf_op jit(solution)/shard_map/assemble/pallas_call | solution.py:331
  296.3 3.1 %assemble.3 = f32[64,8,16,64]{3,2,1,0:T(8,128)} custom-call(s32[1]{0:T(128)} %bitcast.1.me_ref, f32[4,8,8,128]{3,2,1,0:T(8,128)S(1)} %collective-permute-done.45.refs_0_, f32[4,8,8,128]{3,2,1,0:T(8,128)S(1)} %collective-permute-done.46.refs_1_, f32[4,8,8,128]{3,2,1,0:T(8,128)S(1)} %collective-permute-done.47.refs_2_, ...), custom_call_target="tpu_custom_call", output_to_operand_aliasing={{}: (9, {})} | custom-call | tf_op jit(solution)/shard_map/assemble/pallas_call | solution.py:331
  (165 shorter events, 92.5 us)
Async XLA Ops:
  12.7 24.4 %collective-permute-start.1 = (f32[9,2,32,128]{3,2,1,0:T(8,128)S(1)}, f32[9,2,32,128]{3,2,1,0:T(8,128)S(1)}, u32[]{:S(2)}, u32[]{:S(2)}) collective-permute-start(f32[9,2,32,128]{3,2,1,0:T(8,128)S(1)} %get-tuple-element.69), channel_id=1, source_target_pairs={{0,2},{1,3},{2,0},{3,1},{4,6},{5,7},{6,4},{7,5},{8,10},{9,11},{10,... | collective-permute-start | bytes 884744 | tf_op jit(solution)/shard_map/ppermute | solution.py:46
  14.1 64.6 %collective-permute-start.2 = (f32[8,2,32,128]{3,2,1,0:T(8,128)}, f32[8,2,32,128]{3,2,1,0:T(8,128)}, u32[]{:S(2)}, u32[]{:S(2)}) collective-permute-start(f32[8,2,32,128]{3,2,1,0:T(8,128)} %get-tuple-element.70), channel_id=1, source_target_pairs={{0,5},{1,4},{2,7},{3,6},{4,1},{5,0},{6,3},{7,2},{8,13},{9,12},{10,... | collective-permute-start | bytes 786440 | tf_op jit(solution)/shard_map/ppermute | solution.py:46
  16.9 62.8 %collective-permute-start.3 = (f32[8,2,32,128]{3,2,1,0:T(8,128)}, f32[8,2,32,128]{3,2,1,0:T(8,128)}, u32[]{:S(2)}, u32[]{:S(2)}) collective-permute-start(f32[8,2,32,128]{3,2,1,0:T(8,128)} %get-tuple-element.71), channel_id=1, source_target_pairs={{0,3},{1,2},{2,1},{3,0},{4,7},{5,6},{6,5},{7,4},{8,11},{9,10},{10,... | collective-permute-start | bytes 786440 | tf_op jit(solution)/shard_map/ppermute | solution.py:46
  17.0 47.1 %collective-permute-start.4 = (f32[9,2,32,128]{3,2,1,0:T(8,128)S(1)}, f32[9,2,32,128]{3,2,1,0:T(8,128)S(1)}, u32[]{:S(2)}, u32[]{:S(2)}) collective-permute-start(f32[9,2,32,128]{3,2,1,0:T(8,128)S(1)} %get-tuple-element.72), channel_id=1, source_target_pairs={{0,6},{1,7},{2,4},{3,5},{4,2},{5,3},{6,0},{7,1},{8,14},{9,15},{10,... | collective-permute-start | bytes 884744 | tf_op jit(solution)/shard_map/ppermute | solution.py:46
  33.8 32.6 %collective-permute-start.7 = (f32[8,2,32,128]{3,2,1,0:T(8,128)S(1)}, f32[8,2,32,128]{3,2,1,0:T(8,128)S(1)}, u32[]{:S(2)}, u32[]{:S(2)}) collective-permute-start(f32[8,2,32,128]{3,2,1,0:T(8,128)S(1)} %get-tuple-element.77), channel_id=1, source_target_pairs={{0,4},{1,5},{2,6},{3,7},{4,0},{5,1},{6,2},{7,3},{8,12},{9,13},{10,... | collective-permute-start | bytes 786440 | tf_op jit(solution)/shard_map/ppermute | solution.py:46
  37.1 43.9 %collective-permute-start.6 = (f32[8,2,32,128]{3,2,1,0:T(8,128)}, f32[8,2,32,128]{3,2,1,0:T(8,128)S(1)}, u32[]{:S(2)}, u32[]{:S(2)}) collective-permute-start(f32[8,2,32,128]{3,2,1,0:T(8,128)} %get-tuple-element.74), channel_id=1, source_target_pairs={{0,7},{1,6},{2,5},{3,4},{4,3},{5,2},{6,1},{7,0},{8,15},{9,14},{10,... | collective-permute-start | bytes 786440 | tf_op jit(solution)/shard_map/ppermute | solution.py:46
  64.1 17.3 %collective-permute-start.11 = (f32[8,2,32,128]{3,2,1,0:T(8,128)S(1)}, f32[8,2,32,128]{3,2,1,0:T(8,128)S(1)}, u32[]{:S(2)}, u32[]{:S(2)}) collective-permute-start(f32[8,2,32,128]{3,2,1,0:T(8,128)S(1)} %get-tuple-element.83), channel_id=1, source_target_pairs={{0,2},{1,3},{2,0},{3,1},{4,6},{5,7},{6,4},{7,5},{8,10},{9,11},{10,... | collective-permute-start | bytes 786440 | tf_op jit(solution)/shard_map/ppermute | solution.py:46
  66.5 18.0 %collective-permute-start.12 = (f32[8,2,32,128]{3,2,1,0:T(8,128)S(1)}, f32[8,2,32,128]{3,2,1,0:T(8,128)S(1)}, u32[]{:S(2)}, u32[]{:S(2)}) collective-permute-start(f32[8,2,32,128]{3,2,1,0:T(8,128)S(1)} %get-tuple-element.84), channel_id=1, source_target_pairs={{0,5},{1,4},{2,7},{3,6},{4,1},{5,0},{6,3},{7,2},{8,13},{9,12},{10,... | collective-permute-start | bytes 786440 | tf_op jit(solution)/shard_map/ppermute | solution.py:46
  78.6 23.8 %collective-permute-start.13 = (f32[8,2,32,128]{3,2,1,0:T(8,128)S(1)}, f32[8,2,32,128]{3,2,1,0:T(8,128)S(1)}, u32[]{:S(2)}, u32[]{:S(2)}) collective-permute-start(f32[8,2,32,128]{3,2,1,0:T(8,128)S(1)} %get-tuple-element.85), channel_id=1, source_target_pairs={{0,3},{1,2},{2,1},{3,0},{4,7},{5,6},{6,5},{7,4},{8,11},{9,10},{10,... | collective-permute-start | bytes 786440 | tf_op jit(solution)/shard_map/ppermute | solution.py:46
  79.7 24.0 %collective-permute-start.14 = (f32[8,2,32,128]{3,2,1,0:T(8,128)S(1)}, f32[8,2,32,128]{3,2,1,0:T(8,128)S(1)}, u32[]{:S(2)}, u32[]{:S(2)}) collective-permute-start(f32[8,2,32,128]{3,2,1,0:T(8,128)S(1)} %get-tuple-element.86), channel_id=1, source_target_pairs={{0,6},{1,7},{2,4},{3,5},{4,2},{5,3},{6,0},{7,1},{8,14},{9,15},{10,... | collective-permute-start | bytes 786440 | tf_op jit(solution)/shard_map/ppermute | solution.py:46
  81.1 24.6 %collective-permute-start.15 = (f32[8,2,32,128]{3,2,1,0:T(8,128)S(1)}, f32[8,2,32,128]{3,2,1,0:T(8,128)S(1)}, u32[]{:S(2)}, u32[]{:S(2)}) collective-permute-start(f32[8,2,32,128]{3,2,1,0:T(8,128)S(1)} %get-tuple-element.87), channel_id=1, source_target_pairs={{0,1},{1,0},{2,3},{3,2},{4,5},{5,4},{6,7},{7,6},{8,9},{9,8},{10,11... | collective-permute-start | bytes 786440 | tf_op jit(solution)/shard_map/ppermute | solution.py:46
  81.4 27.8 %collective-permute-start.16 = (f32[8,2,32,128]{3,2,1,0:T(8,128)S(1)}, f32[8,2,32,128]{3,2,1,0:T(8,128)S(1)}, u32[]{:S(2)}, u32[]{:S(2)}) collective-permute-start(f32[8,2,32,128]{3,2,1,0:T(8,128)S(1)} %get-tuple-element.88), channel_id=1, source_target_pairs={{0,7},{1,6},{2,5},{3,4},{4,3},{5,2},{6,1},{7,0},{8,15},{9,14},{10,... | collective-permute-start | bytes 786440 | tf_op jit(solution)/shard_map/ppermute | solution.py:46
  84.5 24.6 %collective-permute-start.8 = (f32[2,16,8,256]{3,2,1,0:T(8,128)S(1)}, f32[2,16,8,256]{3,2,1,0:T(8,128)S(1)}, u32[]{:S(2)}, u32[]{:S(2)}) collective-permute-start(f32[2,16,8,256]{3,2,1,0:T(8,128)S(1)} %get-tuple-element.80), channel_id=1, source_target_pairs={{0,8},{8,0},{16,24},{24,16},{1,9},{9,1},{17,25},{25,17},{2,10},{10... | collective-permute-start | bytes 786440 | tf_op jit(solution)/shard_map/ppermute | solution.py:46
  109.2 22.8 %collective-permute-start.22 = (f32[8,2,32,128]{3,2,1,0:T(8,128)S(1)}, f32[8,2,32,128]{3,2,1,0:T(8,128)S(1)}, u32[]{:S(2)}, u32[]{:S(2)}) collective-permute-start(f32[8,2,32,128]{3,2,1,0:T(8,128)S(1)} %get-tuple-element.96), channel_id=1, source_target_pairs={{0,5},{1,4},{2,7},{3,6},{4,1},{5,0},{6,3},{7,2},{8,13},{9,12},{10,... | collective-permute-start | bytes 786440 | tf_op jit(solution)/shard_map/ppermute | solution.py:46
  115.5 37.1 %collective-permute-start.23 = (f32[8,2,32,128]{3,2,1,0:T(8,128)S(1)}, f32[8,2,32,128]{3,2,1,0:T(8,128)S(1)}, u32[]{:S(2)}, u32[]{:S(2)}) collective-permute-start(f32[8,2,32,128]{3,2,1,0:T(8,128)S(1)} %get-tuple-element.97), channel_id=1, source_target_pairs={{0,3},{1,2},{2,1},{3,0},{4,7},{5,6},{6,5},{7,4},{8,11},{9,10},{10,... | collective-permute-start | bytes 786440 | tf_op jit(solution)/shard_map/ppermute | solution.py:46
  118.9 35.3 %collective-permute-start.24 = (f32[8,2,32,128]{3,2,1,0:T(8,128)S(1)}, f32[8,2,32,128]{3,2,1,0:T(8,128)S(1)}, u32[]{:S(2)}, u32[]{:S(2)}) collective-permute-start(f32[8,2,32,128]{3,2,1,0:T(8,128)S(1)} %get-tuple-element.98), channel_id=1, source_target_pairs={{0,6},{1,7},{2,4},{3,5},{4,2},{5,3},{6,0},{7,1},{8,14},{9,15},{10,... | collective-permute-start | bytes 786440 | tf_op jit(solution)/shard_map/ppermute | solution.py:46
  118.9 37.2 %collective-permute-start.25 = (f32[8,2,32,128]{3,2,1,0:T(8,128)S(1)}, f32[8,2,32,128]{3,2,1,0:T(8,128)S(1)}, u32[]{:S(2)}, u32[]{:S(2)}) collective-permute-start(f32[8,2,32,128]{3,2,1,0:T(8,128)S(1)} %get-tuple-element.99), channel_id=1, source_target_pairs={{0,1},{1,0},{2,3},{3,2},{4,5},{5,4},{6,7},{7,6},{8,9},{9,8},{10,11... | collective-permute-start | bytes 786440 | tf_op jit(solution)/shard_map/ppermute | solution.py:46
  120.6 39.4 %collective-permute-start.26 = (f32[8,2,32,128]{3,2,1,0:T(8,128)S(1)}, f32[8,2,32,128]{3,2,1,0:T(8,128)S(1)}, u32[]{:S(2)}, u32[]{:S(2)}) collective-permute-start(f32[8,2,32,128]{3,2,1,0:T(8,128)S(1)} %get-tuple-element.100), channel_id=1, source_target_pairs={{0,7},{1,6},{2,5},{3,4},{4,3},{5,2},{6,1},{7,0},{8,15},{9,14},{10,... | collective-permute-start | bytes 786440 | tf_op jit(solution)/shard_map/ppermute | solution.py:46
  131.9 31.0 %collective-permute-start.30 = (f32[8,2,32,128]{3,2,1,0:T(8,128)}, f32[8,2,32,128]{3,2,1,0:T(8,128)}, u32[]{:S(2)}, u32[]{:S(2)}) collective-permute-start(f32[8,2,32,128]{3,2,1,0:T(8,128)} %get-tuple-element.105), channel_id=1, source_target_pairs={{0,4},{1,5},{2,6},{3,7},{4,0},{5,1},{6,2},{7,3},{8,12},{9,13},{10,... | collective-permute-start | bytes 786440 | tf_op jit(solution)/shard_map/ppermute | solution.py:46
  162.9 16.4 %collective-permute-start.32 = (f32[8,2,32,128]{3,2,1,0:T(8,128)}, f32[8,2,32,128]{3,2,1,0:T(8,128)S(1)}, u32[]{:S(2)}, u32[]{:S(2)}) collective-permute-start(f32[8,2,32,128]{3,2,1,0:T(8,128)} %copy-done.20), channel_id=1, source_target_pairs={{0,5},{1,4},{2,7},{3,6},{4,1},{5,0},{6,3},{7,2},{8,13},{9,12},{10,... | collective-permute-start | bytes 786440 | tf_op jit(solution)/shard_map/ppermute | solution.py:46
  166.2 24.0 %collective-permute-start.33 = (f32[8,2,32,128]{3,2,1,0:T(8,128)}, f32[8,2,32,128]{3,2,1,0:T(8,128)S(1)}, u32[]{:S(2)}, u32[]{:S(2)}) collective-permute-start(f32[8,2,32,128]{3,2,1,0:T(8,128)} %copy-done.19), channel_id=1, source_target_pairs={{0,3},{1,2},{2,1},{3,0},{4,7},{5,6},{6,5},{7,4},{8,11},{9,10},{10,... | collective-permute-start | bytes 786440 | tf_op jit(solution)/shard_map/ppermute | solution.py:46
  167.2 28.2 %collective-permute-start.34 = (f32[8,2,32,128]{3,2,1,0:T(8,128)}, f32[8,2,32,128]{3,2,1,0:T(8,128)S(1)}, u32[]{:S(2)}, u32[]{:S(2)}) collective-permute-start(f32[8,2,32,128]{3,2,1,0:T(8,128)} %copy-done.18), channel_id=1, source_target_pairs={{0,6},{1,7},{2,4},{3,5},{4,2},{5,3},{6,0},{7,1},{8,14},{9,15},{10,... | collective-permute-start | bytes 786440 | tf_op jit(solution)/shard_map/ppermute | solution.py:46
  168.5 28.5 %collective-permute-start.35 = (f32[8,2,32,128]{3,2,1,0:T(8,128)}, f32[8,2,32,128]{3,2,1,0:T(8,128)S(1)}, u32[]{:S(2)}, u32[]{:S(2)}) collective-permute-start(f32[8,2,32,128]{3,2,1,0:T(8,128)} %copy-done.17), channel_id=1, source_target_pairs={{0,1},{1,0},{2,3},{3,2},{4,5},{5,4},{6,7},{7,6},{8,9},{9,8},{10,11... | collective-permute-start | bytes 786440 | tf_op jit(solution)/shard_map/ppermute | solution.py:46
  171.4 29.6 %collective-permute-start.36 = (f32[8,2,32,128]{3,2,1,0:T(8,128)}, f32[8,2,32,128]{3,2,1,0:T(8,128)S(1)}, u32[]{:S(2)}, u32[]{:S(2)}) collective-permute-start(f32[8,2,32,128]{3,2,1,0:T(8,128)} %copy-done.16), channel_id=1, source_target_pairs={{0,7},{1,6},{2,5},{3,4},{4,3},{5,2},{6,1},{7,0},{8,15},{9,14},{10,... | collective-permute-start | bytes 786440 | tf_op jit(solution)/shard_map/ppermute | solution.py:46
  179.3 26.5 %collective-permute-start.27 = (f32[2,16,8,256]{3,2,1,0:T(8,128)S(1)}, f32[2,16,8,256]{3,2,1,0:T(8,128)S(1)}, u32[]{:S(2)}, u32[]{:S(2)}) collective-permute-start(f32[2,16,8,256]{3,2,1,0:T(8,128)S(1)} %get-tuple-element.102), channel_id=1, source_target_pairs={{0,8},{8,0},{16,24},{24,16},{1,9},{9,1},{17,25},{25,17},{2,10},{10... | collective-permute-start | bytes 786440 | tf_op jit(solution)/shard_map/ppermute | solution.py:46
  190.3 16.4 %collective-permute-start.28 = (f32[2,16,8,256]{3,2,1,0:T(8,128)S(1)}, f32[2,16,8,256]{3,2,1,0:T(8,128)S(1)}, u32[]{:S(2)}, u32[]{:S(2)}) collective-permute-start(f32[2,16,8,256]{3,2,1,0:T(8,128)S(1)} %get-tuple-element.103), channel_id=1, source_target_pairs={{0,16},{8,24},{16,0},{24,8},{1,17},{9,25},{17,1},{25,9},{2,18},{10... | collective-permute-start | bytes 786440 | tf_op jit(solution)/shard_map/ppermute | solution.py:46
  252.5 16.0 %collective-permute-start.54 = (f32[4,8,8,128]{3,2,1,0:T(8,128)S(1)}, f32[4,8,8,128]{3,2,1,0:T(8,128)S(1)}, u32[]{:S(2)}, u32[]{:S(2)}) collective-permute-start(f32[4,8,8,128]{3,2,1,0:T(8,128)S(1)} %get-tuple-element.128), channel_id=1, source_target_pairs={{0,5},{1,4},{2,7},{3,6},{4,1},{5,0},{6,3},{7,2},{8,13},{9,12},{10,... | collective-permute-start | bytes 393224 | tf_op jit(solution)/shard_map/ppermute | solution.py:46
  261.5 16.6 %collective-permute-start.56 = (f32[4,8,8,128]{3,2,1,0:T(8,128)S(1)}, f32[4,8,8,128]{3,2,1,0:T(8,128)S(1)}, u32[]{:S(2)}, u32[]{:S(2)}) collective-permute-start(f32[4,8,8,128]{3,2,1,0:T(8,128)S(1)} %get-tuple-element.130), channel_id=1, source_target_pairs={{0,6},{1,7},{2,4},{3,5},{4,2},{5,3},{6,0},{7,1},{8,14},{9,15},{10,... | collective-permute-start | bytes 393224 | tf_op jit(solution)/shard_map/ppermute | solution.py:46
  262.0 18.8 %collective-permute-start.57 = (f32[4,8,8,128]{3,2,1,0:T(8,128)S(1)}, f32[4,8,8,128]{3,2,1,0:T(8,128)S(1)}, u32[]{:S(2)}, u32[]{:S(2)}) collective-permute-start(f32[4,8,8,128]{3,2,1,0:T(8,128)S(1)} %get-tuple-element.131), channel_id=1, source_target_pairs={{0,1},{1,0},{2,3},{3,2},{4,5},{5,4},{6,7},{7,6},{8,9},{9,8},{10,11... | collective-permute-start | bytes 393224 | tf_op jit(solution)/shard_map/ppermute | solution.py:46
  265.0 23.1 %collective-permute-start.58 = (f32[4,8,8,128]{3,2,1,0:T(8,128)S(1)}, f32[4,8,8,128]{3,2,1,0:T(8,128)S(1)}, u32[]{:S(2)}, u32[]{:S(2)}) collective-permute-start(f32[4,8,8,128]{3,2,1,0:T(8,128)S(1)} %get-tuple-element.132), channel_id=1, source_target_pairs={{0,7},{1,6},{2,5},{3,4},{4,3},{5,2},{6,1},{7,0},{8,15},{9,14},{10,... | collective-permute-start | bytes 393224 | tf_op jit(solution)/shard_map/ppermute | solution.py:46
  268.5 23.5 %collective-permute-start.47 = (f32[4,8,8,128]{3,2,1,0:T(8,128)S(1)}, f32[4,8,8,128]{3,2,1,0:T(8,128)S(1)}, u32[]{:S(2)}, u32[]{:S(2)}) collective-permute-start(f32[4,8,8,128]{3,2,1,0:T(8,128)S(1)} %get-tuple-element.120), channel_id=1, source_target_pairs={{0,5},{1,4},{2,7},{3,6},{4,1},{5,0},{6,3},{7,2},{8,13},{9,12},{10,... | collective-permute-start | bytes 393224 | tf_op jit(solution)/shard_map/ppermute | solution.py:46
  269.4 22.5 %collective-permute-start.48 = (f32[4,8,8,128]{3,2,1,0:T(8,128)S(1)}, f32[4,8,8,128]{3,2,1,0:T(8,128)S(1)}, u32[]{:S(2)}, u32[]{:S(2)}) collective-permute-start(f32[4,8,8,128]{3,2,1,0:T(8,128)S(1)} %get-tuple-element.121), channel_id=1, source_target_pairs={{0,3},{1,2},{2,1},{3,0},{4,7},{5,6},{6,5},{7,4},{8,11},{9,10},{10,... | collective-permute-start | bytes 393224 | tf_op jit(solution)/shard_map/ppermute | solution.py:46
  (49 other events, 548.7 us)

commit v3 on v2

--- a/solution.py
+++ b/solution.py
@@ -13,6 +13,7 @@
 HIGHEST = lax.Precision.HIGHEST
 LANES = 128
 TILE = 8
+PIVOTS = 4
 NT = (((1,), (1,)), ((), ()))
 NN = (((1,), (0,)), ((), ()))
 
@@ -62,22 +63,26 @@
 
 def contract_four(tensor, factor, me, first, chunk, parts, after, riders, carriers):
     _, jl, kl, depth = tensor.shape
-    ranks = factor.shape[1]
+    ranks = factor.shape[0]
     m = LANES // jl
     groups = kl // m
+    cuts = 4
     own = ranks // parts
     per = own // m
     steps = chunk + 1 if riders else chunk
 
-    def kernel(me_ref, x_ref, f_ref, *refs):
+    def kernel(me_ref, *refs):
+        x_refs, f_ref, refs = refs[:cuts], refs[cuts], refs[cuts + 1:]
         outs, w_ref, s_ref = refs[len(after) + len(riders):-2], refs[-2], refs[-1]
         step = pl.program_id(0)
 
         @pl.when(step == 0)
         def _():
             high, low = split(f_ref[...].T)
+            none = jnp.zeros_like(high)
+            left, right = [jnp.concatenate(pair, axis=1) for pair in ((high, none), (none, high))]
             w_ref[...] = jnp.concatenate(
-                [jnp.concatenate([high, high], 1), jnp.concatenate([low, jnp.zeros_like(low)], 1)], 0)
+                [left, left, right, right, jnp.concatenate([low, none], 1), jnp.concatenate([none, low], 1)], 0)
 
         if riders:
             @pl.when(step == chunk)
@@ -89,18 +94,25 @@
 
             @pl.when(step < chunk)
             def _():
-                work(me_ref, x_ref, outs, w_ref, s_ref)
+                work(me_ref, x_refs, outs, w_ref, s_ref)
         else:
-            work(me_ref, x_ref, outs, w_ref, s_ref)
-
-    def work(me_ref, x_ref, outs, w_ref, s_ref):
+            work(me_ref, x_refs, outs, w_ref, s_ref)
+
+    def work(me_ref, x_refs, outs, w_ref, s_ref):
         lane = lax.broadcasted_iota(jnp.int32, (1, 1, LANES), 2)
-        weights = w_ref[...]
-        for group in range(groups):
-            rows = jnp.concatenate([x_ref[0, :, q * groups + group, :] for q in range(m)], axis=0)
-            high, low = split(rows)
-            found = dot(weights, jnp.concatenate([high, low], axis=1), NT)
-            s_ref[:, group, :] = found[:ranks] + found[ranks:]
+        half = groups // 2
+        found = []
+        for side in range(2):
+            rows = jnp.concatenate([
+                x_ref[0, :, q * groups + side * half + n, :]
+                for n in range(half) for q in range(m) for x_ref in x_refs], axis=0)
+            found += split(rows)
+        found = dot(jnp.concatenate(found, axis=1), w_ref[:4 * depth]) + dot(
+            jnp.concatenate(found[::2], axis=1), w_ref[4 * depth:])
+        for n in range(half):
+            turned = found[n * LANES:(n + 1) * LANES].T
+            s_ref[:, n, :] = turned[:ranks]
+            s_ref[:, half + n, :] = turned[ranks:]
         for part in range(parts):
             mine = s_ref[pl.ds((me_ref[0] ^ part) * own, own)].reshape(per, m, groups, LANES)
             blocks = [mine[:, q] for q in range(m)]
@@ -123,7 +135,10 @@
             num_scalar_prefetch=1,
             grid=(steps,),
             in_specs=[
-                pl.BlockSpec((1, jl, kl, depth), lambda i, me: (first + jnp.minimum(i, chunk - 1), 0, 0, 0)),
+                pl.BlockSpec(
+                    (1, jl // cuts, kl, depth),
+                    lambda i, me, cut=cut: (first + jnp.minimum(i, chunk - 1), cut, 0, 0)) for cut in range(cuts)
+            ] + [
                 pl.BlockSpec(factor.shape, lambda i, me: (0, 0)),
             ] + [pl.BlockSpec(rider.shape, lambda i, me: (0, 0)) for rider in riders]
             + [pl.BlockSpec(memory_space=pl.ANY)] * len(after),
@@ -132,7 +147,7 @@
                 pl.BlockSpec((1, per, kl, LANES), lambda i, me: (jnp.minimum(i, chunk - 1), 0, 0, 0))
                 for part in range(parts)],
             scratch_shapes=[
-                pltpu.VMEM((2 * ranks, 2 * depth), BF16), pltpu.VMEM((ranks, groups, LANES), F32)],
+                pltpu.VMEM((6 * depth, 2 * ranks), BF16), pltpu.VMEM((ranks, groups, LANES), F32)],
         ),
         out_shape=[
             jax.ShapeDtypeStruct((steps if part in carriers else chunk, per, kl, LANES), F32)
@@ -142,7 +157,7 @@
             flops=12 * chunk * jl * kl * depth * ranks, bytes_accessed=6 * chunk * jl * kl * depth, transcendentals=0
         ),
         name="mode_four",
-    )(me, tensor, factor, *riders, *after)
+    )(me, *[tensor] * cuts, factor, *riders, *after)
 
 
 def spread(own, carried, m, after):
@@ -362,24 +377,28 @@
                 z, z, (((0,), (0,)), ((), ())), precision=HIGHEST, preferred_element_type=F32)
             whole = jnp.concatenate([crossed, eye], axis=1)
             blocks = [whole[b * tile:(b + 1) * tile] for b in range(ranks // tile)]
-            for k in range(0, ranks, 2):
+            for k in range(0, ranks, PIVOTS):
                 home, spot = divmod(k, tile)
-                first = {b: jnp.broadcast_to(blocks[b][:, k:k + 1], (tile, 2 * ranks))
-                         for b in range(home, len(blocks))}
-                second = {b: jnp.broadcast_to(blocks[b][:, k + 1:k + 2], (tile, 2 * ranks))
-                          for b in range(home, len(blocks))}
-                scale_one = lax.rsqrt(first[home][spot:spot + 1])
-                side = first[home][spot + 1:spot + 2] * scale_one
-                scale_two = lax.rsqrt(second[home][spot + 1:spot + 2] - side * side)
-                one = blocks[home][spot:spot + 1] * scale_one
-                two = (blocks[home][spot + 1:spot + 2] - side * one) * scale_two
+                columns = [
+                    {b: jnp.broadcast_to(blocks[b][:, k + t:k + t + 1], (tile, 2 * ranks))
+                     for b in range(home, len(blocks))} for t in range(PIVOTS)]
+                tops = [blocks[home][spot + t:spot + t + 1] for t in range(PIVOTS)]
+                for t in range(PIVOTS):
+                    scale = lax.rsqrt(columns[t][home][spot + t:spot + t + 1])
+                    tops[t] = tops[t] * scale
+                    columns[t] = {b: column * scale for b, column in columns[t].items()}
+                    for u in range(t + 1, PIVOTS):
+                        side = columns[t][home][spot + u:spot + u + 1]
+                        tops[u] = tops[u] - side * tops[t]
+                        columns[u] = {b: column - side * columns[t][b] for b, column in columns[u].items()}
                 for b in range(home, len(blocks)):
-                    left = first[b] * scale_one
-                    right = (second[b] - side * left) * scale_two
-                    fresh = blocks[b] - left * one - right * two
+                    fresh = blocks[b]
+                    for t in range(PIVOTS):
+                        fresh = fresh - columns[t][b] * tops[t]
                     if b == home:
-                        fresh = jnp.where(row > spot + 1, fresh, blocks[b])
-                        fresh = jnp.where(row == spot, one, jnp.where(row == spot + 1, two, fresh))
+                        fresh = jnp.where(row >= spot + PIVOTS, fresh, blocks[b])
+                        for t in range(PIVOTS):
+                            fresh = jnp.where(row == spot + t, tops[t], fresh)
                     blocks[b] = fresh
             inverse = jnp.concatenate(blocks, axis=0)[:, ranks:]
             z = lax.dot_general(z, inverse, NT, precision=HIGHEST, preferred_element_type=F32)
@@ -420,10 +439,10 @@
     def send(after, riders=()):
         c = len(sent)
         parts = contract_four(
-            tensor, factor_four, me, sum(sizes[:c]), sizes[c], grid, after, riders, carriers if riders else ())
+            tensor, factor_four.T, me, sum(sizes[:c]), sizes[c], grid, after, riders, carriers if riders else ())
         sent.append([partner(parts[b], both, grid, b) if b else parts[b] for b in order])
 
-    send([], [factor_two, factor_three])
+    send([], [in_hbm(factor_two), in_hbm(factor_three)])
     if len(sizes) > 1:
         send([sent[0][0]])
     two = spread(factor_two, [sent[0][order.index(b)] for b in range(slabs, grid, slabs)], m, [sent[-1][-1]])
@@ -435,7 +454,7 @@
     for c in range(len(sizes)):
         after = pieces[max(0, c - 1) * fibs:] if c < len(sizes) - 1 else pieces[max(0, c - 2) * fibs:(c - 1) * fibs]
         if c + 2 < len(sizes):
-            send([sent[max(c, 1)][0]])
+            send([sent[1][1 - c]])
             after = after + [sent[-1][-1]]
         shares = contract_two_three(sent[c], order, two, three, rows, slabs, fibs, after)
         pieces.append(shares[0])

time: 301 us -> 298 us (0.990)
  starting transfers between devices: 99.4 us -> 88 us
  waiting for transfers between devices: 120 us -> 125 us
  local copies, waits for them, and re-layouts: 12.5 us -> 16.1 us
    ppermute x59, starting transfers between devices: 99.4 us -> 88 us  [partner(): return lax.ppermute(x, axes, [(s, s ^ distance) for s in range(count)])]
    ppermute x59, waiting for transfers between devices: 120 us -> 125 us  [partner(): return lax.ppermute(x, axes, [(s, s ^ distance) for s in range(count)])]
    unnamed x48 -> x45, local copies, waits for them, and re-layouts: 12.4 us -> 15.9 us
  transfers between devices with their start and end apart: 59 -> 59, of which waited for: 25 -> 26; matrix products, arithmetic and copies ran while one was open for 0% -> 1% of each run, Pallas kernels for 14% -> 15%
where the time goes in v3:
time: 298 us; the launch traced here: 297 us
  waiting for transfers between devices  125 us (42%)
  starting transfers between devices  88 us (30%)
  Pallas kernels  67.1 us (23%)
  local copies, waits for them, and re-layouts  16.1 us (5%)
    ppermute x59, waiting for transfers between devices, partner(): return lax.ppermute(x, axes, [(s, s ^ distance) for s in range(count)])  125 us
    ppermute x59, starting transfers between devices, partner(): return lax.ppermute(x, axes, [(s, s ^ distance) for s in range(count)])  88 us
    pallas_call x4, Pallas kernels, contract_four(): pl.pallas_call(kernel, grid_spec=pltpu.PrefetchScalarGridSpec(num_scalar_...  36.5 us
    unnamed x45, local copies, waits for them, and re-layouts  15.9 us
    pallas_call x4, Pallas kernels, contract_two_three(): pl.pallas_call(kernel, grid=(per,), in_specs=[pl.BlockSpec((chunk, 1, kl,...  11.1 us
    pallas_call x2, Pallas kernels, assemble(): pl.pallas_call(kernel, grid_spec=pltpu.PrefetchScalarGridSpec(num_scalar_...  6.23 us
  transfers between devices with their start and end apart: 59, of which 26 were waited for; matrix products, arithmetic and copies ran while one was open for 1% of the time, Pallas kernels for 15%

profile of v3, /device:TPU:17, one launch (start us, length us, event | category | flops | bytes accessed | tf_op | source)
XLA Modules:
  0.0 296.9 jit_solution(11847112326128811315)
XLA Ops:
  1.4 9.7 %mode_four.4 = (f32[8,2,32,128]{3,2,1,0:T(8,128)S(1)}, f32[9,2,32,128]{3,2,1,0:T(8,128)S(1)}, f32[9,2,32,128]{3,2,1,0:T(8,128)S(1)}, f32[8,2,32,128]{3,2,1,0:T(8...) custom-call(s32[1]{0:T(128)} %bitcast.1.me_ref, ...), custom_call_target="tpu_custom_call" | custom-call | flops 805306368 | bytes 6291456 | tf_op jit(solution)/shard_map/mode_four/pallas_call | solution.py:132
  16.6 8.1 %collective-permute-done.refs_5_.refs_2_.refs_0_ = f32[9,2,32,128]{3,2,1,0:T(8,128)S(1)} collective-permute-done((f32[9,2,32,128]{3,2,1,0:T(8,128)S(1)}, f32[9,2,32,128]{3,2,1,0:T(8,128)S(1)}, u32[]{:S(2)}, u32[]{:S(2)}) %collective-permute-start) | collective-permute-done | bytes 294944 | tf_op jit(solution)/shard_map/ppermute | solution.py:47
  24.7 8.7 %mode_four.5 = (f32[8,2,32,128]{3,2,1,0:T(8,128)S(1)}, f32[8,2,32,128]{3,2,1,0:T(8,128)S(1)}, f32[8,2,32,128]{3,2,1,0:T(8,128)S(1)}, f32[8,2,32,128]{3,2,1,0:T(8...) custom-call(s32[1]{0:T(128)} %bitcast.1.me_ref, ...), custom_call_target="tpu_custom_call" | custom-call | flops 805306368 | bytes 6291456 | tf_op jit(solution)/shard_map/mode_four/pallas_call | solution.py:132
  33.5 5.0 %collective-permute-start.7 = (f32[8,2,32,128]{3,2,1,0:T(8,128)S(1)}, f32[8,2,32,128]{3,2,1,0:T(8,128)S(1)}, u32[]{:S(2)}, u32[]{:S(2)}) collective-permute-start(f32[8,2,32,128]{3,2,1,0:T(8,128)S(1)} %get-tuple-element.77), channel_id=1, source_target_pairs={{0,2},{1,3},{2,0},{3,1},{4,6},{5,7},{6,4},{7,5},{8,10},{9,11},{10,... | collective-permute-start | bytes 786440 | tf_op jit(solution)/shard_map/ppermute | solution.py:47
  38.6 18.9 %collective-permute-done.4.refs_3_.refs_4_ = f32[9,2,32,128]{3,2,1,0:T(8,128)S(1)} collective-permute-done((f32[9,2,32,128]{3,2,1,0:T(8,128)S(1)}, f32[9,2,32,128]{3,2,1,0:T(8,128)S(1)}, u32[]{:S(2)}, u32[]{:S(2)}) %collective-permute-start.4) | collective-permute-done | bytes 294944 | tf_op jit(solution)/shard_map/ppermute | solution.py:47
  57.7 3.1 %collective-permute-start.12 = (f32[8,2,32,128]{3,2,1,0:T(8,128)S(1)}, f32[8,2,32,128]{3,2,1,0:T(8,128)S(1)}, u32[]{:S(2)}, u32[]{:S(2)}) collective-permute-start(f32[8,2,32,128]{3,2,1,0:T(8,128)S(1)} %get-tuple-element.84), channel_id=1, source_target_pairs={{0,5},{1,4},{2,7},{3,6},{4,1},{5,0},{6,3},{7,2},{8,13},{9,12},{10,... | collective-permute-start | bytes 786440 | tf_op jit(solution)/shard_map/ppermute | solution.py:47
  60.8 8.8 %mode_four.6 = (f32[8,2,32,128]{3,2,1,0:T(8,128)S(1)}, f32[8,2,32,128]{3,2,1,0:T(8,128)S(1)}, f32[8,2,32,128]{3,2,1,0:T(8,128)S(1)}, f32[8,2,32,128]{3,2,1,0:T(8...) custom-call(s32[1]{0:T(128)} %bitcast.1.me_ref, ...), custom_call_target="tpu_custom_call" | custom-call | flops 805306368 | bytes 6291456 | tf_op jit(solution)/shard_map/mode_four/pallas_call | solution.py:132
  70.0 4.5 %collective-permute-done.6.refs_6_ = f32[8,2,32,128]{3,2,1,0:T(8,128)S(1)} collective-permute-done((f32[8,2,32,128]{3,2,1,0:T(8,128)}, f32[8,2,32,128]{3,2,1,0:T(8,128)S(1)}, u32[]{:S(2)}, u32[]{:S(2)}) %collective-permute-start.6) | collective-permute-done | bytes 262176 | tf_op jit(solution)/shard_map/ppermute | solution.py:47
  77.4 7.9 %collective-permute-start.16 = (f32[8,2,32,128]{3,2,1,0:T(8,128)S(1)}, f32[8,2,32,128]{3,2,1,0:T(8,128)S(1)}, u32[]{:S(2)}, u32[]{:S(2)}) collective-permute-start(f32[8,2,32,128]{3,2,1,0:T(8,128)S(1)} %get-tuple-element.88), channel_id=1, source_target_pairs={{0,7},{1,6},{2,5},{3,4},{4,3},{5,2},{6,1},{7,0},{8,15},{9,14},{10,... | collective-permute-start | bytes 786440 | tf_op jit(solution)/shard_map/ppermute | solution.py:47
  85.3 3.0 %modes_two_three.4 = (f32[2,16,8,256]{3,2,1,0:T(8,128)S(1)}, f32[2,16,8,256]{3,2,1,0:T(8,128)S(1)}, f32[2,16,8,256]{3,2,1,0:T(8,128)S(1)}, f32[2,16,8,256]{3,2,1,0:T(8,128)S(1)}) custom-call(f32[9,2,32,128]{3,2,1,0:T(8,128)S(1)} %collective-permute-done.refs_5_.refs_2_.refs_0_, f32[9,2,32,128]{3,2,1,0:T(8,128)S(1)} %collective-permute-done.1.refs_1_, ...), custom_call_target="tpu_custom_call" | custom-call | flops 905969664 | bytes 4194304 | tf_op jit(solution)/shard_map/modes_two_three/pallas_call | solution.py:215
  89.6 8.7 %collective-permute-done.13.refs_3_ = f32[8,2,32,128]{3,2,1,0:T(8,128)S(1)} collective-permute-done((f32[8,2,32,128]{3,2,1,0:T(8,128)S(1)}, f32[8,2,32,128]{3,2,1,0:T(8,128)S(1)}, u32[]{:S(2)}, u32[]{:S(2)}) %collective-permute-start.13) | collective-permute-done | bytes 262176 | tf_op jit(solution)/shard_map/ppermute | solution.py:47
  99.5 3.0 %collective-permute-done.14.refs_4_ = f32[8,2,32,128]{3,2,1,0:T(8,128)S(1)} collective-permute-done((f32[8,2,32,128]{3,2,1,0:T(8,128)S(1)}, f32[8,2,32,128]{3,2,1,0:T(8,128)S(1)}, u32[]{:S(2)}, u32[]{:S(2)}) %collective-permute-start.14) | collective-permute-done | bytes 262176 | tf_op jit(solution)/shard_map/ppermute | solution.py:47
  104.7 3.5 %collective-permute-done.16.refs_6_ = f32[8,2,32,128]{3,2,1,0:T(8,128)S(1)} collective-permute-done((f32[8,2,32,128]{3,2,1,0:T(8,128)S(1)}, f32[8,2,32,128]{3,2,1,0:T(8,128)S(1)}, u32[]{:S(2)}, u32[]{:S(2)}) %collective-permute-start.16) | collective-permute-done | bytes 262176 | tf_op jit(solution)/shard_map/ppermute | solution.py:47
  109.2 5.3 %collective-permute-start.23 = (f32[8,2,32,128]{3,2,1,0:T(8,128)S(1)}, f32[8,2,32,128]{3,2,1,0:T(8,128)S(1)}, u32[]{:S(2)}, u32[]{:S(2)}) collective-permute-start(f32[8,2,32,128]{3,2,1,0:T(8,128)S(1)} %get-tuple-element.97), channel_id=1, source_target_pairs={{0,3},{1,2},{2,1},{3,0},{4,7},{5,6},{6,5},{7,4},{8,11},{9,10},{10,... | collective-permute-start | bytes 786440 | tf_op jit(solution)/shard_map/ppermute | solution.py:47
  122.1 9.3 %mode_four.7 = (f32[8,2,32,128]{3,2,1,0:T(8,128)S(1)}, f32[8,2,32,128]{3,2,1,0:T(8,128)S(1)}, f32[8,2,32,128]{3,2,1,0:T(8,128)}, f32[8,2,32,128]{3,2,1,0:T(8,128...) custom-call(s32[1]{0:T(128)} %bitcast.1.me_ref, ...), custom_call_target="tpu_custom_call" | custom-call | flops 805306368 | bytes 6291456 | tf_op jit(solution)/shard_map/mode_four/pallas_call | solution.py:132
  135.7 3.6 %collective-permute-start.30 = (f32[8,2,32,128]{3,2,1,0:T(8,128)}, f32[8,2,32,128]{3,2,1,0:T(8,128)}, u32[]{:S(2)}, u32[]{:S(2)}) collective-permute-start(f32[8,2,32,128]{3,2,1,0:T(8,128)} %get-tuple-element.105), channel_id=1, source_target_pairs={{0,4},{1,5},{2,6},{3,7},{4,0},{5,1},{6,2},{7,3},{8,12},{9,13},{10,... | collective-permute-start | bytes 786440 | tf_op jit(solution)/shard_map/ppermute | solution.py:47
  144.7 8.5 %collective-permute-done.24.refs_4_ = f32[8,2,32,128]{3,2,1,0:T(8,128)S(1)} collective-permute-done((f32[8,2,32,128]{3,2,1,0:T(8,128)S(1)}, f32[8,2,32,128]{3,2,1,0:T(8,128)S(1)}, u32[]{:S(2)}, u32[]{:S(2)}) %collective-permute-start.24) | collective-permute-done | bytes 262176 | tf_op jit(solution)/shard_map/ppermute | solution.py:47
  167.4 3.0 collective-permute-start.35
  178.4 10.6 %collective-permute-done.33.refs_3_ = f32[8,2,32,128]{3,2,1,0:T(8,128)S(1)} collective-permute-done((f32[8,2,32,128]{3,2,1,0:T(8,128)}, f32[8,2,32,128]{3,2,1,0:T(8,128)S(1)}, u32[]{:S(2)}, u32[]{:S(2)}) %collective-permute-start.33) | collective-permute-done | bytes 262176 | tf_op jit(solution)/shard_map/ppermute | solution.py:47
  190.4 4.7 %collective-permute-done.34.refs_4_ = f32[8,2,32,128]{3,2,1,0:T(8,128)S(1)} collective-permute-done((f32[8,2,32,128]{3,2,1,0:T(8,128)}, f32[8,2,32,128]{3,2,1,0:T(8,128)S(1)}, u32[]{:S(2)}, u32[]{:S(2)}) %collective-permute-start.34) | collective-permute-done | bytes 262176 | tf_op jit(solution)/shard_map/ppermute | solution.py:47
  196.1 4.6 %collective-permute-done.36.refs_6_ = f32[8,2,32,128]{3,2,1,0:T(8,128)S(1)} collective-permute-done((f32[8,2,32,128]{3,2,1,0:T(8,128)}, f32[8,2,32,128]{3,2,1,0:T(8,128)S(1)}, u32[]{:S(2)}, u32[]{:S(2)}) %collective-permute-start.36) | collective-permute-done | bytes 262176 | tf_op jit(solution)/shard_map/ppermute | solution.py:47
  200.7 3.0 %modes_two_three.7 = (f32[2,16,8,256]{3,2,1,0:T(8,128)S(1)}, f32[2,16,8,256]{3,2,1,0:T(8,128)S(1)}, f32[2,16,8,256]{3,2,1,0:T(8,128)S(1)}, f32[2,16,8,256]{3,2,1,0:T(8,128)S(1)}) custom-call(f32[8,2,32,128]{3,2,1,0:T(8,128)} %collective-permute-done.30.refs_0_, f32[8,2,32,128]{3,2,1,0:T(8,128)} %collective-permute-done.31.refs_1_, ...), custom_call_target="tpu_custom_call" | custom-call | flops 905969664 | bytes 4194304 | tf_op jit(solution)/shard_map/modes_two_three/pallas_call | solution.py:215
  206.5 4.9 %collective-permute-done.37.refs_13_ = f32[2,16,8,256]{3,2,1,0:T(8,128)S(1)} collective-permute-done((f32[2,16,8,256]{3,2,1,0:T(8,128)S(1)}, f32[2,16,8,256]{3,2,1,0:T(8,128)S(1)}, u32[]{:S(2)}, u32[]{:S(2)}) %collective-permute-start.37) | collective-permute-done | bytes 262176 | tf_op jit(solution)/shard_map/ppermute | solution.py:47
  211.4 5.4 %collective-permute-done.39.refs_15_ = f32[2,16,8,256]{3,2,1,0:T(8,128)S(1)} collective-permute-done((f32[2,16,8,256]{3,2,1,0:T(8,128)S(1)}, f32[2,16,8,256]{3,2,1,0:T(8,128)S(1)}, u32[]{:S(2)}, u32[]{:S(2)}) %collective-permute-start.39) | collective-permute-done | bytes 262176 | tf_op jit(solution)/shard_map/ppermute | solution.py:47
  216.8 3.0 %gram.1 = f32[128,64]{1,0:T(8,128)S(1)} custom-call(s32[1]{0:T(128)} %bitcast.fib_ref, f32[2,16,8,256]{3,2,1,0:T(8,128)S(1)} %get-tuple-element.79.refs_10_.refs_0_, f32[2,16,8,256]{3,2,1,0:T(8,128)S(1)} %collective-permute-done.8.refs_11_.refs_1_, f32[2,16,8,256]{3,2,1,0:T(8,128)S(1)} %collective-permute-done.9.refs_12_.refs_2_, ...), custom_call_target="tpu_custom_call" | custom-call | tf_op jit(solution)/shard_map/gram/pallas_call | solution.py:267
  222.4 3.1 %collective-permute-done.41 = f32[128,64]{1,0:T(8,128)S(1)} collective-permute-done((f32[128,64]{1,0:T(8,128)S(1)}, f32[128,64]{1,0:T(8,128)S(1)}, u32[]{:S(2)}, u32[]{:S(2)}) %collective-permute-start.41) | collective-permute-done | bytes 32800 | tf_op jit(solution)/shard_map/ppermute | solution.py:47
  236.2 5.2 %orthonormal.1 = (f32[128,64]{1,0:T(8,128)S(1)}, f32[128,64]{1,0:T(8,128)S(1)}) custom-call(s32[1]{0:T(128)} %bitcast.fib_ref, f32[128,64]{1,0:T(8,128)S(1)} %add.36.t_ref), custom_call_target="tpu_custom_call" | custom-call | tf_op jit(solution)/shard_map/orthonormal/pallas_call | solution.py:410
  250.4 6.9 %collective-permute-start.54 = (f32[4,8,8,128]{3,2,1,0:T(8,128)S(1)}, f32[4,8,8,128]{3,2,1,0:T(8,128)S(1)}, u32[]{:S(2)}, u32[]{:S(2)}) collective-permute-start(f32[4,8,8,128]{3,2,1,0:T(8,128)S(1)} %get-tuple-element.128), channel_id=1, source_target_pairs={{0,5},{1,4},{2,7},{3,6},{4,1},{5,0},{6,3},{7,2},{8,13},{9,12},{10,... | collective-permute-start | bytes 393224 | tf_op jit(solution)/shard_map/ppermute | solution.py:47
  268.6 8.8 %collective-permute-done.56.refs_4_ = f32[4,8,8,128]{3,2,1,0:T(8,128)S(1)} collective-permute-done((f32[4,8,8,128]{3,2,1,0:T(8,128)S(1)}, f32[4,8,8,128]{3,2,1,0:T(8,128)S(1)}, u32[]{:S(2)}, u32[]{:S(2)}) %collective-permute-start.56) | collective-permute-done | bytes 131104 | tf_op jit(solution)/shard_map/ppermute | solution.py:47
  278.9 6.8 %collective-permute-done.58.refs_6_ = f32[4,8,8,128]{3,2,1,0:T(8,128)S(1)} collective-permute-done((f32[4,8,8,128]{3,2,1,0:T(8,128)S(1)}, f32[4,8,8,128]{3,2,1,0:T(8,128)S(1)}, u32[]{:S(2)}, u32[]{:S(2)}) %collective-permute-start.58) | collective-permute-done | bytes 131104 | tf_op jit(solution)/shard_map/ppermute | solution.py:47
  286.5 3.1 %assemble.2.refs_8_ = f32[64,8,16,64]{3,2,1,0:T(8,128)} custom-call(s32[1]{0:T(128)} %bitcast.1.me_ref, f32[4,8,8,128]{3,2,1,0:T(8,128)S(1)} %collective-permute-done.52.refs_0_, f32[4,8,8,128]{3,2,1,0:T(8,128)S(1)} %collective-permute-done.53.refs_1_, f32[4,8,8,128]{3,2,1,0:T(8,128)S(1)} %collective-permute-done.54.refs_2_, ...), custom_call_target="tpu_custom_call" | custom-call | tf_op jit(solution)/shard_map/assemble/pallas_call | solution.py:346
  293.8 3.1 %assemble.3 = f32[64,8,16,64]{3,2,1,0:T(8,128)} custom-call(s32[1]{0:T(128)} %bitcast.1.me_ref, f32[4,8,8,128]{3,2,1,0:T(8,128)S(1)} %collective-permute-done.45.refs_0_, f32[4,8,8,128]{3,2,1,0:T(8,128)S(1)} %collective-permute-done.46.refs_1_, f32[4,8,8,128]{3,2,1,0:T(8,128)S(1)} %collective-permute-done.47.refs_2_, ...), custom_call_target="tpu_custom_call", output_to_operand_aliasing={{}: (9, {})} | custom-call | tf_op jit(solution)/shard_map/assemble/pallas_call | solution.py:346
  (162 shorter events, 100.2 us)
Async XLA Ops:
  11.8 26.8 %collective-permute-start.1 = (f32[9,2,32,128]{3,2,1,0:T(8,128)S(1)}, f32[9,2,32,128]{3,2,1,0:T(8,128)S(1)}, u32[]{:S(2)}, u32[]{:S(2)}) collective-permute-start(f32[9,2,32,128]{3,2,1,0:T(8,128)S(1)} %get-tuple-element.69), channel_id=1, source_target_pairs={{0,2},{1,3},{2,0},{3,1},{4,6},{5,7},{6,4},{7,5},{8,10},{9,11},{10,... | collective-permute-start | bytes 884744 | tf_op jit(solution)/shard_map/ppermute | solution.py:47
  13.1 56.5 %collective-permute-start.2 = (f32[8,2,32,128]{3,2,1,0:T(8,128)}, f32[8,2,32,128]{3,2,1,0:T(8,128)}, u32[]{:S(2)}, u32[]{:S(2)}) collective-permute-start(f32[8,2,32,128]{3,2,1,0:T(8,128)} %get-tuple-element.70), channel_id=1, source_target_pairs={{0,5},{1,4},{2,7},{3,6},{4,1},{5,0},{6,3},{7,2},{8,13},{9,12},{10,... | collective-permute-start | bytes 786440 | tf_op jit(solution)/shard_map/ppermute | solution.py:47
  16.0 53.7 %collective-permute-start.3 = (f32[8,2,32,128]{3,2,1,0:T(8,128)}, f32[8,2,32,128]{3,2,1,0:T(8,128)}, u32[]{:S(2)}, u32[]{:S(2)}) collective-permute-start(f32[8,2,32,128]{3,2,1,0:T(8,128)} %get-tuple-element.71), channel_id=1, source_target_pairs={{0,3},{1,2},{2,1},{3,0},{4,7},{5,6},{6,5},{7,4},{8,11},{9,10},{10,... | collective-permute-start | bytes 786440 | tf_op jit(solution)/shard_map/ppermute | solution.py:47
  16.1 41.5 %collective-permute-start.4 = (f32[9,2,32,128]{3,2,1,0:T(8,128)S(1)}, f32[9,2,32,128]{3,2,1,0:T(8,128)S(1)}, u32[]{:S(2)}, u32[]{:S(2)}) collective-permute-start(f32[9,2,32,128]{3,2,1,0:T(8,128)S(1)} %get-tuple-element.72), channel_id=1, source_target_pairs={{0,6},{1,7},{2,4},{3,5},{4,2},{5,3},{6,0},{7,1},{8,14},{9,15},{10,... | collective-permute-start | bytes 884744 | tf_op jit(solution)/shard_map/ppermute | solution.py:47
  33.5 24.2 %collective-permute-start.7 = (f32[8,2,32,128]{3,2,1,0:T(8,128)S(1)}, f32[8,2,32,128]{3,2,1,0:T(8,128)S(1)}, u32[]{:S(2)}, u32[]{:S(2)}) collective-permute-start(f32[8,2,32,128]{3,2,1,0:T(8,128)S(1)} %get-tuple-element.77), channel_id=1, source_target_pairs={{0,2},{1,3},{2,0},{3,1},{4,6},{5,7},{6,4},{7,5},{8,10},{9,11},{10,... | collective-permute-start | bytes 786440 | tf_op jit(solution)/shard_map/ppermute | solution.py:47
  38.5 35.9 %collective-permute-start.6 = (f32[8,2,32,128]{3,2,1,0:T(8,128)}, f32[8,2,32,128]{3,2,1,0:T(8,128)S(1)}, u32[]{:S(2)}, u32[]{:S(2)}) collective-permute-start(f32[8,2,32,128]{3,2,1,0:T(8,128)} %get-tuple-element.74), channel_id=1, source_target_pairs={{0,7},{1,6},{2,5},{3,4},{4,3},{5,2},{6,1},{7,0},{8,15},{9,14},{10,... | collective-permute-start | bytes 786440 | tf_op jit(solution)/shard_map/ppermute | solution.py:47
  57.5 19.8 %collective-permute-start.11 = (f32[8,2,32,128]{3,2,1,0:T(8,128)S(1)}, f32[8,2,32,128]{3,2,1,0:T(8,128)S(1)}, u32[]{:S(2)}, u32[]{:S(2)}) collective-permute-start(f32[8,2,32,128]{3,2,1,0:T(8,128)S(1)} %get-tuple-element.83), channel_id=1, source_target_pairs={{0,4},{1,5},{2,6},{3,7},{4,0},{5,1},{6,2},{7,3},{8,12},{9,13},{10,... | collective-permute-start | bytes 786440 | tf_op jit(solution)/shard_map/ppermute | solution.py:47
  57.7 30.6 %collective-permute-start.12 = (f32[8,2,32,128]{3,2,1,0:T(8,128)S(1)}, f32[8,2,32,128]{3,2,1,0:T(8,128)S(1)}, u32[]{:S(2)}, u32[]{:S(2)}) collective-permute-start(f32[8,2,32,128]{3,2,1,0:T(8,128)S(1)} %get-tuple-element.84), channel_id=1, source_target_pairs={{0,5},{1,4},{2,7},{3,6},{4,1},{5,0},{6,3},{7,2},{8,13},{9,12},{10,... | collective-permute-start | bytes 786440 | tf_op jit(solution)/shard_map/ppermute | solution.py:47
  69.6 28.7 %collective-permute-start.13 = (f32[8,2,32,128]{3,2,1,0:T(8,128)S(1)}, f32[8,2,32,128]{3,2,1,0:T(8,128)S(1)}, u32[]{:S(2)}, u32[]{:S(2)}) collective-permute-start(f32[8,2,32,128]{3,2,1,0:T(8,128)S(1)} %get-tuple-element.85), channel_id=1, source_target_pairs={{0,3},{1,2},{2,1},{3,0},{4,7},{5,6},{6,5},{7,4},{8,11},{9,10},{10,... | collective-permute-start | bytes 786440 | tf_op jit(solution)/shard_map/ppermute | solution.py:47
  69.7 32.8 %collective-permute-start.14 = (f32[8,2,32,128]{3,2,1,0:T(8,128)S(1)}, f32[8,2,32,128]{3,2,1,0:T(8,128)S(1)}, u32[]{:S(2)}, u32[]{:S(2)}) collective-permute-start(f32[8,2,32,128]{3,2,1,0:T(8,128)S(1)} %get-tuple-element.86), channel_id=1, source_target_pairs={{0,6},{1,7},{2,4},{3,5},{4,2},{5,3},{6,0},{7,1},{8,14},{9,15},{10,... | collective-permute-start | bytes 786440 | tf_op jit(solution)/shard_map/ppermute | solution.py:47
  74.5 30.2 %collective-permute-start.15 = (f32[8,2,32,128]{3,2,1,0:T(8,128)S(1)}, f32[8,2,32,128]{3,2,1,0:T(8,128)S(1)}, u32[]{:S(2)}, u32[]{:S(2)}) collective-permute-start(f32[8,2,32,128]{3,2,1,0:T(8,128)S(1)} %get-tuple-element.87), channel_id=1, source_target_pairs={{0,1},{1,0},{2,3},{3,2},{4,5},{5,4},{6,7},{7,6},{8,9},{9,8},{10,11... | collective-permute-start | bytes 786440 | tf_op jit(solution)/shard_map/ppermute | solution.py:47
  77.4 30.9 %collective-permute-start.16 = (f32[8,2,32,128]{3,2,1,0:T(8,128)S(1)}, f32[8,2,32,128]{3,2,1,0:T(8,128)S(1)}, u32[]{:S(2)}, u32[]{:S(2)}) collective-permute-start(f32[8,2,32,128]{3,2,1,0:T(8,128)S(1)} %get-tuple-element.88), channel_id=1, source_target_pairs={{0,7},{1,6},{2,5},{3,4},{4,3},{5,2},{6,1},{7,0},{8,15},{9,14},{10,... | collective-permute-start | bytes 786440 | tf_op jit(solution)/shard_map/ppermute | solution.py:47
  88.3 19.9 %collective-permute-start.8 = (f32[2,16,8,256]{3,2,1,0:T(8,128)S(1)}, f32[2,16,8,256]{3,2,1,0:T(8,128)S(1)}, u32[]{:S(2)}, u32[]{:S(2)}) collective-permute-start(f32[2,16,8,256]{3,2,1,0:T(8,128)S(1)} %get-tuple-element.80), channel_id=1, source_target_pairs={{0,8},{8,0},{16,24},{24,16},{1,9},{9,1},{17,25},{25,17},{2,10},{10... | collective-permute-start | bytes 786440 | tf_op jit(solution)/shard_map/ppermute | solution.py:47
  108.2 26.7 %collective-permute-start.22 = (f32[8,2,32,128]{3,2,1,0:T(8,128)S(1)}, f32[8,2,32,128]{3,2,1,0:T(8,128)S(1)}, u32[]{:S(2)}, u32[]{:S(2)}) collective-permute-start(f32[8,2,32,128]{3,2,1,0:T(8,128)S(1)} %get-tuple-element.96), channel_id=1, source_target_pairs={{0,5},{1,4},{2,7},{3,6},{4,1},{5,0},{6,3},{7,2},{8,13},{9,12},{10,... | collective-permute-start | bytes 786440 | tf_op jit(solution)/shard_map/ppermute | solution.py:47
  109.2 33.0 %collective-permute-start.23 = (f32[8,2,32,128]{3,2,1,0:T(8,128)S(1)}, f32[8,2,32,128]{3,2,1,0:T(8,128)S(1)}, u32[]{:S(2)}, u32[]{:S(2)}) collective-permute-start(f32[8,2,32,128]{3,2,1,0:T(8,128)S(1)} %get-tuple-element.97), channel_id=1, source_target_pairs={{0,3},{1,2},{2,1},{3,0},{4,7},{5,6},{6,5},{7,4},{8,11},{9,10},{10,... | collective-permute-start | bytes 786440 | tf_op jit(solution)/shard_map/ppermute | solution.py:47
  114.5 38.6 %collective-permute-start.24 = (f32[8,2,32,128]{3,2,1,0:T(8,128)S(1)}, f32[8,2,32,128]{3,2,1,0:T(8,128)S(1)}, u32[]{:S(2)}, u32[]{:S(2)}) collective-permute-start(f32[8,2,32,128]{3,2,1,0:T(8,128)S(1)} %get-tuple-element.98), channel_id=1, source_target_pairs={{0,6},{1,7},{2,4},{3,5},{4,2},{5,3},{6,0},{7,1},{8,14},{9,15},{10,... | collective-permute-start | bytes 786440 | tf_op jit(solution)/shard_map/ppermute | solution.py:47
  116.3 38.8 %collective-permute-start.25 = (f32[8,2,32,128]{3,2,1,0:T(8,128)S(1)}, f32[8,2,32,128]{3,2,1,0:T(8,128)S(1)}, u32[]{:S(2)}, u32[]{:S(2)}) collective-permute-start(f32[8,2,32,128]{3,2,1,0:T(8,128)S(1)} %get-tuple-element.99), channel_id=1, source_target_pairs={{0,1},{1,0},{2,3},{3,2},{4,5},{5,4},{6,7},{7,6},{8,9},{9,8},{10,11... | collective-permute-start | bytes 786440 | tf_op jit(solution)/shard_map/ppermute | solution.py:47
  119.4 39.5 %collective-permute-start.26 = (f32[8,2,32,128]{3,2,1,0:T(8,128)S(1)}, f32[8,2,32,128]{3,2,1,0:T(8,128)S(1)}, u32[]{:S(2)}, u32[]{:S(2)}) collective-permute-start(f32[8,2,32,128]{3,2,1,0:T(8,128)S(1)} %get-tuple-element.100), channel_id=1, source_target_pairs={{0,7},{1,6},{2,5},{3,4},{4,3},{5,2},{6,1},{7,0},{8,15},{9,14},{10,... | collective-permute-start | bytes 786440 | tf_op jit(solution)/shard_map/ppermute | solution.py:47
  135.7 27.0 %collective-permute-start.30 = (f32[8,2,32,128]{3,2,1,0:T(8,128)}, f32[8,2,32,128]{3,2,1,0:T(8,128)}, u32[]{:S(2)}, u32[]{:S(2)}) collective-permute-start(f32[8,2,32,128]{3,2,1,0:T(8,128)} %get-tuple-element.105), channel_id=1, source_target_pairs={{0,4},{1,5},{2,6},{3,7},{4,0},{5,1},{6,2},{7,3},{8,12},{9,13},{10,... | collective-permute-start | bytes 786440 | tf_op jit(solution)/shard_map/ppermute | solution.py:47
  142.9 22.0 %collective-permute-start.31 = (f32[8,2,32,128]{3,2,1,0:T(8,128)}, f32[8,2,32,128]{3,2,1,0:T(8,128)}, u32[]{:S(2)}, u32[]{:S(2)}) collective-permute-start(f32[8,2,32,128]{3,2,1,0:T(8,128)} %get-tuple-element.106), channel_id=1, source_target_pairs={{0,2},{1,3},{2,0},{3,1},{4,6},{5,7},{6,4},{7,5},{8,10},{9,11},{10,... | collective-permute-start | bytes 786440 | tf_op jit(solution)/shard_map/ppermute | solution.py:47
  162.7 15.5 %collective-permute-start.32 = (f32[8,2,32,128]{3,2,1,0:T(8,128)}, f32[8,2,32,128]{3,2,1,0:T(8,128)S(1)}, u32[]{:S(2)}, u32[]{:S(2)}) collective-permute-start(f32[8,2,32,128]{3,2,1,0:T(8,128)} %copy-done.19), channel_id=1, source_target_pairs={{0,5},{1,4},{2,7},{3,6},{4,1},{5,0},{6,3},{7,2},{8,13},{9,12},{10,... | collective-permute-start | bytes 786440 | tf_op jit(solution)/shard_map/ppermute | solution.py:47
  165.0 24.1 %collective-permute-start.33 = (f32[8,2,32,128]{3,2,1,0:T(8,128)}, f32[8,2,32,128]{3,2,1,0:T(8,128)S(1)}, u32[]{:S(2)}, u32[]{:S(2)}) collective-permute-start(f32[8,2,32,128]{3,2,1,0:T(8,128)} %copy-done.18), channel_id=1, source_target_pairs={{0,3},{1,2},{2,1},{3,0},{4,7},{5,6},{6,5},{7,4},{8,11},{9,10},{10,... | collective-permute-start | bytes 786440 | tf_op jit(solution)/shard_map/ppermute | solution.py:47
  166.1 29.0 %collective-permute-start.34 = (f32[8,2,32,128]{3,2,1,0:T(8,128)}, f32[8,2,32,128]{3,2,1,0:T(8,128)S(1)}, u32[]{:S(2)}, u32[]{:S(2)}) collective-permute-start(f32[8,2,32,128]{3,2,1,0:T(8,128)} %copy-done.17), channel_id=1, source_target_pairs={{0,6},{1,7},{2,4},{3,5},{4,2},{5,3},{6,0},{7,1},{8,14},{9,15},{10,... | collective-permute-start | bytes 786440 | tf_op jit(solution)/shard_map/ppermute | solution.py:47
  167.4 28.7 %collective-permute-start.35 = (f32[8,2,32,128]{3,2,1,0:T(8,128)}, f32[8,2,32,128]{3,2,1,0:T(8,128)S(1)}, u32[]{:S(2)}, u32[]{:S(2)}) collective-permute-start(f32[8,2,32,128]{3,2,1,0:T(8,128)} %copy-done.16), channel_id=1, source_target_pairs={{0,1},{1,0},{2,3},{3,2},{4,5},{5,4},{6,7},{7,6},{8,9},{9,8},{10,11... | collective-permute-start | bytes 786440 | tf_op jit(solution)/shard_map/ppermute | solution.py:47
  170.3 30.4 %collective-permute-start.36 = (f32[8,2,32,128]{3,2,1,0:T(8,128)}, f32[8,2,32,128]{3,2,1,0:T(8,128)S(1)}, u32[]{:S(2)}, u32[]{:S(2)}) collective-permute-start(f32[8,2,32,128]{3,2,1,0:T(8,128)} %copy-done.15), channel_id=1, source_target_pairs={{0,7},{1,6},{2,5},{3,4},{4,3},{5,2},{6,1},{7,0},{8,15},{9,14},{10,... | collective-permute-start | bytes 786440 | tf_op jit(solution)/shard_map/ppermute | solution.py:47
  178.2 26.6 %collective-permute-start.27 = (f32[2,16,8,256]{3,2,1,0:T(8,128)S(1)}, f32[2,16,8,256]{3,2,1,0:T(8,128)S(1)}, u32[]{:S(2)}, u32[]{:S(2)}) collective-permute-start(f32[2,16,8,256]{3,2,1,0:T(8,128)S(1)} %get-tuple-element.102), channel_id=1, source_target_pairs={{0,8},{8,0},{16,24},{24,16},{1,9},{9,1},{17,25},{25,17},{2,10},{10... | collective-permute-start | bytes 786440 | tf_op jit(solution)/shard_map/ppermute | solution.py:47
  189.0 17.5 %collective-permute-start.28 = (f32[2,16,8,256]{3,2,1,0:T(8,128)S(1)}, f32[2,16,8,256]{3,2,1,0:T(8,128)S(1)}, u32[]{:S(2)}, u32[]{:S(2)}) collective-permute-start(f32[2,16,8,256]{3,2,1,0:T(8,128)S(1)} %get-tuple-element.103), channel_id=1, source_target_pairs={{0,16},{8,24},{16,0},{24,8},{1,17},{9,25},{17,1},{25,9},{2,18},{10... | collective-permute-start | bytes 786440 | tf_op jit(solution)/shard_map/ppermute | solution.py:47
  259.1 18.3 %collective-permute-start.56 = (f32[4,8,8,128]{3,2,1,0:T(8,128)S(1)}, f32[4,8,8,128]{3,2,1,0:T(8,128)S(1)}, u32[]{:S(2)}, u32[]{:S(2)}) collective-permute-start(f32[4,8,8,128]{3,2,1,0:T(8,128)S(1)} %get-tuple-element.130), channel_id=1, source_target_pairs={{0,6},{1,7},{2,4},{3,5},{4,2},{5,3},{6,0},{7,1},{8,14},{9,15},{10,... | collective-permute-start | bytes 393224 | tf_op jit(solution)/shard_map/ppermute | solution.py:47
  259.4 17.9 %collective-permute-start.57 = (f32[4,8,8,128]{3,2,1,0:T(8,128)S(1)}, f32[4,8,8,128]{3,2,1,0:T(8,128)S(1)}, u32[]{:S(2)}, u32[]{:S(2)}) collective-permute-start(f32[4,8,8,128]{3,2,1,0:T(8,128)S(1)} %get-tuple-element.131), channel_id=1, source_target_pairs={{0,1},{1,0},{2,3},{3,2},{4,5},{5,4},{6,7},{7,6},{8,9},{9,8},{10,11... | collective-permute-start | bytes 393224 | tf_op jit(solution)/shard_map/ppermute | solution.py:47
  260.8 24.9 %collective-permute-start.58 = (f32[4,8,8,128]{3,2,1,0:T(8,128)S(1)}, f32[4,8,8,128]{3,2,1,0:T(8,128)S(1)}, u32[]{:S(2)}, u32[]{:S(2)}) collective-permute-start(f32[4,8,8,128]{3,2,1,0:T(8,128)S(1)} %get-tuple-element.132), channel_id=1, source_target_pairs={{0,7},{1,6},{2,5},{3,4},{4,3},{5,2},{6,1},{7,0},{8,15},{9,14},{10,... | collective-permute-start | bytes 393224 | tf_op jit(solution)/shard_map/ppermute | solution.py:47
  265.8 23.8 %collective-permute-start.47 = (f32[4,8,8,128]{3,2,1,0:T(8,128)}, f32[4,8,8,128]{3,2,1,0:T(8,128)S(1)}, u32[]{:S(2)}, u32[]{:S(2)}) collective-permute-start(f32[4,8,8,128]{3,2,1,0:T(8,128)} %get-tuple-element.120), channel_id=1, source_target_pairs={{0,5},{1,4},{2,7},{3,6},{4,1},{5,0},{6,3},{7,2},{8,13},{9,12},{10,... | collective-permute-start | bytes 393224 | tf_op jit(solution)/shard_map/ppermute | solution.py:47
  267.1 22.5 %collective-permute-start.48 = (f32[4,8,8,128]{3,2,1,0:T(8,128)}, f32[4,8,8,128]{3,2,1,0:T(8,128)S(1)}, u32[]{:S(2)}, u32[]{:S(2)}) collective-permute-start(f32[4,8,8,128]{3,2,1,0:T(8,128)} %get-tuple-element.121), channel_id=1, source_target_pairs={{0,3},{1,2},{2,1},{3,0},{4,7},{5,6},{6,5},{7,4},{8,11},{9,10},{10,... | collective-permute-start | bytes 393224 | tf_op jit(solution)/shard_map/ppermute | solution.py:47
  (48 other events, 353.7 us)

commit v4 on v3

--- a/solution.py
+++ b/solution.py
@@ -13,7 +13,7 @@
 HIGHEST = lax.Precision.HIGHEST
 LANES = 128
 TILE = 8
-PIVOTS = 4
+PIVOTS = 8
 NT = (((1,), (1,)), ((), ()))
 NN = (((1,), (0,)), ((), ()))
 
@@ -66,10 +66,12 @@
     ranks = factor.shape[0]
     m = LANES // jl
     groups = kl // m
-    cuts = 4
+    cuts = 1
+    unit = 1 if riders else 2
     own = ranks // parts
     per = own // m
-    steps = chunk + 1 if riders else chunk
+    steps = chunk + 1 if riders else chunk // unit
+    last = chunk // unit - 1
 
     def kernel(me_ref, *refs):
         x_refs, f_ref, refs = refs[:cuts], refs[cuts], refs[cuts + 1:]
@@ -78,11 +80,9 @@
 
         @pl.when(step == 0)
         def _():
-            high, low = split(f_ref[...].T)
-            none = jnp.zeros_like(high)
-            left, right = [jnp.concatenate(pair, axis=1) for pair in ((high, none), (none, high))]
+            high, low = split(f_ref[...])
             w_ref[...] = jnp.concatenate(
-                [left, left, right, right, jnp.concatenate([low, none], 1), jnp.concatenate([none, low], 1)], 0)
+                [jnp.concatenate([high, high], 1), jnp.concatenate([low, jnp.zeros_like(low)], 1)], 0)
 
         if riders:
             @pl.when(step == chunk)
@@ -100,34 +100,29 @@
 
     def work(me_ref, x_refs, outs, w_ref, s_ref):
         lane = lax.broadcasted_iota(jnp.int32, (1, 1, LANES), 2)
-        half = groups // 2
-        found = []
-        for side in range(2):
-            rows = jnp.concatenate([
-                x_ref[0, :, q * groups + side * half + n, :]
-                for n in range(half) for q in range(m) for x_ref in x_refs], axis=0)
-            found += split(rows)
-        found = dot(jnp.concatenate(found, axis=1), w_ref[:4 * depth]) + dot(
-            jnp.concatenate(found[::2], axis=1), w_ref[4 * depth:])
-        for n in range(half):
-            turned = found[n * LANES:(n + 1) * LANES].T
-            s_ref[:, n, :] = turned[:ranks]
-            s_ref[:, half + n, :] = turned[ranks:]
-        for part in range(parts):
-            mine = s_ref[pl.ds((me_ref[0] ^ part) * own, own)].reshape(per, m, groups, LANES)
-            blocks = [mine[:, q] for q in range(m)]
-            width = m // 2
-            while width:
-                upper = (lane // (jl * width)) % 2 == 1
-                shift = jl * width
+        weights = w_ref[...]
+        for n in range(unit):
+            for group in range(groups):
+                rows = jnp.concatenate(
+                    [x_ref[n, :, q * groups + group, :] for q in range(m) for x_ref in x_refs], axis=0)
+                high, low = split(rows)
+                found = dot(weights, jnp.concatenate([high, low], axis=1), NT)
+                s_ref[n, :, group, :] = found[:ranks] + found[ranks:]
+            for part in range(parts):
+                mine = s_ref[n, pl.ds((me_ref[0] ^ part) * own, own)].reshape(per, m, groups, LANES)
+                blocks = [mine[:, q] for q in range(m)]
+                width = m // 2
+                while width:
+                    upper = (lane // (jl * width)) % 2 == 1
+                    shift = jl * width
+                    for q in range(m):
+                        if q & width == 0:
+                            a, b = blocks[q], blocks[q + width]
+                            blocks[q] = jnp.where(upper, pltpu.roll(b, shift, 2), a)
+                            blocks[q + width] = jnp.where(upper, b, pltpu.roll(a, LANES - shift, 2))
+                    width //= 2
                 for q in range(m):
-                    if q & width == 0:
-                        a, b = blocks[q], blocks[q + width]
-                        blocks[q] = jnp.where(upper, pltpu.roll(b, shift, 2), a)
-                        blocks[q + width] = jnp.where(upper, b, pltpu.roll(a, LANES - shift, 2))
-                width //= 2
-            for q in range(m):
-                outs[part][0, :, q * groups:(q + 1) * groups, :] = blocks[q]
+                    outs[part][n, :, q * groups:(q + 1) * groups, :] = blocks[q]
 
     return pl.pallas_call(
         kernel,
@@ -136,21 +131,21 @@
             grid=(steps,),
             in_specs=[
                 pl.BlockSpec(
-                    (1, jl // cuts, kl, depth),
-                    lambda i, me, cut=cut: (first + jnp.minimum(i, chunk - 1), cut, 0, 0)) for cut in range(cuts)
+                    (unit, jl // cuts, kl, depth),
+                    lambda i, me, cut=cut: (first // unit + jnp.minimum(i, last), cut, 0, 0)) for cut in range(cuts)
             ] + [
                 pl.BlockSpec(factor.shape, lambda i, me: (0, 0)),
             ] + [pl.BlockSpec(rider.shape, lambda i, me: (0, 0)) for rider in riders]
             + [pl.BlockSpec(memory_space=pl.ANY)] * len(after),
             out_specs=[
                 pl.BlockSpec((1, per, kl, LANES), lambda i, me: (i, 0, 0, 0)) if riders and part in carriers else
-                pl.BlockSpec((1, per, kl, LANES), lambda i, me: (jnp.minimum(i, chunk - 1), 0, 0, 0))
+                pl.BlockSpec((unit, per, kl, LANES), lambda i, me: (jnp.minimum(i, last), 0, 0, 0))
                 for part in range(parts)],
             scratch_shapes=[
-                pltpu.VMEM((6 * depth, 2 * ranks), BF16), pltpu.VMEM((ranks, groups, LANES), F32)],
+                pltpu.VMEM((2 * ranks, 2 * depth), BF16), pltpu.VMEM((unit, ranks, groups, LANES), F32)],
         ),
         out_shape=[
-            jax.ShapeDtypeStruct((steps if part in carriers else chunk, per, kl, LANES), F32)
+            jax.ShapeDtypeStruct((chunk + 1 if part in carriers else chunk, per, kl, LANES), F32)
             for part in range(parts)],
         compiler_params=params(1),
         cost_estimate=pl.CostEstimate(
@@ -454,7 +449,7 @@
     for c in range(len(sizes)):
         after = pieces[max(0, c - 1) * fibs:] if c < len(sizes) - 1 else pieces[max(0, c - 2) * fibs:(c - 1) * fibs]
         if c + 2 < len(sizes):
-            send([sent[1][1 - c]])
+            send([sent[max(c, 1)][0]])
             after = after + [sent[-1][-1]]
         shares = contract_two_three(sent[c], order, two, three, rows, slabs, fibs, after)
         pieces.append(shares[0])

time: 298 us -> 296 us (level)
  Pallas kernels: 67.1 us -> 59.1 us
  starting transfers between devices: 88 us -> 94.8 us
  local copies, waits for them, and re-layouts: 16.1 us -> 11.1 us
  waiting for transfers between devices: 125 us -> 129 us
    pallas_call x4, Pallas kernels: 36.5 us -> 29.5 us  [contract_four(): pl.pallas_call(kernel, grid_spec=pltpu.PrefetchScalarGridSpec(num_scalar_...]
    ppermute x59, starting transfers between devices: 88 us -> 94.8 us  [partner(): return lax.ppermute(x, axes, [(s, s ^ distance) for s in range(count)])]
    unnamed x45, local copies, waits for them, and re-layouts: 15.9 us -> 10.9 us
    ppermute x59, waiting for transfers between devices: 125 us -> 129 us  [partner(): return lax.ppermute(x, axes, [(s, s ^ distance) for s in range(count)])]
  transfers between devices with their start and end apart: 59 -> 59, of which waited for: 26 -> 27; matrix products, arithmetic and copies ran while one was open for 1% -> 1% of each run, Pallas kernels for 15% -> 12%
where the time goes in v4:
time: 296 us; the launch traced here: 295 us
  waiting for transfers between devices  129 us (44%)
  starting transfers between devices  94.8 us (32%)
  Pallas kernels  59.1 us (20%)
  local copies, waits for them, and re-layouts  11.1 us (4%)
    ppermute x59, waiting for transfers between devices, partner(): return lax.ppermute(x, axes, [(s, s ^ distance) for s in range(count)])  129 us
    ppermute x59, starting transfers between devices, partner(): return lax.ppermute(x, axes, [(s, s ^ distance) for s in range(count)])  94.8 us
    pallas_call x4, Pallas kernels, contract_four(): pl.pallas_call(kernel, grid_spec=pltpu.PrefetchScalarGridSpec(num_scalar_...  29.5 us
    pallas_call x4, Pallas kernels, contract_two_three(): pl.pallas_call(kernel, grid=(per,), in_specs=[pl.BlockSpec((chunk, 1, kl,...  11 us
    unnamed x45, local copies, waits for them, and re-layouts  10.9 us
    pallas_call x2, Pallas kernels, assemble(): pl.pallas_call(kernel, grid_spec=pltpu.PrefetchScalarGridSpec(num_scalar_...  6.23 us
  transfers between devices with their start and end apart: 59, of which 27 were waited for; matrix products, arithmetic and copies ran while one was open for 1% of the time, Pallas kernels for 12%

profile of v4, /device:TPU:17, one launch (start us, length us, event | category | flops | bytes accessed | tf_op | source)
XLA Modules:
  0.0 295.4 jit_solution(2552768783608421467)
XLA Ops:
  1.4 9.0 %mode_four.4 = (f32[8,2,32,128]{3,2,1,0:T(8,128)S(1)}, f32[9,2,32,128]{3,2,1,0:T(8,128)S(1)}, f32[9,2,32,128]{3,2,1,0:T(8,128)S(1)}, f32[8,2,32,128]{3,2,1,0:T(8...) custom-call(s32[1]{0:T(128)} %bitcast.1.me_ref, ...), custom_call_target="tpu_custom_call" | custom-call | flops 805306368 | bytes 6291456 | tf_op jit(solution)/shard_map/mode_four/pallas_call | solution.py:127
  15.9 8.2 %collective-permute-done.refs_2_.refs_0_ = f32[9,2,32,128]{3,2,1,0:T(8,128)S(1)} collective-permute-done((f32[9,2,32,128]{3,2,1,0:T(8,128)S(1)}, f32[9,2,32,128]{3,2,1,0:T(8,128)S(1)}, u32[]{:S(2)}, u32[]{:S(2)}) %collective-permute-start) | collective-permute-done | bytes 294944 | tf_op jit(solution)/shard_map/ppermute | solution.py:47
  24.1 6.6 %mode_four.5 = (f32[8,2,32,128]{3,2,1,0:T(8,128)S(1)}, f32[8,2,32,128]{3,2,1,0:T(8,128)S(1)}, f32[8,2,32,128]{3,2,1,0:T(8,128)S(1)}, f32[8,2,32,128]{3,2,1,0:T(8...) custom-call(s32[1]{0:T(128)} %bitcast.1.me_ref, ...), custom_call_target="tpu_custom_call" | custom-call | flops 805306368 | bytes 6291456 | tf_op jit(solution)/shard_map/mode_four/pallas_call | solution.py:127
  30.7 3.2 %collective-permute-start.7 = (f32[8,2,32,128]{3,2,1,0:T(8,128)S(1)}, f32[8,2,32,128]{3,2,1,0:T(8,128)S(1)}, u32[]{:S(2)}, u32[]{:S(2)}) collective-permute-start(f32[8,2,32,128]{3,2,1,0:T(8,128)S(1)} %get-tuple-element.77), channel_id=1, source_target_pairs={{0,4},{1,5},{2,6},{3,7},{4,0},{5,1},{6,2},{7,3},{8,12},{9,13},{10,... | collective-permute-start | bytes 786440 | tf_op jit(solution)/shard_map/ppermute | solution.py:47
  34.0 3.7 %collective-permute-start.6 = (f32[8,2,32,128]{3,2,1,0:T(8,128)}, f32[8,2,32,128]{3,2,1,0:T(8,128)S(1)}, u32[]{:S(2)}, u32[]{:S(2)}) collective-permute-start(f32[8,2,32,128]{3,2,1,0:T(8,128)} %get-tuple-element.74), channel_id=1, source_target_pairs={{0,7},{1,6},{2,5},{3,4},{4,3},{5,2},{6,1},{7,0},{8,15},{9,14},{10,... | collective-permute-start | bytes 786440 | tf_op jit(solution)/shard_map/ppermute | solution.py:47
  37.7 24.8 %collective-permute-done.4.refs_3_.refs_4_ = f32[9,2,32,128]{3,2,1,0:T(8,128)S(1)} collective-permute-done((f32[9,2,32,128]{3,2,1,0:T(8,128)S(1)}, f32[9,2,32,128]{3,2,1,0:T(8,128)S(1)}, u32[]{:S(2)}, u32[]{:S(2)}) %collective-permute-start.4) | collective-permute-done | bytes 294944 | tf_op jit(solution)/shard_map/ppermute | solution.py:47
  64.9 3.9 %collective-permute-start.12 = (f32[8,2,32,128]{3,2,1,0:T(8,128)S(1)}, f32[8,2,32,128]{3,2,1,0:T(8,128)S(1)}, u32[]{:S(2)}, u32[]{:S(2)}) collective-permute-start(f32[8,2,32,128]{3,2,1,0:T(8,128)S(1)} %get-tuple-element.84), channel_id=1, source_target_pairs={{0,5},{1,4},{2,7},{3,6},{4,1},{5,0},{6,3},{7,2},{8,13},{9,12},{10,... | collective-permute-start | bytes 786440 | tf_op jit(solution)/shard_map/ppermute | solution.py:47
  68.9 6.6 %mode_four.6 = (f32[8,2,32,128]{3,2,1,0:T(8,128)S(1)}, f32[8,2,32,128]{3,2,1,0:T(8,128)S(1)}, f32[8,2,32,128]{3,2,1,0:T(8,128)S(1)}, f32[8,2,32,128]{3,2,1,0:T(8...) custom-call(s32[1]{0:T(128)} %bitcast.1.me_ref, ...), custom_call_target="tpu_custom_call" | custom-call | flops 805306368 | bytes 6291456 | tf_op jit(solution)/shard_map/mode_four/pallas_call | solution.py:127
  79.8 3.0 %modes_two_three.4 = (f32[2,16,8,256]{3,2,1,0:T(8,128)S(1)}, f32[2,16,8,256]{3,2,1,0:T(8,128)S(1)}, f32[2,16,8,256]{3,2,1,0:T(8,128)S(1)}, f32[2,16,8,256]{3,2,1,0:T(8,128)S(1)}) custom-call(f32[9,2,32,128]{3,2,1,0:T(8,128)S(1)} %collective-permute-done.refs_2_.refs_0_, f32[9,2,32,128]{3,2,1,0:T(8,128)S(1)} %collective-permute-done.1.refs_1_, ...), custom_call_target="tpu_custom_call" | custom-call | flops 905969664 | bytes 4194304 | tf_op jit(solution)/shard_map/modes_two_three/pallas_call | solution.py:210
  84.1 15.2 %collective-permute-done.13.refs_3_ = f32[8,2,32,128]{3,2,1,0:T(8,128)S(1)} collective-permute-done((f32[8,2,32,128]{3,2,1,0:T(8,128)S(1)}, f32[8,2,32,128]{3,2,1,0:T(8,128)S(1)}, u32[]{:S(2)}, u32[]{:S(2)}) %collective-permute-start.13) | collective-permute-done | bytes 262176 | tf_op jit(solution)/shard_map/ppermute | solution.py:47
  104.4 3.2 %collective-permute-done.16.refs_6_ = f32[8,2,32,128]{3,2,1,0:T(8,128)S(1)} collective-permute-done((f32[8,2,32,128]{3,2,1,0:T(8,128)S(1)}, f32[8,2,32,128]{3,2,1,0:T(8,128)S(1)}, u32[]{:S(2)}, u32[]{:S(2)}) %collective-permute-start.16) | collective-permute-done | bytes 262176 | tf_op jit(solution)/shard_map/ppermute | solution.py:47
  108.6 3.6 %collective-permute-done.9.refs_12_.refs_2_ = f32[2,16,8,256]{3,2,1,0:T(8,128)S(1)} collective-permute-done((f32[2,16,8,256]{3,2,1,0:T(8,128)S(1)}, f32[2,16,8,256]{3,2,1,0:T(8,128)S(1)}, u32[]{:S(2)}, u32[]{:S(2)}) %collective-permute-start.9) | collective-permute-done | bytes 262176 | tf_op jit(solution)/shard_map/ppermute | solution.py:47
  112.2 3.5 %collective-permute-start.23 = (f32[8,2,32,128]{3,2,1,0:T(8,128)S(1)}, f32[8,2,32,128]{3,2,1,0:T(8,128)S(1)}, u32[]{:S(2)}, u32[]{:S(2)}) collective-permute-start(f32[8,2,32,128]{3,2,1,0:T(8,128)S(1)} %get-tuple-element.97), channel_id=1, source_target_pairs={{0,3},{1,2},{2,1},{3,0},{4,7},{5,6},{6,5},{7,4},{8,11},{9,10},{10,... | collective-permute-start | bytes 786440 | tf_op jit(solution)/shard_map/ppermute | solution.py:47
  120.7 7.2 %mode_four.7 = (f32[8,2,32,128]{3,2,1,0:T(8,128)S(1)}, f32[8,2,32,128]{3,2,1,0:T(8,128)S(1)}, f32[8,2,32,128]{3,2,1,0:T(8,128)}, f32[8,2,32,128]{3,2,1,0:T(8,128...) custom-call(s32[1]{0:T(128)} %bitcast.1.me_ref, ...), custom_call_target="tpu_custom_call" | custom-call | flops 805306368 | bytes 6291456 | tf_op jit(solution)/shard_map/mode_four/pallas_call | solution.py:127
  128.0 6.5 %collective-permute-start.30 = (f32[8,2,32,128]{3,2,1,0:T(8,128)}, f32[8,2,32,128]{3,2,1,0:T(8,128)}, u32[]{:S(2)}, u32[]{:S(2)}) collective-permute-start(f32[8,2,32,128]{3,2,1,0:T(8,128)} %get-tuple-element.105), channel_id=1, source_target_pairs={{0,4},{1,5},{2,6},{3,7},{4,0},{5,1},{6,2},{7,3},{8,12},{9,13},{10,... | collective-permute-start | bytes 786440 | tf_op jit(solution)/shard_map/ppermute | solution.py:47
  134.5 2.9 modes_two_three.5
  140.8 10.9 %collective-permute-start.31 = (f32[8,2,32,128]{3,2,1,0:T(8,128)}, f32[8,2,32,128]{3,2,1,0:T(8,128)}, u32[]{:S(2)}, u32[]{:S(2)}) collective-permute-start(f32[8,2,32,128]{3,2,1,0:T(8,128)} %get-tuple-element.106), channel_id=1, source_target_pairs={{0,2},{1,3},{2,0},{3,1},{4,6},{5,7},{6,4},{7,5},{8,10},{9,11},{10,... | collective-permute-start | bytes 786440 | tf_op jit(solution)/shard_map/ppermute | solution.py:47
  166.8 3.1 %collective-permute-start.35 = (f32[8,2,32,128]{3,2,1,0:T(8,128)}, f32[8,2,32,128]{3,2,1,0:T(8,128)S(1)}, u32[]{:S(2)}, u32[]{:S(2)}) collective-permute-start(f32[8,2,32,128]{3,2,1,0:T(8,128)} %copy-done.16), channel_id=1, source_target_pairs={{0,1},{1,0},{2,3},{3,2},{4,5},{5,4},{6,7},{7,6},{8,9},{9,8},{10,11... | collective-permute-start | bytes 786440 | tf_op jit(solution)/shard_map/ppermute | solution.py:47
  178.2 10.4 %collective-permute-done.33.refs_3_ = f32[8,2,32,128]{3,2,1,0:T(8,128)S(1)} collective-permute-done((f32[8,2,32,128]{3,2,1,0:T(8,128)}, f32[8,2,32,128]{3,2,1,0:T(8,128)S(1)}, u32[]{:S(2)}, u32[]{:S(2)}) %collective-permute-start.33) | collective-permute-done | bytes 262176 | tf_op jit(solution)/shard_map/ppermute | solution.py:47
  189.8 4.8 %collective-permute-done.34.refs_4_ = f32[8,2,32,128]{3,2,1,0:T(8,128)S(1)} collective-permute-done((f32[8,2,32,128]{3,2,1,0:T(8,128)}, f32[8,2,32,128]{3,2,1,0:T(8,128)S(1)}, u32[]{:S(2)}, u32[]{:S(2)}) %collective-permute-start.34) | collective-permute-done | bytes 262176 | tf_op jit(solution)/shard_map/ppermute | solution.py:47
  195.4 4.8 %collective-permute-done.36.refs_6_ = f32[8,2,32,128]{3,2,1,0:T(8,128)S(1)} collective-permute-done((f32[8,2,32,128]{3,2,1,0:T(8,128)}, f32[8,2,32,128]{3,2,1,0:T(8,128)S(1)}, u32[]{:S(2)}, u32[]{:S(2)}) %collective-permute-start.36) | collective-permute-done | bytes 262176 | tf_op jit(solution)/shard_map/ppermute | solution.py:47
  200.2 3.0 %modes_two_three.7 = (f32[2,16,8,256]{3,2,1,0:T(8,128)S(1)}, f32[2,16,8,256]{3,2,1,0:T(8,128)S(1)}, f32[2,16,8,256]{3,2,1,0:T(8,128)S(1)}, f32[2,16,8,256]{3,2,1,0:T(8,128)S(1)}) custom-call(f32[8,2,32,128]{3,2,1,0:T(8,128)} %collective-permute-done.30.refs_0_, f32[8,2,32,128]{3,2,1,0:T(8,128)} %collective-permute-done.31.refs_1_, ...), custom_call_target="tpu_custom_call" | custom-call | flops 905969664 | bytes 4194304 | tf_op jit(solution)/shard_map/modes_two_three/pallas_call | solution.py:210
  205.9 4.8 %collective-permute-done.37.refs_13_ = f32[2,16,8,256]{3,2,1,0:T(8,128)S(1)} collective-permute-done((f32[2,16,8,256]{3,2,1,0:T(8,128)S(1)}, f32[2,16,8,256]{3,2,1,0:T(8,128)S(1)}, u32[]{:S(2)}, u32[]{:S(2)}) %collective-permute-start.37) | collective-permute-done | bytes 262176 | tf_op jit(solution)/shard_map/ppermute | solution.py:47
  210.8 5.6 %collective-permute-done.39.refs_15_ = f32[2,16,8,256]{3,2,1,0:T(8,128)S(1)} collective-permute-done((f32[2,16,8,256]{3,2,1,0:T(8,128)S(1)}, f32[2,16,8,256]{3,2,1,0:T(8,128)S(1)}, u32[]{:S(2)}, u32[]{:S(2)}) %collective-permute-start.39) | collective-permute-done | bytes 262176 | tf_op jit(solution)/shard_map/ppermute | solution.py:47
  221.7 3.1 %collective-permute-done.41 = f32[128,64]{1,0:T(8,128)S(1)} collective-permute-done((f32[128,64]{1,0:T(8,128)S(1)}, f32[128,64]{1,0:T(8,128)S(1)}, u32[]{:S(2)}, u32[]{:S(2)}) %collective-permute-start.41) | collective-permute-done | bytes 32800 | tf_op jit(solution)/shard_map/ppermute | solution.py:47
  235.5 4.4 %orthonormal.1 = (f32[128,64]{1,0:T(8,128)S(1)}, f32[128,64]{1,0:T(8,128)S(1)}) custom-call(s32[1]{0:T(128)} %bitcast.fib_ref, f32[128,64]{1,0:T(8,128)S(1)} %add.36.t_ref), custom_call_target="tpu_custom_call" | custom-call | tf_op jit(solution)/shard_map/orthonormal/pallas_call | solution.py:405
  239.9 2.9 core.2
  248.9 6.9 %collective-permute-start.54 = (f32[4,8,8,128]{3,2,1,0:T(8,128)S(1)}, f32[4,8,8,128]{3,2,1,0:T(8,128)S(1)}, u32[]{:S(2)}, u32[]{:S(2)}) collective-permute-start(f32[4,8,8,128]{3,2,1,0:T(8,128)S(1)} %get-tuple-element.128), channel_id=1, source_target_pairs={{0,5},{1,4},{2,7},{3,6},{4,1},{5,0},{6,3},{7,2},{8,13},{9,12},{10,... | collective-permute-start | bytes 393224 | tf_op jit(solution)/shard_map/ppermute | solution.py:47
  267.0 8.8 %collective-permute-done.56.refs_4_ = f32[4,8,8,128]{3,2,1,0:T(8,128)S(1)} collective-permute-done((f32[4,8,8,128]{3,2,1,0:T(8,128)S(1)}, f32[4,8,8,128]{3,2,1,0:T(8,128)S(1)}, u32[]{:S(2)}, u32[]{:S(2)}) %collective-permute-start.56) | collective-permute-done | bytes 131104 | tf_op jit(solution)/shard_map/ppermute | solution.py:47
  277.3 6.8 %collective-permute-done.58.refs_6_ = f32[4,8,8,128]{3,2,1,0:T(8,128)S(1)} collective-permute-done((f32[4,8,8,128]{3,2,1,0:T(8,128)S(1)}, f32[4,8,8,128]{3,2,1,0:T(8,128)S(1)}, u32[]{:S(2)}, u32[]{:S(2)}) %collective-permute-start.58) | collective-permute-done | bytes 131104 | tf_op jit(solution)/shard_map/ppermute | solution.py:47
  285.0 3.1 %assemble.2.refs_8_ = f32[64,8,16,64]{3,2,1,0:T(8,128)} custom-call(s32[1]{0:T(128)} %bitcast.1.me_ref, f32[4,8,8,128]{3,2,1,0:T(8,128)S(1)} %collective-permute-done.52.refs_0_, f32[4,8,8,128]{3,2,1,0:T(8,128)S(1)} %collective-permute-done.53.refs_1_, f32[4,8,8,128]{3,2,1,0:T(8,128)S(1)} %collective-permute-done.54.refs_2_, ...), custom_call_target="tpu_custom_call" | custom-call | tf_op jit(solution)/shard_map/assemble/pallas_call | solution.py:341
  292.3 3.1 %assemble.3 = f32[64,8,16,64]{3,2,1,0:T(8,128)} custom-call(s32[1]{0:T(128)} %bitcast.1.me_ref, f32[4,8,8,128]{3,2,1,0:T(8,128)S(1)} %collective-permute-done.45.refs_0_, f32[4,8,8,128]{3,2,1,0:T(8,128)S(1)} %collective-permute-done.46.refs_1_, f32[4,8,8,128]{3,2,1,0:T(8,128)S(1)} %collective-permute-done.47.refs_2_, ...), custom_call_target="tpu_custom_call", output_to_operand_aliasing={{}: (9, {})} | custom-call | tf_op jit(solution)/shard_map/assemble/pallas_call | solution.py:341
  (162 shorter events, 96.7 us)
Async XLA Ops:
  11.1 22.8 %collective-permute-start.1 = (f32[9,2,32,128]{3,2,1,0:T(8,128)S(1)}, f32[9,2,32,128]{3,2,1,0:T(8,128)S(1)}, u32[]{:S(2)}, u32[]{:S(2)}) collective-permute-start(f32[9,2,32,128]{3,2,1,0:T(8,128)S(1)} %get-tuple-element.69), channel_id=1, source_target_pairs={{0,2},{1,3},{2,0},{3,1},{4,6},{5,7},{6,4},{7,5},{8,10},{9,11},{10,... | collective-permute-start | bytes 884744 | tf_op jit(solution)/shard_map/ppermute | solution.py:47
  12.5 63.0 %collective-permute-start.2 = (f32[8,2,32,128]{3,2,1,0:T(8,128)}, f32[8,2,32,128]{3,2,1,0:T(8,128)}, u32[]{:S(2)}, u32[]{:S(2)}) collective-permute-start(f32[8,2,32,128]{3,2,1,0:T(8,128)} %get-tuple-element.70), channel_id=1, source_target_pairs={{0,5},{1,4},{2,7},{3,6},{4,1},{5,0},{6,3},{7,2},{8,13},{9,12},{10,... | collective-permute-start | bytes 786440 | tf_op jit(solution)/shard_map/ppermute | solution.py:47
  15.3 61.2 %collective-permute-start.3 = (f32[8,2,32,128]{3,2,1,0:T(8,128)}, f32[8,2,32,128]{3,2,1,0:T(8,128)}, u32[]{:S(2)}, u32[]{:S(2)}) collective-permute-start(f32[8,2,32,128]{3,2,1,0:T(8,128)} %get-tuple-element.71), channel_id=1, source_target_pairs={{0,3},{1,2},{2,1},{3,0},{4,7},{5,6},{6,5},{7,4},{8,11},{9,10},{10,... | collective-permute-start | bytes 786440 | tf_op jit(solution)/shard_map/ppermute | solution.py:47
  15.4 47.1 %collective-permute-start.4 = (f32[9,2,32,128]{3,2,1,0:T(8,128)S(1)}, f32[9,2,32,128]{3,2,1,0:T(8,128)S(1)}, u32[]{:S(2)}, u32[]{:S(2)}) collective-permute-start(f32[9,2,32,128]{3,2,1,0:T(8,128)S(1)} %get-tuple-element.72), channel_id=1, source_target_pairs={{0,6},{1,7},{2,4},{3,5},{4,2},{5,3},{6,0},{7,1},{8,14},{9,15},{10,... | collective-permute-start | bytes 884744 | tf_op jit(solution)/shard_map/ppermute | solution.py:47
  30.7 34.2 %collective-permute-start.7 = (f32[8,2,32,128]{3,2,1,0:T(8,128)S(1)}, f32[8,2,32,128]{3,2,1,0:T(8,128)S(1)}, u32[]{:S(2)}, u32[]{:S(2)}) collective-permute-start(f32[8,2,32,128]{3,2,1,0:T(8,128)S(1)} %get-tuple-element.77), channel_id=1, source_target_pairs={{0,4},{1,5},{2,6},{3,7},{4,0},{5,1},{6,2},{7,3},{8,12},{9,13},{10,... | collective-permute-start | bytes 786440 | tf_op jit(solution)/shard_map/ppermute | solution.py:47
  34.0 45.5 %collective-permute-start.6 = (f32[8,2,32,128]{3,2,1,0:T(8,128)}, f32[8,2,32,128]{3,2,1,0:T(8,128)S(1)}, u32[]{:S(2)}, u32[]{:S(2)}) collective-permute-start(f32[8,2,32,128]{3,2,1,0:T(8,128)} %get-tuple-element.74), channel_id=1, source_target_pairs={{0,7},{1,6},{2,5},{3,4},{4,3},{5,2},{6,1},{7,0},{8,15},{9,14},{10,... | collective-permute-start | bytes 786440 | tf_op jit(solution)/shard_map/ppermute | solution.py:47
  62.5 17.3 %collective-permute-start.11 = (f32[8,2,32,128]{3,2,1,0:T(8,128)S(1)}, f32[8,2,32,128]{3,2,1,0:T(8,128)S(1)}, u32[]{:S(2)}, u32[]{:S(2)}) collective-permute-start(f32[8,2,32,128]{3,2,1,0:T(8,128)S(1)} %get-tuple-element.83), channel_id=1, source_target_pairs={{0,2},{1,3},{2,0},{3,1},{4,6},{5,7},{6,4},{7,5},{8,10},{9,11},{10,... | collective-permute-start | bytes 786440 | tf_op jit(solution)/shard_map/ppermute | solution.py:47
  64.9 17.9 %collective-permute-start.12 = (f32[8,2,32,128]{3,2,1,0:T(8,128)S(1)}, f32[8,2,32,128]{3,2,1,0:T(8,128)S(1)}, u32[]{:S(2)}, u32[]{:S(2)}) collective-permute-start(f32[8,2,32,128]{3,2,1,0:T(8,128)S(1)} %get-tuple-element.84), channel_id=1, source_target_pairs={{0,5},{1,4},{2,7},{3,6},{4,1},{5,0},{6,3},{7,2},{8,13},{9,12},{10,... | collective-permute-start | bytes 786440 | tf_op jit(solution)/shard_map/ppermute | solution.py:47
  75.5 23.8 %collective-permute-start.13 = (f32[8,2,32,128]{3,2,1,0:T(8,128)S(1)}, f32[8,2,32,128]{3,2,1,0:T(8,128)S(1)}, u32[]{:S(2)}, u32[]{:S(2)}) collective-permute-start(f32[8,2,32,128]{3,2,1,0:T(8,128)S(1)} %get-tuple-element.85), channel_id=1, source_target_pairs={{0,3},{1,2},{2,1},{3,0},{4,7},{5,6},{6,5},{7,4},{8,11},{9,10},{10,... | collective-permute-start | bytes 786440 | tf_op jit(solution)/shard_map/ppermute | solution.py:47
  76.5 25.4 %collective-permute-start.14 = (f32[8,2,32,128]{3,2,1,0:T(8,128)S(1)}, f32[8,2,32,128]{3,2,1,0:T(8,128)S(1)}, u32[]{:S(2)}, u32[]{:S(2)}) collective-permute-start(f32[8,2,32,128]{3,2,1,0:T(8,128)S(1)} %get-tuple-element.86), channel_id=1, source_target_pairs={{0,6},{1,7},{2,4},{3,5},{4,2},{5,3},{6,0},{7,1},{8,14},{9,15},{10,... | collective-permute-start | bytes 786440 | tf_op jit(solution)/shard_map/ppermute | solution.py:47
  79.5 24.6 %collective-permute-start.15 = (f32[8,2,32,128]{3,2,1,0:T(8,128)S(1)}, f32[8,2,32,128]{3,2,1,0:T(8,128)S(1)}, u32[]{:S(2)}, u32[]{:S(2)}) collective-permute-start(f32[8,2,32,128]{3,2,1,0:T(8,128)S(1)} %get-tuple-element.87), channel_id=1, source_target_pairs={{0,1},{1,0},{2,3},{3,2},{4,5},{5,4},{6,7},{7,6},{8,9},{9,8},{10,11... | collective-permute-start | bytes 786440 | tf_op jit(solution)/shard_map/ppermute | solution.py:47
  79.8 27.8 %collective-permute-start.16 = (f32[8,2,32,128]{3,2,1,0:T(8,128)S(1)}, f32[8,2,32,128]{3,2,1,0:T(8,128)S(1)}, u32[]{:S(2)}, u32[]{:S(2)}) collective-permute-start(f32[8,2,32,128]{3,2,1,0:T(8,128)S(1)} %get-tuple-element.88), channel_id=1, source_target_pairs={{0,7},{1,6},{2,5},{3,4},{4,3},{5,2},{6,1},{7,0},{8,15},{9,14},{10,... | collective-permute-start | bytes 786440 | tf_op jit(solution)/shard_map/ppermute | solution.py:47
  82.8 24.8 %collective-permute-start.8 = (f32[2,16,8,256]{3,2,1,0:T(8,128)S(1)}, f32[2,16,8,256]{3,2,1,0:T(8,128)S(1)}, u32[]{:S(2)}, u32[]{:S(2)}) collective-permute-start(f32[2,16,8,256]{3,2,1,0:T(8,128)S(1)} %get-tuple-element.80), channel_id=1, source_target_pairs={{0,8},{8,0},{16,24},{24,16},{1,9},{9,1},{17,25},{25,17},{2,10},{10... | collective-permute-start | bytes 786440 | tf_op jit(solution)/shard_map/ppermute | solution.py:47
  107.6 20.4 %collective-permute-start.22 = (f32[8,2,32,128]{3,2,1,0:T(8,128)S(1)}, f32[8,2,32,128]{3,2,1,0:T(8,128)S(1)}, u32[]{:S(2)}, u32[]{:S(2)}) collective-permute-start(f32[8,2,32,128]{3,2,1,0:T(8,128)S(1)} %get-tuple-element.96), channel_id=1, source_target_pairs={{0,5},{1,4},{2,7},{3,6},{4,1},{5,0},{6,3},{7,2},{8,13},{9,12},{10,... | collective-permute-start | bytes 786440 | tf_op jit(solution)/shard_map/ppermute | solution.py:47
  112.2 28.0 %collective-permute-start.23 = (f32[8,2,32,128]{3,2,1,0:T(8,128)S(1)}, f32[8,2,32,128]{3,2,1,0:T(8,128)S(1)}, u32[]{:S(2)}, u32[]{:S(2)}) collective-permute-start(f32[8,2,32,128]{3,2,1,0:T(8,128)S(1)} %get-tuple-element.97), channel_id=1, source_target_pairs={{0,3},{1,2},{2,1},{3,0},{4,7},{5,6},{6,5},{7,4},{8,11},{9,10},{10,... | collective-permute-start | bytes 786440 | tf_op jit(solution)/shard_map/ppermute | solution.py:47
  115.7 36.6 %collective-permute-start.24 = (f32[8,2,32,128]{3,2,1,0:T(8,128)S(1)}, f32[8,2,32,128]{3,2,1,0:T(8,128)S(1)}, u32[]{:S(2)}, u32[]{:S(2)}) collective-permute-start(f32[8,2,32,128]{3,2,1,0:T(8,128)S(1)} %get-tuple-element.98), channel_id=1, source_target_pairs={{0,6},{1,7},{2,4},{3,5},{4,2},{5,3},{6,0},{7,1},{8,14},{9,15},{10,... | collective-permute-start | bytes 786440 | tf_op jit(solution)/shard_map/ppermute | solution.py:47
  116.5 38.1 %collective-permute-start.25 = (f32[8,2,32,128]{3,2,1,0:T(8,128)S(1)}, f32[8,2,32,128]{3,2,1,0:T(8,128)S(1)}, u32[]{:S(2)}, u32[]{:S(2)}) collective-permute-start(f32[8,2,32,128]{3,2,1,0:T(8,128)S(1)} %get-tuple-element.99), channel_id=1, source_target_pairs={{0,1},{1,0},{2,3},{3,2},{4,5},{5,4},{6,7},{7,6},{8,9},{9,8},{10,11... | collective-permute-start | bytes 786440 | tf_op jit(solution)/shard_map/ppermute | solution.py:47
  118.1 40.4 %collective-permute-start.26 = (f32[8,2,32,128]{3,2,1,0:T(8,128)S(1)}, f32[8,2,32,128]{3,2,1,0:T(8,128)S(1)}, u32[]{:S(2)}, u32[]{:S(2)}) collective-permute-start(f32[8,2,32,128]{3,2,1,0:T(8,128)S(1)} %get-tuple-element.100), channel_id=1, source_target_pairs={{0,7},{1,6},{2,5},{3,4},{4,3},{5,2},{6,1},{7,0},{8,15},{9,14},{10,... | collective-permute-start | bytes 786440 | tf_op jit(solution)/shard_map/ppermute | solution.py:47
  128.0 34.1 %collective-permute-start.30 = (f32[8,2,32,128]{3,2,1,0:T(8,128)}, f32[8,2,32,128]{3,2,1,0:T(8,128)}, u32[]{:S(2)}, u32[]{:S(2)}) collective-permute-start(f32[8,2,32,128]{3,2,1,0:T(8,128)} %get-tuple-element.105), channel_id=1, source_target_pairs={{0,4},{1,5},{2,6},{3,7},{4,0},{5,1},{6,2},{7,3},{8,12},{9,13},{10,... | collective-permute-start | bytes 786440 | tf_op jit(solution)/shard_map/ppermute | solution.py:47
  140.8 23.7 %collective-permute-start.31 = (f32[8,2,32,128]{3,2,1,0:T(8,128)}, f32[8,2,32,128]{3,2,1,0:T(8,128)}, u32[]{:S(2)}, u32[]{:S(2)}) collective-permute-start(f32[8,2,32,128]{3,2,1,0:T(8,128)} %get-tuple-element.106), channel_id=1, source_target_pairs={{0,2},{1,3},{2,0},{3,1},{4,6},{5,7},{6,4},{7,5},{8,10},{9,11},{10,... | collective-permute-start | bytes 786440 | tf_op jit(solution)/shard_map/ppermute | solution.py:47
  162.1 15.6 %collective-permute-start.32 = (f32[8,2,32,128]{3,2,1,0:T(8,128)}, f32[8,2,32,128]{3,2,1,0:T(8,128)S(1)}, u32[]{:S(2)}, u32[]{:S(2)}) collective-permute-start(f32[8,2,32,128]{3,2,1,0:T(8,128)} %copy-done.19), channel_id=1, source_target_pairs={{0,5},{1,4},{2,7},{3,6},{4,1},{5,0},{6,3},{7,2},{8,13},{9,12},{10,... | collective-permute-start | bytes 786440 | tf_op jit(solution)/shard_map/ppermute | solution.py:47
  164.5 24.1 %collective-permute-start.33 = (f32[8,2,32,128]{3,2,1,0:T(8,128)}, f32[8,2,32,128]{3,2,1,0:T(8,128)S(1)}, u32[]{:S(2)}, u32[]{:S(2)}) collective-permute-start(f32[8,2,32,128]{3,2,1,0:T(8,128)} %copy-done.18), channel_id=1, source_target_pairs={{0,3},{1,2},{2,1},{3,0},{4,7},{5,6},{6,5},{7,4},{8,11},{9,10},{10,... | collective-permute-start | bytes 786440 | tf_op jit(solution)/shard_map/ppermute | solution.py:47
  165.5 29.1 %collective-permute-start.34 = (f32[8,2,32,128]{3,2,1,0:T(8,128)}, f32[8,2,32,128]{3,2,1,0:T(8,128)S(1)}, u32[]{:S(2)}, u32[]{:S(2)}) collective-permute-start(f32[8,2,32,128]{3,2,1,0:T(8,128)} %copy-done.17), channel_id=1, source_target_pairs={{0,6},{1,7},{2,4},{3,5},{4,2},{5,3},{6,0},{7,1},{8,14},{9,15},{10,... | collective-permute-start | bytes 786440 | tf_op jit(solution)/shard_map/ppermute | solution.py:47
  166.8 28.6 %collective-permute-start.35 = (f32[8,2,32,128]{3,2,1,0:T(8,128)}, f32[8,2,32,128]{3,2,1,0:T(8,128)S(1)}, u32[]{:S(2)}, u32[]{:S(2)}) collective-permute-start(f32[8,2,32,128]{3,2,1,0:T(8,128)} %copy-done.16), channel_id=1, source_target_pairs={{0,1},{1,0},{2,3},{3,2},{4,5},{5,4},{6,7},{7,6},{8,9},{9,8},{10,11... | collective-permute-start | bytes 786440 | tf_op jit(solution)/shard_map/ppermute | solution.py:47
  169.8 30.4 %collective-permute-start.36 = (f32[8,2,32,128]{3,2,1,0:T(8,128)}, f32[8,2,32,128]{3,2,1,0:T(8,128)S(1)}, u32[]{:S(2)}, u32[]{:S(2)}) collective-permute-start(f32[8,2,32,128]{3,2,1,0:T(8,128)} %copy-done.15), channel_id=1, source_target_pairs={{0,7},{1,6},{2,5},{3,4},{4,3},{5,2},{6,1},{7,0},{8,15},{9,14},{10,... | collective-permute-start | bytes 786440 | tf_op jit(solution)/shard_map/ppermute | solution.py:47
  177.7 26.5 %collective-permute-start.27 = (f32[2,16,8,256]{3,2,1,0:T(8,128)S(1)}, f32[2,16,8,256]{3,2,1,0:T(8,128)S(1)}, u32[]{:S(2)}, u32[]{:S(2)}) collective-permute-start(f32[2,16,8,256]{3,2,1,0:T(8,128)S(1)} %get-tuple-element.102), channel_id=1, source_target_pairs={{0,8},{8,0},{16,24},{24,16},{1,9},{9,1},{17,25},{25,17},{2,10},{10... | collective-permute-start | bytes 786440 | tf_op jit(solution)/shard_map/ppermute | solution.py:47
  188.6 17.3 %collective-permute-start.28 = (f32[2,16,8,256]{3,2,1,0:T(8,128)S(1)}, f32[2,16,8,256]{3,2,1,0:T(8,128)S(1)}, u32[]{:S(2)}, u32[]{:S(2)}) collective-permute-start(f32[2,16,8,256]{3,2,1,0:T(8,128)S(1)} %get-tuple-element.103), channel_id=1, source_target_pairs={{0,16},{8,24},{16,0},{24,8},{1,17},{9,25},{17,1},{25,9},{2,18},{10... | collective-permute-start | bytes 786440 | tf_op jit(solution)/shard_map/ppermute | solution.py:47
  257.5 18.3 %collective-permute-start.56 = (f32[4,8,8,128]{3,2,1,0:T(8,128)S(1)}, f32[4,8,8,128]{3,2,1,0:T(8,128)S(1)}, u32[]{:S(2)}, u32[]{:S(2)}) collective-permute-start(f32[4,8,8,128]{3,2,1,0:T(8,128)S(1)} %get-tuple-element.130), channel_id=1, source_target_pairs={{0,6},{1,7},{2,4},{3,5},{4,2},{5,3},{6,0},{7,1},{8,14},{9,15},{10,... | collective-permute-start | bytes 393224 | tf_op jit(solution)/shard_map/ppermute | solution.py:47
  257.6 18.2 %collective-permute-start.57 = (f32[4,8,8,128]{3,2,1,0:T(8,128)S(1)}, f32[4,8,8,128]{3,2,1,0:T(8,128)S(1)}, u32[]{:S(2)}, u32[]{:S(2)}) collective-permute-start(f32[4,8,8,128]{3,2,1,0:T(8,128)S(1)} %get-tuple-element.131), channel_id=1, source_target_pairs={{0,1},{1,0},{2,3},{3,2},{4,5},{5,4},{6,7},{7,6},{8,9},{9,8},{10,11... | collective-permute-start | bytes 393224 | tf_op jit(solution)/shard_map/ppermute | solution.py:47
  259.2 24.9 %collective-permute-start.58 = (f32[4,8,8,128]{3,2,1,0:T(8,128)S(1)}, f32[4,8,8,128]{3,2,1,0:T(8,128)S(1)}, u32[]{:S(2)}, u32[]{:S(2)}) collective-permute-start(f32[4,8,8,128]{3,2,1,0:T(8,128)S(1)} %get-tuple-element.132), channel_id=1, source_target_pairs={{0,7},{1,6},{2,5},{3,4},{4,3},{5,2},{6,1},{7,0},{8,15},{9,14},{10,... | collective-permute-start | bytes 393224 | tf_op jit(solution)/shard_map/ppermute | solution.py:47
  264.2 23.9 %collective-permute-start.47 = (f32[4,8,8,128]{3,2,1,0:T(8,128)}, f32[4,8,8,128]{3,2,1,0:T(8,128)S(1)}, u32[]{:S(2)}, u32[]{:S(2)}) collective-permute-start(f32[4,8,8,128]{3,2,1,0:T(8,128)} %get-tuple-element.120), channel_id=1, source_target_pairs={{0,5},{1,4},{2,7},{3,6},{4,1},{5,0},{6,3},{7,2},{8,13},{9,12},{10,... | collective-permute-start | bytes 393224 | tf_op jit(solution)/shard_map/ppermute | solution.py:47
  265.6 22.5 %collective-permute-start.48 = (f32[4,8,8,128]{3,2,1,0:T(8,128)}, f32[4,8,8,128]{3,2,1,0:T(8,128)S(1)}, u32[]{:S(2)}, u32[]{:S(2)}) collective-permute-start(f32[4,8,8,128]{3,2,1,0:T(8,128)} %get-tuple-element.121), channel_id=1, source_target_pairs={{0,3},{1,2},{2,1},{3,0},{4,7},{5,6},{6,5},{7,4},{8,11},{9,10},{10,... | collective-permute-start | bytes 393224 | tf_op jit(solution)/shard_map/ppermute | solution.py:47
  (48 other events, 549.1 us)
